TPU v7x, 128 devices: a whole 4x4x4 slice. The times are simulated.
128 devices in a mesh: scene: 2 (over core), brick: 64 (over z, x, y).
Axes of the slice: x: 4, y: 4, z: 4, core: 2. Of those that a mesh axis runs over, the one named last changes fastest.
Arguments:
- features: float32 [2, 768, 512, 64], P('scene', 'brick'), may hold values from -6 to 6
- voxel_mask: int32 [2, 768, 512], P('scene', 'brick'), may hold values 0 or 1
- weight: float32 [27, 64, 64], replicated, may hold values from -0.15625 to 0.15625
- bias: float32 [64], replicated, may hold values from -3 to 3
- cotangent: float32 [2, 768, 512, 64], P('scene', 'brick'), may hold values from -6 to 6
- owner: int32 [2, 768, 26, 1], P('scene', 'brick'), may hold values from 0 to 63, as said below
- slot: int32 [2, 768, 26], P('scene', 'brick'), may hold values from 0 to 11
- live: int32 [2, 768, 26], P('scene', 'brick'), may hold values 0 or 1
Outputs:
- activated: float32 [2, 768, 512, 64], P('scene', 'brick')
- feature_grad: float32 [2, 768, 512, 64], P('scene', 'brick')
- kernel_grad: float32 [110592], P(('scene', 'brick'))
Inputs may be any that keep to these rules, and one draw needn't show every extreme that they name: `owner`: offsets fall in classes: faces (k = 4, 10, 12, 13, 15, 21), corners (k = 0, 2, 6, 8, 17, 19, 23, 25) and edges (the other twelve). Among the rows of one device (its bricks times the offsets of one class), no value is named by more than 2 face rows, 3 edge rows or 2 corner rows, and for each class some value is named by exactly that many.
All inputs are finite; a program needn't handle non-finite values. No bound on the sum of `voxel_mask` or of `live` on one device may be relied on, other than what follows from the above.
Results may differ from a plain program's by a relative error of at most 0.0001.
Values sent between devices are 32-bit elements; how exact they have to be, the bound alone decides.
No kernel may reach another device: no remote copies, remote signals or barrier semaphores. Data moves between devices by JAX's collectives and lax.ppermute only.
A program may use at most 384 MiB of HBM per device.

v0:
```python
import math

import jax
import jax.numpy as jnp
import numpy as np
from jax import lax
from jax.sharding import PartitionSpec as P


def offset_list():
    return [
        (a, b, c)
        for a in (-1, 0, 1)
        for b in (-1, 0, 1)
        for c in (-1, 0, 1)
        if (a, b, c) != (0, 0, 0)
    ]


def offset_classes():
    return np.array([sum((1 for v in o if v != 0)) - 1 for o in offset_list()], np.int32)


def lane_tables():
    source = np.full((26, 64), 512, np.int32)
    target = np.full((26, 64), 1000, np.int32)
    for k, offset in enumerate(offset_list()):
        ranges = []
        for d in range(3):
            if offset[d] == 1:
                ranges.append([(0, 9)])
            elif offset[d] == -1:
                ranges.append([(7, 0)])
            else:
                ranges.append([(q, q + 1) for q in range(8)])
        counter = 0
        for p in ranges[0]:
            for q in ranges[1]:
                for r in ranges[2]:
                    source[k, counter] = p[0] * 64 + q[0] * 8 + r[0]
                    target[k, counter] = p[1] * 100 + q[1] * 10 + r[1]
                    counter += 1
    return (source, target)


def pad_tables():
    source, target = lane_tables()
    table = np.zeros(1000, np.int32)
    interior = np.zeros(512, np.int32)
    for x in range(8):
        for y in range(8):
            for z in range(8):
                table[(x + 1) * 100 + (y + 1) * 10 + z + 1] = x * 64 + y * 8 + z
                interior[x * 64 + y * 8 + z] = (x + 1) * 100 + (y + 1) * 10 + z + 1
    for k in range(26):
        for j in range(64):
            if target[k, j] < 1000:
                table[target[k, j]] = 512 + k * 64 + j
    return (table, interior)


def rank_within(targets, groups):
    onehot = (targets[:, None] == jnp.arange(groups, dtype=jnp.int32)[None, :]).astype(jnp.int32)
    ranks = jnp.cumsum(onehot, axis=0) - 1
    return jnp.sum(ranks * onehot, axis=1)


def on_device(features, voxel_mask, weight, bias, cotangent, owner, slot, live):
    peers = lax.axis_size("brick")
    scenes = lax.axis_size("scene")
    count = features.shape[1]
    channels = features.shape[3]
    limits = [(m * count + peers - 1) // peers for m in (6, 12, 8)]
    total_cap = sum(limits)
    bases = [0, limits[0], limits[0] + limits[1]]
    class_np = offset_classes()
    source_lane, target_lane = lane_tables()
    pad_source, interior = pad_tables()
    maskf = voxel_mask[0].astype(jnp.float32)[:, :, None]
    masked = features[0] * maskf
    dest_peer = owner[0, :, :, 0].reshape(-1)
    wanted = slot[0].reshape(-1)
    livef = live[0].reshape(-1).astype(jnp.float32)
    codes = jnp.tile(jnp.arange(26, dtype=jnp.int32), count)
    row_class = jnp.asarray(np.tile(class_np, count))
    base_table = jnp.asarray(np.array(bases, np.int32))
    rank = rank_within(dest_peer * 3 + row_class, 3 * peers)
    position = base_table[row_class] + rank
    requests = jnp.full((peers, total_cap, 2), -1, jnp.int32)
    requests = requests.at[dest_peer, position].set(jnp.stack([wanted, codes], axis=1))
    incoming = lax.all_to_all(requests, "brick", split_axis=0, concat_axis=0, tiled=True)
    valid = incoming[..., 0] >= 0
    safe_slot = jnp.where(valid, incoming[..., 0], 0)
    safe_code = jnp.where(valid, incoming[..., 1], 0)
    flat_index = safe_slot[..., None] * 513 + jnp.asarray(source_lane)[safe_code]
    blank = count * 513
    lane_pos = jnp.arange(64, dtype=jnp.int32)[None, :]
    send_index = jnp.where(valid[..., None], flat_index, blank).reshape(peers, total_cap * 64)
    lanes = total_cap * 64
    recv_index = dest_peer[:, None] * lanes + position[:, None] * 64 + lane_pos
    extended = jnp.concatenate(
        [masked, jnp.zeros((count, 1, channels), jnp.float32)], axis=1
    ).reshape(count * 513, channels)
    extended = jnp.concatenate([extended, jnp.zeros((1, channels), jnp.float32)], axis=0)
    outgoing = extended[send_index]
    returned = lax.all_to_all(outgoing, "brick", split_axis=0, concat_axis=0, tiled=True)
    returned_ext = jnp.concatenate(
        [returned.reshape(peers * lanes, channels), jnp.zeros((1, channels), jnp.float32)], axis=0
    )
    slabs = returned_ext[recv_index] * livef[:, None, None]
    joined = jnp.concatenate([masked, slabs.reshape(count, 26 * 64, channels)], axis=1)
    padded = joined[:, pad_source, :].reshape(count, 10, 10, 10, channels)
    pre = jnp.zeros((count, 512, channels), jnp.float32) + bias
    taps = [(a, b, c) for a in range(3) for b in range(3) for c in range(3)]
    for t, (a, b, c) in enumerate(taps):
        window = padded[:, a : a + 8, b : b + 8, c : c + 8, :].reshape(count, 512, channels)
        pre = pre + jnp.einsum("bvc,cd->bvd", window, weight[t], precision=lax.Precision.HIGHEST)
    sigma = jax.nn.sigmoid(pre)
    activated = pre * sigma * maskf
    dpre = cotangent[0] * maskf * (sigma + pre * sigma * (1.0 - sigma))
    dpadded = jnp.zeros((count, 10, 10, 10, channels), jnp.float32)
    kernel_terms = []
    for t, (a, b, c) in enumerate(taps):
        window = padded[:, a : a + 8, b : b + 8, c : c + 8, :].reshape(count, 512, channels)
        kernel_terms.append(
            jnp.einsum("bvc,bvd->cd", window, dpre, precision=lax.Precision.HIGHEST)
        )
        back = jnp.einsum("bvd,cd->bvc", dpre, weight[t], precision=lax.Precision.HIGHEST)
        dpadded = dpadded.at[:, a : a + 8, b : b + 8, c : c + 8, :].add(
            back.reshape(count, 8, 8, 8, channels)
        )
    kernel_local = jnp.stack(kernel_terms).reshape(-1)
    dflat = dpadded.reshape(count, 1000, channels)
    own_grad = dflat[:, interior, :]
    dextended = jnp.concatenate([dflat, jnp.zeros((count, 1, channels), jnp.float32)], axis=1)
    halo_grad = (
        dextended[:, target_lane.reshape(-1), :].reshape(count * 26, 64, channels)
        * livef[:, None, None]
    )
    sendback = (
        jnp.zeros((peers * lanes + 1, channels), jnp.float32)
        .at[recv_index.reshape(-1)]
        .set(halo_grad.reshape(-1, channels))
    )
    sendback = sendback[: peers * lanes].reshape(peers, lanes, channels)
    backflow = lax.all_to_all(sendback, "brick", split_axis=0, concat_axis=0, tiled=True)
    collected = (
        jnp.zeros((count * 513 + 1, channels), jnp.float32)
        .at[send_index.reshape(-1)]
        .add(backflow.reshape(-1, channels))
    )
    remote = collected[: count * 513].reshape(count, 513, channels)[:, :512, :]
    feature_grad = (own_grad + remote) * maskf
    scale = 1.0 / math.sqrt(float(scenes * peers * count * 512))
    kernel_share = lax.psum_scatter(
        kernel_local, ("scene", "brick"), scatter_dimension=0, tiled=True
    )
    return (activated[None], feature_grad[None], kernel_share * scale)


def solution(mesh):
    in_specs = (
        P("scene", "brick", None, None),
        P("scene", "brick", None),
        P(),
        P(),
        P("scene", "brick", None, None),
        P("scene", "brick", None, None),
        P("scene", "brick", None),
        P("scene", "brick", None),
    )
    out_specs = (
        P("scene", "brick", None, None),
        P("scene", "brick", None, None),
        P(("scene", "brick")),
    )
    return jax.shard_map(
        on_device, mesh=mesh, in_specs=in_specs, out_specs=out_specs, check_vma=False
    )
```

profile of v0, /device:TPU:0, one launch (start us, length us, event | category | flops | bytes accessed | tf_op | source)
XLA Modules:
  0.0 1516.4 jit_solution(6067628706957035557)
XLA Ops:
  9.8 16.5 %scatter_fusion = s32[64,7,2]{2,0,1:T(8,128)S(1)} fusion(s32[64,7,2]{2,0,1:T(8,128)S(1)} %broadcast_in_dim.35, s32[312]{0:T(512)S(1)} %fusion.417, s32[312,2]{1,0:T(8,128)S(1)} %copy.650), kind=kCustom, calls=%fused_computation.6 | custom fusion | bytes 9984 | tf_op jit(solution)/shard_map/scatter | solution.py:90
  27.4 11.5 all-to-all-start
  58.5 94.7 %gather_fusion.1 = f32[28672,64]{1,0:T(8,128)} fusion(f32[6157,64]{1,0:T(8,128)S(1)} %concatenate.120, s32[28672]{0:T(1024)S(1)} %broadcast_clamp_fusion), kind=kCustom, calls=%fused_computation.1 | custom fusion | bytes 14794752 | tf_op jit(solution)/shard_map/gather | solution.py:105
  153.2 12.2 copy.657
  165.4 11.0 all-to-all-start.1
  181.7 114.2 %all-to-all-done.1 = f32[64,448,64]{1,2,0:T(8,128)} async-done(((f32[64,448,64]{1,2,0:T(8,128)}), f32[64,448,64]{1,2,0:T(8,128)}, u32[]{:S(2)}, u32[]{:S(2)}) %all-to-all-start.1) | async-done | bytes 7340064 | tf_op jit(solution)/shard_map/all_to_all | solution.py:106
  295.8 11.7 copy.658
  307.5 10.4 concatenate.122
  317.9 42.6 %gather_fusion.2 = f32[19968,64]{1,0:T(8,128)} fusion(f32[28673,64]{1,0:T(8,128)} %concatenate.122, s32[20480]{0:T(1024)S(1)} %pad_clamp_fusion), kind=kCustom, calls=%fused_computation.2 | custom fusion | bytes 10303488 | tf_op jit(solution)/shard_map/gather | solution.py:110
  360.5 8.6 copy.659
  375.4 14.5 copy.660
  389.9 15.6 %gather_fusion.3 = f32[1000,12,64]{2,1,0:T(8,128)} fusion(f32[12,2176,64]{2,0,1:T(8,128)} %copy.660, s32[1024]{0:T(1024)S(1)} %get-tuple-element.369), kind=kCustom, calls=%fused_computation.3 | custom fusion | bytes 6148000 | tf_op jit(solution)/shard_map/gather | solution.py:112
  405.5 51.1 %fusion.419 = (f32[12,8,8,8,64]{4,0,3,2,1:T(8,128)}, f32[12,8,8,8,64]{4,0,3,2,1:T(8,128)S(1)}, f32[12,8,8,8,64]{4,0,3,2,1:T(8,128)}, f32[12,8,8,8,64]{4,0,3,2,1:...) fusion(f32[12,10,10,10,64]{4,0,3,2,1:T(8,128)} %bitcast.661), kind=kLoop, calls=%fused_computation.388 | loop fusion | bytes 59768832 | tf_op jit(solution)/shard_map/slice | solution.py:116
  457.2 10.1 fusion.420
  484.3 6.0 fusion.40
  501.9 6.0 fusion.52
  513.7 5.8 fusion.60
  519.5 6.2 fusion.64
  537.3 6.0 fusion.76
  560.7 6.0 fusion.92
  578.2 6.2 fusion.104
  590.3 5.8 fusion.112
  596.1 5.9 fusion.116
  602.0 5.9 fusion.120
  613.6 6.1 fusion.128
  619.8 21.4 %fusion.138 = (f32[12,512,64]{1,2,0:T(8,128)S(1)}, f32[1,12,512,64]{2,3,1,0:T(8,128)}) fusion(f32[1,12,512,64]{2,3,1,0:T(8,128)} %param.75, f32[12,512]{1,0:T(8,128)S(1)} %bitcast.729, f32[12,512,64]{1,2,0:T(8,128)S(1)} %fusion.28, f32[12,512,64]{1,2,0:T(8,128)} %fusion.32, f32[12,512,64]{1,2,0:T(8,128)} %fusion.36, f32[12,512,64]{1,2,0:T(8,128)} %fusion.40, ...), kind=kOutput, calls=%fused_computation.178 | convolution fusion | flops 316538880 | bytes 49864960 | tf_op jit(solution)/shard_map/bvc,cd->bvd/dot_general | solution.py:117
  641.2 8.1 fusion.145
  653.3 8.3 fusion.151
  661.6 8.3 fusion.157
  669.9 6.2 fusion.163
  676.1 6.0 fusion.169
  682.1 6.4 fusion.175
  688.5 6.0 fusion.181
  694.6 6.2 fusion.187
  700.7 6.0 fusion.193
  706.8 6.2 fusion.199
  713.0 6.0 fusion.205
  719.0 6.0 fusion.211
  725.0 6.4 fusion.217
  731.4 6.0 fusion.223
  737.4 6.2 fusion.229
  743.6 6.0 fusion.235
  749.6 6.2 fusion.241
  755.8 6.0 fusion.247
  761.8 6.4 fusion.253
  768.2 6.0 fusion.259
  774.3 6.2 fusion.265
  780.4 6.0 fusion.271
  786.5 6.0 fusion.277
  792.5 6.1 fusion.283
  944.9 12.2 gather_fusion.5
  957.0 13.4 copy.798
  977.6 8.2 copy.799
  985.8 55.4 %scatter_custom_fusion.1 = f32[28673,64]{1,0:T(8,128)} fusion(s32[19968]{0:T(1024)} %fusion.306, f32[19968,64]{1,0:T(8,128)} %copy.799, f32[]{:T(128)} %constant.930.clone.1), kind=kCustom, calls=%fused_computation.9 | custom fusion | bytes 7340800 | tf_op jit(solution)/shard_map/scatter | solution.py:143
  1041.2 10.3 slice.1623
  1051.5 12.2 copy.800
  1063.7 9.5 all-to-all-start.2
  1073.7 8.3 fusion.289
  1082.0 8.1 fusion.295
  1090.1 6.1 fusion.301
  1097.4 6.4 gather_fusion.4
  1107.8 194.5 %all-reduce.9.cloned.1.call-done = f32[110592]{0:T(1024)} async-done(((f32[110592]{0:T(1024)}), f32[110592]{0:T(1024)}) %all-reduce.9.cloned.1.call-update) | async-done | bytes 442384
  1303.7 11.6 copy.1022
  1315.2 184.9 %scatter_custom_fusion.2 = f32[6157,64]{1,0:T(8,128)S(1)} fusion(s32[28672]{0:T(1024)S(1)} %bitcast.731, f32[28672,64]{1,0:T(8,128)} %bitcast.724, f32[]{:T(128)} %constant.930.clone.1), kind=kCustom, calls=%fused_computation.172 | custom fusion | flops 1835008 | bytes 1576704 | tf_op jit(solution)/shard_map/scatter-add | solution.py:150
  (274 shorter events, 295.0 us)
Async XLA Ops:
  8.3 30.7 %copy-start.63 = (s32[1,12,512]{2,0,1:T(1,128)S(1)}, s32[1,12,512]{2,0,1:T(1,128)}, u32[]{:S(2)}) copy-start(s32[1,12,512]{2,0,1:T(1,128)} %param.72) | copy-start | bytes 73732
  8.3 31.3 %copy-start.56 = (f32[1,12,512,64]{2,3,1,0:T(8,128)S(1)}, f32[1,12,512,64]{2,3,1,0:T(8,128)}, u32[]{:S(2)}) copy-start(f32[1,12,512,64]{2,3,1,0:T(8,128)} %param.71) | copy-start | bytes 4718596
  27.4 23.9 %all-to-all-start = ((s32[64,7,2]{1,2,0:T(2,128)}), s32[64,7,2]{1,2,0:T(2,128)S(1)}, u32[]{:S(2)}, u32[]{:S(2)}) async-start(s32[64,7,2]{1,2,0:T(2,128)} %copy.651), calls=%async_computation | async-start | bytes 131072 | tf_op jit(solution)/shard_map/all_to_all | solution.py:91
  165.4 11.3 copy-start.64
  165.4 13.3 copy-start.66
  165.4 13.9 copy-start.68
  165.4 13.9 copy-start.69
  165.4 130.4 %all-to-all-start.1 = ((f32[64,448,64]{1,2,0:T(8,128)}), f32[64,448,64]{1,2,0:T(8,128)}, u32[]{:S(2)}, u32[]{:S(2)}) async-start(f32[64,448,64]{1,2,0:T(8,128)} %copy.657), calls=%async_computation.1 | async-start | bytes 16777216 | tf_op jit(solution)/shard_map/all_to_all | solution.py:106
  405.5 51.7 %copy-start.2 = (f32[1000,12,64]{2,1,0:T(8,128)S(1)}, f32[1000,12,64]{2,1,0:T(8,128)}, u32[]{:S(2)}) copy-start(f32[1000,12,64]{2,1,0:T(8,128)} %gather_fusion.3) | copy-start | bytes 9216004
  457.2 10.9 copy-start.4
  457.2 10.9 copy-start.54
  467.3 105.1 %copy-start.38 = (f32[12,8,8,8,64]{4,0,3,2,1:T(8,128)}, f32[12,8,8,8,64]{4,0,3,2,1:T(8,128)S(1)}, u32[]{:S(2)}) copy-start(f32[12,8,8,8,64]{4,0,3,2,1:T(8,128)S(1)} %get-tuple-element.352) | copy-start | bytes 4718596
  468.1 10.5 copy-start.7
  472.8 11.6 copy-start.8
  478.5 11.8 copy-start.10
  484.3 11.8 copy-start.12
  490.3 11.6 copy-start.14
  496.1 11.8 copy-start.16
  501.9 11.8 copy-start.18
  507.9 11.6 copy-start.20
  513.7 12.0 copy-start.22
  519.5 12.0 copy-start.24
  525.7 11.6 copy-start.26
  531.5 11.8 copy-start.28
  537.3 11.8 copy-start.30
  543.3 11.6 copy-start.32
  549.1 11.6 copy-start.34
  554.9 11.8 copy-start.36
  566.6 11.6 copy-start.40
  572.4 12.0 copy-start.42
  578.2 12.1 copy-start.44
  584.5 11.6 copy-start.46
  590.3 11.8 copy-start.48
  596.1 11.8 copy-start.50
  602.0 11.6 copy-start.51
  607.9 11.9 copy-start.58
  607.9 11.9 copy-start.71
  653.3 16.6 %copy-start.49 = (f32[12,8,8,8,64]{4,0,3,2,1:T(8,128)S(1)}, f32[12,8,8,8,64]{4,0,3,2,1:T(8,128)}, u32[]{:S(2)}) copy-start(f32[12,8,8,8,64]{4,0,3,2,1:T(8,128)} %get-tuple-element.357) | copy-start | bytes 4718596
  661.6 14.5 copy-start.47
  669.9 12.2 copy-start.45
  676.1 12.4 copy-start.43
  682.1 12.4 copy-start.41
  688.5 12.2 copy-start.39
  694.6 12.2 copy-start.37
  700.7 12.2 copy-start.35
  706.7 12.2 copy-start.33
  713.0 12.0 copy-start.31
  719.0 12.4 copy-start.29
  725.0 12.4 copy-start.27
  731.4 12.2 copy-start.25
  737.4 12.2 copy-start.23
  743.6 12.2 copy-start.21
  749.6 12.2 copy-start.19
  755.8 12.4 copy-start.17
  761.8 12.4 copy-start.15
  768.2 12.2 copy-start.13
  774.2 12.2 copy-start.11
  780.4 12.0 copy-start.9
  786.4 12.2 copy-start
  786.4 12.2 copy-start.55
  1063.7 240.0 %all-to-all-start.2 = ((f32[64,448,64]{1,2,0:T(8,128)}), f32[64,448,64]{1,2,0:T(8,128)}, u32[]{:S(2)}, u32[]{:S(2)}) async-start(f32[64,448,64]{1,2,0:T(8,128)} %copy.800), calls=%async_computation.2 | async-start | bytes 16777216 | tf_op jit(solution)/shard_map/all_to_all | solution.py:146
  1073.3 229.0 %all-reduce.9.cloned.1.call-start = ((), (), s32[]{:S(2)}) async-start(), calls=%async_computation.3 | async-start | bytes 884736
  1073.7 16.4 %copy-start.5 = (f32[12,8,8,8,64]{4,0,3,2,1:T(8,128)S(1)}, f32[12,8,8,8,64]{4,0,3,2,1:T(8,128)}, u32[]{:S(2)}) copy-start(f32[12,8,8,8,64]{4,0,3,2,1:T(8,128)} %copy-done.4) | copy-start | bytes 4718596
  1090.1 7.2 copy-start.65
  (13 other events, 46.9 us)
Sparse Core Ops, SparseCore 0:
  1097.3 204.9 all-reduce.8
where the time goes:
time: 1520 us
  matrix products  486 us (32%)
  local copies, waits for them, and re-layouts  468 us (31%)
  waiting for transfers between devices  309 us (20%)
  other arithmetic  205 us (13%)
  starting transfers between devices  32.5 us (2%)
  between operations  15.6 us (1%)
    unnamed x2, waiting for transfers between devices  195 us
    scatter-add x1, other arithmetic, on_device(): collected = jnp.zeros((count * 513 + 1, channels), jnp.float32).at[send_i...  185 us
    dot_general x27, matrix products, on_device(): jnp.einsum('bvc,bvd->cd', window, dpre, precision=lax.Precision.HIGHEST)  175 us
    dot_general x27, matrix products, on_device(): jnp.einsum('bvc,cd->bvd', window, weight[t], precision=lax.Precision.HIGH...  173 us
    dot_general x27, matrix products, on_device(): jnp.einsum('bvd,cd->bvc', dpre, weight[t], precision=lax.Precision.HIGHEST)  138 us
    all_to_all x1, waiting for transfers between devices, on_device(): lax.all_to_all(outgoing, 'brick', split_axis=0, concat_axis=0, tiled=True)  114 us
    gather x2, local copies, waits for them, and re-layouts, on_device(): outgoing = extended[send_index]  107 us
    slice x2, local copies, waits for them, and re-layouts, on_device(): padded[:, a:a + 8, b:b + 8, c:c + 8, :].reshape(count, 512, channels)  61.2 us
  transfers between devices with their start and end apart: 4, of which 2 were waited for; matrix products, arithmetic and copies ran while one was open for 3% of the time, Pallas kernels for 0%

commit v1 on v0

v1 whole, which is shorter than its diff:
```python
import math

import jax
import jax.numpy as jnp
import numpy as np
from jax import lax
from jax.experimental import pallas as pl
from jax.experimental.pallas import tpu as pltpu
from jax.sharding import PartitionSpec as P

OFFSETS = [(a, b, c) for a in (-1, 0, 1) for b in (-1, 0, 1) for c in (-1, 0, 1) if (a, b, c) != (0, 0, 0)]
KIND = [sum(1 for v in o if v != 0) - 1 for o in OFFSETS]
ORDINAL = [KIND[:k].count(KIND[k]) for k in range(26)]
PER_KIND = (6, 12, 8)
FIRST = (0, 2, 5)
PITCH = 24
F32, BF16 = jnp.float32, jnp.bfloat16


def source_coord(step):
    return 0 if step == 1 else 7


def target_coord(step):
    return 9 if step == 1 else 0


def z_row(step):
    return 16 if step == 1 else 7


def half_of(shape):
    return lax.broadcasted_iota(jnp.int32, shape, len(shape) - 1) >= 64


def swap(v):
    return pltpu.roll(v, 64, axis=v.ndim - 1)


def split_halves(v, low):
    top = v.astype(BF16).astype(F32)
    return jnp.where(low, top, v - top).astype(BF16)


def tables_kernel(x_ref, m_ref, face_ref, edge_ref, corner_ref, rows):
    x = (x_ref[...] * m_ref[...]).reshape(512, 64)
    rows[...] = jnp.concatenate([x, x], axis=1)
    for k, (a, b, c) in enumerate(OFFSETS):
        n = ORDINAL[k]
        x0, y0, z0 = source_coord(a), source_coord(b), source_coord(c)
        if KIND[k] == 0:
            for i in range(8):
                if a:
                    v = rows[x0 * 64 + i * 8:x0 * 64 + i * 8 + 8, :]
                elif b:
                    v = rows[i * 64 + y0 * 8:i * 64 + y0 * 8 + 8, :]
                else:
                    v = rows[pl.ds(i * 64 + z0, 8, stride=8), :]
                face_ref[n, i * 8:i * 8 + 8, :] = v
        elif KIND[k] == 1:
            if not c:
                v = rows[x0 * 64 + y0 * 8:x0 * 64 + y0 * 8 + 8, :]
            elif not b:
                v = rows[pl.ds(x0 * 64 + z0, 8, stride=8), :]
            else:
                v = rows[pl.ds(y0 * 8 + z0, 8, stride=64), :]
            edge_ref[n] = v
        else:
            r = x0 * 64 + y0 * 8 + z0
            corner_ref[n] = jnp.broadcast_to(rows[r:r + 1, :], (8, 128))


def pack_kernel(want_ref, face_ref, edge_ref, corner_ref, out_ref):
    high = half_of((64, 128))
    high8 = half_of((8, 128))
    row0 = lax.broadcasted_iota(jnp.int32, (8, 128), 0) == 0

    def body(p, carry):
        q = [jnp.maximum(want_ref[p, j], 0) for j in range(7)]
        out_ref[p, 0:64, :] = jnp.where(high, face_ref[q[1]], face_ref[q[0]])
        out_ref[p, 64:72, :] = jnp.where(high8, edge_ref[q[3]], edge_ref[q[2]])
        corners = jnp.where(row0, corner_ref[q[5]], corner_ref[q[6]])
        out_ref[p, 72:80, :] = jnp.where(high8, corners, edge_ref[q[4]])
        return carry

    lax.fori_loop(0, 64, body, 0)


def packed(ref):
    sides = [jnp.concatenate([ref[b, :, 0], ref[b, :, 1]], axis=-1) for b in range(2)]
    return jnp.concatenate(sides, axis=2).reshape(512, 128)


def layer_kernel(code_ref, recv_ref, x_ref, m_ref, cot_ref, wf_ref, wb_ref, bias_ref,
                 act_ref, own_ref, send_ref, a_ref, dt_ref, pf, dpad, dxf, tmp):
    g = pl.program_id(0)
    high8 = lax.broadcasted_iota(jnp.int32, (8, 128), 1) >= 64
    half8 = high8.astype(jnp.int32)
    rowi = lax.broadcasted_iota(jnp.int32, (8, 128), 0)

    @pl.when(g == 0)
    def _():
        dpad[...] = jnp.zeros_like(dpad)
        send_ref[...] = jnp.zeros_like(send_ref)

    def prow(b, x, y, z):
        return ((b * 10 + x) * 10 + y) * PITCH + z

    def fetch(k, b):
        c = code_ref[(2 * g + b) * 26 + k]
        return c >> 4, (c >> 1) & 7, c & 1

    for b in range(2):
        for x in range(8):
            v = x_ref[b, x // 2, x % 2] * m_ref[b, x // 2, x % 2]
            v = jnp.concatenate([v, v], axis=-1)
            for y in range(8):
                r = prow(b, x + 1, y + 1, 8)
                pf[r:r + 8, :] = v[y]
    for b in range(2):
        for k, (a, bb, c) in enumerate(OFFSETS):
            o, pos, alive = fetch(k, b)
            scale = alive.astype(F32)
            xt, yt, zt = target_coord(a), target_coord(bb), z_row(c)
            if KIND[k] == 0:
                for i in range(8):
                    v = recv_ref[o, i * 8:i * 8 + 8, :]
                    v = jnp.where(half8 == pos, v, swap(v)) * scale
                    if a:
                        r = prow(b, xt, i + 1, 8)
                        pf[r:r + 8, :] = v
                    elif bb:
                        r = prow(b, i + 1, yt, 8)
                        pf[r:r + 8, :] = v
                    else:
                        pf[pl.ds(prow(b, i + 1, 1, zt), 8, stride=PITCH), :] = v
            elif KIND[k] == 1:
                e = pos - 2
                v = recv_ref[o, pl.ds(pl.multiple_of(64 + 8 * (e >> 1), 8), 8), :]
                v = jnp.where(half8 == (e & 1), v, swap(v)) * scale
                if not c:
                    r = prow(b, xt, yt, 8)
                    pf[r:r + 8, :] = v
                elif not bb:
                    pf[pl.ds(prow(b, xt, 1, zt), 8, stride=PITCH), :] = v
                else:
                    pf[pl.ds(prow(b, 1, yt, zt), 8, stride=10 * PITCH), :] = v
            else:
                v = recv_ref[o, 72:80, :]
                v = jnp.where(pos == 5, v[0:1, :], v[1:2, :])
                v = jnp.where(high8[0:1], v, swap(v)) * scale
                r = prow(b, xt, yt, zt)
                pf[r:r + 1, :] = v
    low = jnp.logical_not(half_of((16, 128)))
    for l in range(3):
        for x in range(10):
            for y in range(10):
                r0, r1 = prow(0, x, y, 7 + l), prow(1, x, y, 7 + l)
                v = jnp.concatenate([pf[r0:r0 + 8, :], pf[r1:r1 + 8, :]], axis=0)
                a_ref[l, 0, x % 2, x // 2, y] = split_halves(v, low)
    acc = None
    for i in range(4):
        for j in range(3):
            parts = [a_ref[l, 0, i % 2, i // 2:i // 2 + 4, j:j + 8].reshape(512, 128) for l in range(3)]
            lhs = jnp.concatenate(parts, axis=1)
            at = (i * 3 + j) * 384
            d = jnp.dot(lhs, wf_ref[at:at + 384, :], preferred_element_type=F32)
            acc = d if acc is None else acc + d
    pre = acc[:, :128] + acc[:, 128:] + bias_ref[...]
    mask = packed(m_ref)
    sig = jax.nn.sigmoid(pre)
    act = (pre * sig * mask).reshape(4, 8, 16, 128)
    for b in range(2):
        act_ref[b, :, 0] = act[:, :, b * 8:b * 8 + 8, :64]
        act_ref[b, :, 1] = act[:, :, b * 8:b * 8 + 8, 64:]
    dpre = packed(cot_ref) * mask * (sig + pre * sig * (1.0 - sig))
    lowl = jnp.logical_not(half_of((512, 128)))
    turned = swap(dpre)
    for p in range(2):
        v = jnp.where(lowl, dpre, turned) if p == 0 else jnp.where(lowl, turned, dpre)
        dpad[p, 1:5, 2:10] = split_halves(v, lowl).reshape(4, 8, 16, 128)
    t = dpre.T
    top = t.astype(BF16)
    dt_ref[0:128, :] = top
    dt_ref[128:256, :] = (t - top.astype(F32)).astype(BF16)
    acc = None
    for i in range(4):
        parts = [dpad[i % 2, i // 2:i // 2 + 5, j:j + 10].reshape(800, 128) for j in range(3)]
        lhs = jnp.concatenate(parts, axis=1)
        d = jnp.dot(lhs, wb_ref[i * 384:i * 384 + 384, :], preferred_element_type=F32)
        acc = d if acc is None else acc + d
    y3 = (acc[:, :384] + acc[:, 384:]).reshape(5, 10, 16, 384)

    def drow(b, x, y, z):
        return ((b * 5 + x) * 10 + y) * PITCH + z

    zero = jnp.zeros((8, 128), F32)
    for b in range(2):
        for x in range(5):
            for y in range(10):
                v = y3[x, y, b * 8:b * 8 + 8]
                r = drow(b, x, y, 0)
                dxf[r:r + 8, :] = zero
                dxf[r + 16:r + 24, :] = zero
                dxf[r + 8:r + 16, :] = v[:, 128:256]
                dxf[r + 7:r + 15, :] += v[:, :128]
                dxf[r + 9:r + 17, :] += v[:, 256:]
    for b in range(2):
        for x in range(8):
            for y in range(8):
                r = drow(b, (x + 1) // 2, y + 1, 8)
                v = dxf[r:r + 8, :]
                own_ref[b, x // 2, x % 2, y] = v[:, :64] if (x + 1) % 2 == 0 else v[:, 64:]
        for k, (a, bb, c) in enumerate(OFFSETS):
            o, pos, _ = fetch(k, b)
            xt, yt, zt = target_coord(a), target_coord(bb), z_row(c)
            if KIND[k] == 0:
                for i in range(8):
                    xx = xt if a else i + 1
                    if a:
                        r = drow(b, xx // 2, i + 1, 8)
                        v = dxf[r:r + 8, :]
                    elif bb:
                        r = drow(b, xx // 2, yt, 8)
                        v = dxf[r:r + 8, :]
                    else:
                        v = dxf[pl.ds(drow(b, xx // 2, 1, zt), 8, stride=PITCH), :]
                    v = jnp.where(half8 == xx % 2, v, swap(v))
                    s = slice(i * 8, i * 8 + 8)
                    send_ref[o, s, :] = jnp.where(half8 == pos, v, send_ref[o, s, :])
            elif KIND[k] == 1:
                par = jnp.full((8, 128), xt % 2, jnp.int32)
                if not c:
                    r = drow(b, xt // 2, yt, 8)
                    v = dxf[r:r + 8, :]
                elif not bb:
                    v = dxf[pl.ds(drow(b, xt // 2, 1, zt), 8, stride=PITCH), :]
                else:
                    for q in range(2):
                        tmp[pl.ds(q, 4, stride=2), :] = dxf[pl.ds(drow(b, q, yt, zt), 4, stride=10 * PITCH), :]
                    v = tmp[...]
                    par = 1 - (rowi & 1)
                v = jnp.where(half8 == par, v, swap(v))
                e = pos - 2
                s = pl.ds(pl.multiple_of(64 + 8 * (e >> 1), 8), 8)
                send_ref[o, s, :] = jnp.where(half8 == (e & 1), v, send_ref[o, s, :])
            else:
                r = drow(b, xt // 2, yt, zt)
                v = jnp.broadcast_to(dxf[r:r + 1, :], (8, 128))
                v = jnp.where(half8 == xt % 2, v, swap(v))
                spot = jnp.logical_and(rowi == pos - 5, high8)
                send_ref[o, 72:80, :] = jnp.where(spot, v, send_ref[o, 72:80, :])


def kernel_grad_kernel(a_ref, dt_ref, out_ref):
    d = dt_ref[...]
    for j in range(3):
        for h in range(2):
            parts = [a_ref[0, :, q, h:h + 4, j:j + 8].reshape(3072, 128) for q in range(2)]
            s = jnp.dot(d, jnp.concatenate(parts, axis=1), preferred_element_type=F32)
            s = s[:128] + s[128:]
            for q in range(2):
                v = s[:, q * 128:q * 128 + 128]
                v = v + swap(v)
                out_ref[0, j, 2 * h + q] = v[:, :64]


def collect_kernel(want_ref, back_ref, own_ref, m_ref, out_ref, faces, edges, corners, rows):
    g = pl.program_id(0)
    high = half_of((64, 128))
    high8 = half_of((8, 128))
    rowi = lax.broadcasted_iota(jnp.int32, (8, 128), 0)

    @pl.when(g == 0)
    def _():
        faces[...] = jnp.zeros_like(faces)
        edges[...] = jnp.zeros_like(edges)
        corners[...] = jnp.zeros_like(corners)

        def index(p, j, spare):
            q = want_ref[p, j]
            return jnp.where(q < 0, spare, q)

        def body(p, carry):
            v = back_ref[p, 0:64, :]
            faces[index(p, 0, 72)] += jnp.where(high, 0.0, v)
            faces[index(p, 1, 72)] += jnp.where(high, v, 0.0)
            v = back_ref[p, 64:72, :]
            edges[index(p, 2, 144)] += jnp.where(high8, 0.0, v)
            edges[index(p, 3, 144)] += jnp.where(high8, v, 0.0)
            v = back_ref[p, 72:80, :]
            edges[index(p, 4, 144)] += jnp.where(high8, 0.0, v)
            v = jnp.where(high8, v, 0.0)
            corners[index(p, 5, 96)] += jnp.where(rowi == 0, v, 0.0)
            corners[index(p, 6, 96)] += jnp.where(rowi == 1, v, 0.0)
            return carry

        lax.fori_loop(0, 64, body, 0)

    def fold(v):
        return (v + swap(v))[:, :64]

    rows[...] = own_ref[...].reshape(512, 64)
    for k, (a, b, c) in enumerate(OFFSETS):
        n = g * PER_KIND[KIND[k]] + ORDINAL[k]
        x0, y0, z0 = source_coord(a), source_coord(b), source_coord(c)
        if KIND[k] == 0:
            for i in range(8):
                v = fold(faces[n, i * 8:i * 8 + 8, :])
                if a:
                    s = slice(x0 * 64 + i * 8, x0 * 64 + i * 8 + 8)
                elif b:
                    s = slice(i * 64 + y0 * 8, i * 64 + y0 * 8 + 8)
                else:
                    s = pl.ds(i * 64 + z0, 8, stride=8)
                rows[s, :] = rows[s, :] + v
        elif KIND[k] == 1:
            v = fold(edges[n])
            if not c:
                s = slice(x0 * 64 + y0 * 8, x0 * 64 + y0 * 8 + 8)
            elif not b:
                s = pl.ds(x0 * 64 + z0, 8, stride=8)
            else:
                s = pl.ds(y0 * 8 + z0, 8, stride=64)
            rows[s, :] = rows[s, :] + v
        else:
            r = x0 * 64 + y0 * 8 + z0
            v = fold(corners[n])
            rows[r:r + 1, :] = rows[r:r + 1, :] + (v[0:1] + v[1:2])
    out_ref[...] = rows[...].reshape(out_ref.shape) * m_ref[...]


def two_terms(w):
    top = lax.reduce_precision(w, 8, 7)
    return jnp.stack([top, w - top], axis=0)


def layer_weights(weight):
    w = weight.reshape(3, 3, 3, 64, 64)
    zero = jnp.zeros((1, 3, 3, 64, 64), F32)
    sides = jnp.stack([jnp.concatenate([w, zero]), jnp.concatenate([zero, w])])
    f = two_terms(sides)
    f = f.transpose(2, 3, 4, 5, 0, 1, 6)
    f = jnp.broadcast_to(f[:, :, :, None], (4, 3, 3, 2, 64, 2, 2, 64)).reshape(36 * 128, 256).astype(BF16)
    r = w[::-1, ::-1]
    sides = jnp.stack([jnp.concatenate([r, zero]), jnp.concatenate([zero, r])])
    b = two_terms(sides)
    b = b.transpose(2, 3, 6, 0, 4, 1, 5)
    b = jnp.broadcast_to(b[:, :, None], (4, 3, 2, 64, 2, 3, 2, 64)).reshape(12 * 128, 768).astype(BF16)
    return f, b


def whole(memory=pltpu.VMEM):
    return pl.BlockSpec(memory_space=memory)


def const_block(shape):
    return pl.BlockSpec(shape, lambda g: (0,) * len(shape))


def lead_block(shape):
    return pl.BlockSpec(shape, lambda g: (g,) + (0,) * (len(shape) - 1))


def params():
    return pltpu.CompilerParams(vmem_limit_bytes=56 * 1024 * 1024)


def on_device(features, voxel_mask, weight, bias, cotangent, owner, slot, live):
    x = features.reshape(12, 4, 2, 8, 8, 64)
    cot = cotangent.reshape(12, 4, 2, 8, 8, 64)
    mask = jnp.broadcast_to(voxel_mask[0].astype(F32)[:, :, None], (12, 512, 64)).reshape(12, 4, 2, 8, 8, 64)

    peer = owner.reshape(312)
    alive = live.reshape(312)
    kinds = jnp.asarray(np.tile(np.array(KIND, np.int32), 12))
    first = jnp.asarray(np.tile(np.array([FIRST[q] for q in KIND], np.int32), 12))
    per = jnp.asarray(np.tile(np.array([PER_KIND[q] for q in KIND], np.int32), 12))
    ordinal = jnp.asarray(np.tile(np.array(ORDINAL, np.int32), 12))
    entry = slot.reshape(312) * per + ordinal
    key = peer * 3 + kinds
    order = jnp.arange(312, dtype=jnp.int32)
    same = jnp.logical_and(key[:, None] == key[None, :], order[:, None] < order[None, :])
    place = first + jnp.sum(same.astype(jnp.int32), axis=0)
    spot = jnp.where(alive > 0, peer * 8 + place, -1)
    hit = spot[None, :] == jnp.arange(512, dtype=jnp.int32)[:, None]
    wanted = jnp.sum(jnp.where(hit, entry[None, :] + 1, 0), axis=1).reshape(64, 8) - 1
    code = (peer * 8 + place) * 2 + alive
    asked = lax.all_to_all(wanted, "brick", split_axis=0, concat_axis=0, tiled=True)

    faces, edges, corners = pl.pallas_call(
        tables_kernel,
        grid=(12,),
        in_specs=[lead_block((1, 4, 2, 8, 8, 64))] * 2,
        out_specs=[lead_block((6, 64, 128)), lead_block((12, 8, 128)), lead_block((8, 8, 128))],
        out_shape=[
            jax.ShapeDtypeStruct((72, 64, 128), F32),
            jax.ShapeDtypeStruct((144, 8, 128), F32),
            jax.ShapeDtypeStruct((96, 8, 128), F32),
        ],
        scratch_shapes=[pltpu.VMEM((512, 128), F32)],
        compiler_params=params(),
        name="tables",
    )(x, mask)

    out = pl.pallas_call(
        pack_kernel,
        in_specs=[whole(pltpu.SMEM), whole(), whole(), whole()],
        out_specs=whole(),
        out_shape=jax.ShapeDtypeStruct((64, 80, 128), F32),
        compiler_params=params(),
        name="pack",
    )(asked, faces, edges, corners)
    recv = lax.all_to_all(out, "brick", split_axis=0, concat_axis=0, tiled=True)

    wf, wb = layer_weights(weight)
    bias2 = jnp.concatenate([bias, bias]).reshape(1, 128)
    brick_block = lead_block((2, 4, 2, 8, 8, 64))
    brick_shape = jax.ShapeDtypeStruct((12, 4, 2, 8, 8, 64), F32)
    act, own, send, windows, dpre_t = pl.pallas_call(
        layer_kernel,
        grid=(6,),
        in_specs=[
            pl.BlockSpec(memory_space=pltpu.SMEM),
            const_block((64, 80, 128)),
            brick_block,
            brick_block,
            brick_block,
            const_block((36 * 128, 256)),
            const_block((12 * 128, 768)),
            const_block((1, 128)),
        ],
        out_specs=[
            brick_block,
            brick_block,
            const_block((64, 80, 128)),
            pl.BlockSpec((3, 1, 2, 5, 10, 16, 128), lambda g: (0, g, 0, 0, 0, 0, 0)),
            pl.BlockSpec((256, 512), lambda g: (0, g)),
        ],
        out_shape=[
            brick_shape,
            brick_shape,
            jax.ShapeDtypeStruct((64, 80, 128), F32),
            jax.ShapeDtypeStruct((3, 6, 2, 5, 10, 16, 128), BF16),
            jax.ShapeDtypeStruct((256, 3072), BF16),
        ],
        scratch_shapes=[
            pltpu.VMEM((200 * PITCH, 128), F32),
            pltpu.VMEM((2, 6, 12, 16, 128), BF16),
            pltpu.VMEM((100 * PITCH, 128), F32),
            pltpu.VMEM((8, 128), F32),
        ],
        compiler_params=params(),
        name="layer",
    )(code, recv, x, mask, cot, wf, wb, bias2)
    back = lax.all_to_all(send, "brick", split_axis=0, concat_axis=0, tiled=True)

    z = pl.pallas_call(
        kernel_grad_kernel,
        grid=(3,),
        in_specs=[
            pl.BlockSpec((1, 6, 2, 5, 10, 16, 128), lambda l: (l, 0, 0, 0, 0, 0, 0)),
            const_block((256, 3072)),
        ],
        out_specs=lead_block((1, 3, 4, 128, 64)),
        out_shape=jax.ShapeDtypeStruct((3, 3, 4, 128, 64), F32),
        compiler_params=params(),
        cost_estimate=pl.CostEstimate(flops=2 * 256 * 3072 * 4608, bytes_accessed=11000000, transcendentals=0),
        name="kernel_grad",
    )(windows, dpre_t)
    kernel = z[:, :, 0:3, 0:64] + z[:, :, 1:4, 64:128]
    kernel = kernel.transpose(2, 1, 0, 4, 3).reshape(128, 864)
    kernel = jnp.pad(kernel, ((0, 0), (0, 32))).reshape(128, 7, 128)
    shares = lax.all_to_all(kernel, ("scene", "brick"), split_axis=0, concat_axis=0, tiled=True)
    scale = 1.0 / math.sqrt(float(2 * 768 * 512))
    share = jnp.sum(shares, axis=0).reshape(896)[:864] * scale

    grad = pl.pallas_call(
        collect_kernel,
        grid=(12,),
        in_specs=[
            pl.BlockSpec(memory_space=pltpu.SMEM),
            const_block((64, 80, 128)),
            lead_block((1, 4, 2, 8, 8, 64)),
            lead_block((1, 4, 2, 8, 8, 64)),
        ],
        out_specs=lead_block((1, 4, 2, 8, 8, 64)),
        out_shape=brick_shape,
        scratch_shapes=[
            pltpu.VMEM((73, 64, 128), F32),
            pltpu.VMEM((145, 8, 128), F32),
            pltpu.VMEM((97, 8, 128), F32),
            pltpu.VMEM((512, 64), F32),
        ],
        compiler_params=params(),
        name="collect",
    )(asked, back, own, mask)
    shape = features.shape
    return act.reshape(shape), grad.reshape(shape), share


def solution(mesh):
    big = P("scene", "brick", None, None)
    flat = P("scene", "brick", None)
    return jax.shard_map(
        on_device,
        mesh=mesh,
        in_specs=(big, flat, P(), P(), big, big, flat, flat),
        out_specs=(big, big, P(("scene", "brick"))),
        check_vma=False,
    )
```

time: 1520 us -> 251 us (0.17)
  matrix products: 486 us -> 0 us
  local copies, waits for them, and re-layouts: 468 us -> 61.6 us
  waiting for transfers between devices: 309 us -> 31.2 us
  other arithmetic: 205 us -> 11.3 us
  Pallas kernels: 0 us -> 94.5 us
  blocking collectives: 0 us -> 22.5 us
    dot_general x81 -> x0, matrix products: 486 us -> none  [the longest x27 175 us: on_device(): jnp.einsum('bvc,bvd->cd', window, dpre, precision=lax.Precision.HIGHEST)]
    gather x11 -> x0, local copies, waits for them, and re-layouts: 212 us -> none  [the longest x2 107 us: on_device(): outgoing = extended[send_index]]
    unnamed x2 -> x0, waiting for transfers between devices: 195 us -> none
    scatter-add x1 -> x0, other arithmetic: 185 us -> none  [on_device(): collected = jnp.zeros((count * 513 + 1, channels), jnp.float32).at[send_i...]
    pallas_call x0 -> x5, Pallas kernels: none -> 94.5 us  [the longest x1 57.4 us: on_device(): pl.pallas_call(layer_kernel, grid=(6,), in_specs=[pl.BlockSpec(memory_spa...]
    all_to_all x3, waiting for transfers between devices: 114 us -> 31.2 us  [the longest x1 31.1 us: on_device(): lax.all_to_all(send, 'brick', split_axis=0, concat_axis=0, tiled=True)]
    slice x6 -> x0, local copies, waits for them, and re-layouts: 73.5 us -> none  [the longest x2 61.2 us: on_device(): padded[:, a:a + 8, b:b + 8, c:c + 8, :].reshape(count, 512, channels)]
    scatter x3 -> x0, local copies, waits for them, and re-layouts: 73.1 us -> none  [the longest x1 55.4 us: on_device(): sendback = jnp.zeros((peers * lanes + 1, channels), jnp.float32).at[recv_...]
  transfers between devices with their start and end apart: 4 -> 3, of which waited for: 2 -> 1; matrix products, arithmetic and copies ran while one was open for 3% -> 24% of each run, Pallas kernels for 0% -> 4%
where the time goes in v1:
time: 251 us; the launch traced here: 249 us
  Pallas kernels  94.5 us (38%)
  local copies, waits for them, and re-layouts  61.6 us (25%)
  waiting for transfers between devices  31.2 us (12%)
  starting transfers between devices  27.4 us (11%)
  blocking collectives  22.5 us (9%)
  other arithmetic  11.3 us (5%)
    pallas_call x1, Pallas kernels, on_device(): pl.pallas_call(layer_kernel, grid=(6,), in_specs=[pl.BlockSpec(memory_spa...  57.4 us
    all_to_all x1, waiting for transfers between devices, on_device(): lax.all_to_all(send, 'brick', split_axis=0, concat_axis=0, tiled=True)  31.1 us
    all_to_all x1, blocking collectives, on_device(): lax.all_to_all(kernel, ('scene', 'brick'), split_axis=0, concat_axis=0, t...  22.5 us
    unnamed x15, local copies, waits for them, and re-layouts  16.9 us
    convert_element_type x2, local copies, waits for them, and re-layouts, layer_weights(): jnp.broadcast_to(b[:, :, None], (4, 3, 2, 64, 2, 3, 2, 64))  15.9 us
    pallas_call x1, Pallas kernels, on_device(): pl.pallas_call(collect_kernel, grid=(12,), in_specs=[pl.BlockSpec(memory_...  12.2 us
    convert_element_type x2, local copies, waits for them, and re-layouts, layer_weights(): jnp.broadcast_to(f[:, :, :, None], (4, 3, 3, 2, 64, 2, 2, 64))  12 us
    all_to_all x1, starting transfers between devices, on_device(): lax.all_to_all(wanted, 'brick', split_axis=0, concat_axis=0, tiled=True)  11.5 us
  transfers between devices with their start and end apart: 3, of which 1 were waited for; matrix products, arithmetic and copies ran while one was open for 24% of the time, Pallas kernels for 4%

profile of v1, /device:TPU:0, one launch (start us, length us, event | category | flops | bytes accessed | tf_op | source)
XLA Modules:
  0.0 249.1 jit_solution(15544456025661114972)
XLA Ops:
  0.6 0.8 add_reduce_fusion
  1.4 0.1 reshape.245
  1.5 0.7 reduce.2
  2.2 0.1 reshape.227
  2.3 0.8 add_reduce_fusion.1
  3.0 0.1 reshape.239
  3.1 0.1 convert_reduce_fusion
  3.3 0.1 mul.32
  3.3 1.3 compare_select_fusion
  4.6 0.2 select_reduce_fusion
  4.8 0.7 sub.27
  5.5 11.5 %all-to-all-start = ((s32[64,1,8]{2,1,0:T(1,128)}), s32[64,1,8]{2,1,0:T(1,128)S(1)}, u32[]{:S(2)}, u32[]{:S(2)}) async-start(s32[64,1,8]{2,1,0:T(1,128)} %bitcast), calls=%async_computation | async-start | bytes 65536 | tf_op jit(solution)/shard_map/all_to_all | solution.py:389
  17.0 0.8 convert_reduce_fusion.1
  17.8 0.2 convert_element_type.27
  18.0 3.4 %copy.40 = f32[1,12,512,64]{3,2,1,0:T(8,128)} copy(f32[1,12,512,64]{2,3,1,0:T(8,128)} %param.12) | data formatting | bytes 3145728 | tf_op args[0]
  21.4 2.2 broadcast_in_dim.25.m_ref
  23.6 9.1 %tables.1 = (f32[72,64,128]{2,1,0:T(8,128)}, f32[144,8,128]{2,1,0:T(8,128)}, f32[96,8,128]{2,1,0:T(8,128)}) custom-call(f32[12,4,2,8,8,64]{5,4,3,2,1,0:T(8,128)} %bitcast.27, f32[12,4,2,8,8,64]{5,4,3,2,1,0:T(8,128)} %broadcast_in_dim.25.m_ref), custom_call_target="tpu_custom_call" | custom-call | tf_op jit(solution)/shard_map/tables/pallas_call | solution.py:391
  32.7 0.0 all-to-all-done
  32.7 0.0 copy-start.3
  32.7 0.6 copy-done.3
  33.3 4.5 %pack.1 = f32[64,80,128]{2,1,0:T(8,128)} custom-call(s32[64,8]{1,0:T(8,128)} %bitcast.35, f32[72,64,128]{2,1,0:T(8,128)} %get-tuple-element.11.face_ref, f32[144,8,128]{2,1,0:T(8,128)} %get-tuple-element.12.edge_ref, f32[96,8,128]{2,1,0:T(8,128)} %get-tuple-element.13.corner_ref), custom_call_target="tpu_custom_call" | custom-call | tf_op jit(solution)/shard_map/pack/pallas_call | solution.py:406
  37.8 0.0 copy-start.2
  37.8 10.6 %all-to-all-start.1 = ((f32[64,80,128]{2,1,0:T(8,128)}), f32[64,80,128]{2,1,0:T(8,128)S(1)}, u32[]{:S(2)}, u32[]{:S(2)}) async-start(f32[64,80,128]{2,1,0:T(8,128)} %pack.1), calls=%async_computation.1 | async-start | bytes 5242880 | tf_op jit(solution)/shard_map/all_to_all | solution.py:414
  48.5 0.0 copy-done.2
  48.5 1.0 rev.3
  49.4 1.8 pad_bitcast_fusion.1
  51.2 0.7 reduce-precision_convert_fusion
  51.9 1.9 maximum_bitcast_fusion.1
  53.8 6.4 %copy.43 = bf16[4,3,64,2,3,2,64]{6,5,4,3,2,1,0:T(2,128)(2,1)} copy(bf16[4,3,64,2,3,2,64]{2,6,4,1,0,5,3:T(8,128)(2,1)} %maximum_bitcast_fusion.1) | data formatting | bytes 2359296 | tf_op jit(solution)/shard_map/convert_element_type | solution.py:349
  60.2 5.6 %broadcast_in_dim.27 = bf16[4,3,2,64,2,3,2,64]{7,6,5,4,3,2,1,0:T(2,128)(2,1)} broadcast(bf16[4,3,64,2,3,2,64]{6,5,4,3,2,1,0:T(2,128)(2,1)} %copy.43), dimensions={0,1,3,4,5,6,7} | broadcast | bytes 3538944 | tf_op jit(solution)/shard_map/broadcast_in_dim | solution.py:349
  65.8 9.6 %convert_element_type.31.wb_ref = bf16[1536,768]{1,0:T(8,128)(2,1)} reshape(bf16[4,3,2,64,2,3,2,64]{7,6,5,4,3,2,1,0:T(2,128)(2,1)} %broadcast_in_dim.27) | data formatting | bytes 4718592 | tf_op jit(solution)/shard_map/convert_element_type | solution.py:349
  75.4 0.3 pad_bitcast_fusion.3
  75.6 0.7 reduce-precision_convert_fusion.1
  76.3 0.5 maximum_bitcast_fusion
  76.8 2.4 copy.42
  79.3 3.9 %broadcast_in_dim.26 = bf16[4,3,3,2,64,2,2,64]{7,6,5,4,3,2,1,0:T(2,128)(2,1)} broadcast(bf16[4,3,3,64,2,2,64]{6,5,4,3,2,1,0:T(2,128)(2,1)S(1)} %copy.42), dimensions={0,1,2,4,5,6,7} | broadcast | bytes 3538944 | tf_op jit(solution)/shard_map/broadcast_in_dim | solution.py:344
  83.1 9.5 %convert_element_type.29.wf_ref = bf16[4608,256]{1,0:T(8,128)(2,1)} reshape(bf16[4,3,3,2,64,2,2,64]{7,6,5,4,3,2,1,0:T(2,128)(2,1)} %broadcast_in_dim.26) | data formatting | bytes 4718592 | tf_op jit(solution)/shard_map/convert_element_type | solution.py:344
  92.7 0.0 copy-start.4
  92.7 3.3 %copy.41 = f32[1,12,512,64]{3,2,1,0:T(8,128)} copy(f32[1,12,512,64]{2,3,1,0:T(8,128)} %param.16) | data formatting | bytes 3145728 | tf_op args[4]
  96.0 0.0 copy-done.4
  96.0 0.6 maximum_bitcast_fusion.2.bias_ref
  96.6 0.0 all-to-all-done.1.recv_ref
  96.6 0.0 copy-start.1
  96.6 1.6 copy-done.1
  98.1 57.4 %layer.1 = (f32[12,4,2,8,8,64]{5,4,3,2,1,0:T(8,128)}, f32[12,4,2,8,8,64]{5,4,3,2,1,0:T(8,128)}, f32[64,80,128]{2,1,0:T(8,128)}, bf16[3,6,2,5,10,16,128]{6,5,4,3,2,1,0:T(8,128)(2,1)}, bf16[256,3072]{1,0:T(8,128)(2,1)}) custom-call(s32[312]{0:T(512)} %get-tuple-element.42.code_ref, f32[64,80,128]{2,1,0:T(8,128)} %copy-done.1, ...), custom_call_target="tpu_custom_call" | custom-call | tf_op jit(solution)/shard_map/layer/pallas_call | solution.py:420
  155.5 11.2 %kernel_grad.1 = f32[3,3,4,128,64]{4,3,2,1,0:T(8,128)} custom-call(bf16[3,6,2,5,10,16,128]{6,5,4,3,2,1,0:T(8,128)(2,1)} %get-tuple-element.17.a_ref, bf16[256,3072]{1,0:T(8,128)(2,1)} %get-tuple-element.18.dt_ref), custom_call_target="tpu_custom_call" | custom-call | flops 7247757312 | bytes 11000000 | tf_op jit(solution)/shard_map/kernel_grad/pallas_call | solution.py:458
  166.7 1.5 fusion.2
  168.3 0.3 copy.44
  168.6 0.3 reshape.235
  168.9 0.2 copy.49
  169.1 0.2 copy.46
  169.3 22.5 %all_to_all.23 = f32[128,7,128]{2,1,0:T(8,128)S(1)} all-to-all(f32[128,7,128]{2,1,0:T(8,128)S(1)} %copy.46), channel_id=1, replica_groups=mesh['scene'=2,'brick'=64] {'scene','brick'}, dimensions={0} | all-to-all | bytes 917504 | tf_op jit(solution)/shard_map/all_to_all | solution.py:474
  191.8 5.2 %all-to-all-start.2 = ((f32[64,80,128]{2,1,0:T(8,128)}), f32[64,80,128]{2,1,0:T(8,128)S(1)}, u32[]{:S(2)}, u32[]{:S(2)}) async-start(f32[64,80,128]{2,1,0:T(8,128)} %get-tuple-element.15), calls=%async_computation.2 | async-start | bytes 5242880 | tf_op jit(solution)/shard_map/all_to_all | solution.py:456
  197.1 3.2 %copy.47 = f32[1,12,512,64]{2,3,1,0:T(8,128)} copy(f32[1,12,512,64]{3,2,1,0:T(8,128)} %bitcast.33) | data formatting | bytes 3145728
  200.3 0.1 reduce_sum.29
  200.4 0.6 slice_multiply_fusion
  201.0 31.1 %all-to-all-done.2.back_ref = f32[64,80,128]{2,1,0:T(8,128)S(1)} async-done(((f32[64,80,128]{2,1,0:T(8,128)}), f32[64,80,128]{2,1,0:T(8,128)S(1)}, u32[]{:S(2)}, u32[]{:S(2)}) %all-to-all-start.2) | async-done | bytes 2621472 | tf_op jit(solution)/shard_map/all_to_all | solution.py:456
  232.2 0.0 copy-start
  232.2 1.5 copy-done
  233.7 12.2 %collect.1 = f32[12,4,2,8,8,64]{5,4,3,2,1,0:T(8,128)} custom-call(s32[64,8]{1,0:T(8,128)} %bitcast.36, f32[64,80,128]{2,1,0:T(8,128)} %copy-done, f32[12,4,2,8,8,64]{5,4,3,2,1,0:T(8,128)} %get-tuple-element.16.own_ref, f32[12,4,2,8,8,64]{5,4,3,2,1,0:T(8,128)} %broadcast_in_dim.25.m_ref), custom_call_target="tpu_custom_call" | custom-call | tf_op jit(solution)/shard_map/collect/pallas_call | solution.py:478
  245.9 3.2 %copy.48 = f32[1,12,512,64]{2,3,1,0:T(8,128)} copy(f32[1,12,512,64]{3,2,1,0:T(8,128)} %bitcast.29) | data formatting | bytes 3145728
  (2 shorter events, 0.0 us)
Async XLA Ops:
  5.5 27.2 %all-to-all-start = ((s32[64,1,8]{2,1,0:T(1,128)}), s32[64,1,8]{2,1,0:T(1,128)S(1)}, u32[]{:S(2)}, u32[]{:S(2)}) async-start(s32[64,1,8]{2,1,0:T(1,128)} %bitcast), calls=%async_computation | async-start | bytes 65536 | tf_op jit(solution)/shard_map/all_to_all | solution.py:389
  32.7 0.6 copy-start.3
  37.8 10.7 %copy-start.2 = (f32[27,64,64]{2,1,0:T(8,128)S(1)}, f32[27,64,64]{2,1,0:T(8,128)}, u32[]{:S(2)}) copy-start(f32[27,64,64]{2,1,0:T(8,128)} %param.14) | copy-start | bytes 1327108
  37.8 58.8 %all-to-all-start.1 = ((f32[64,80,128]{2,1,0:T(8,128)}), f32[64,80,128]{2,1,0:T(8,128)S(1)}, u32[]{:S(2)}, u32[]{:S(2)}) async-start(f32[64,80,128]{2,1,0:T(8,128)} %pack.1), calls=%async_computation.1 | async-start | bytes 5242880 | tf_op jit(solution)/shard_map/all_to_all | solution.py:414
  92.7 3.3 %copy-start.4 = (f32[64]{0:T(128)S(1)}, f32[64]{0:T(128)}, u32[]{:S(2)}) copy-start(f32[64]{0:T(128)} %param.15) | copy-start | bytes 772
  96.6 1.6 copy-start.1
  191.8 40.4 %all-to-all-start.2 = ((f32[64,80,128]{2,1,0:T(8,128)}), f32[64,80,128]{2,1,0:T(8,128)S(1)}, u32[]{:S(2)}, u32[]{:S(2)}) async-start(f32[64,80,128]{2,1,0:T(8,128)} %get-tuple-element.15), calls=%async_computation.2 | async-start | bytes 5242880 | tf_op jit(solution)/shard_map/all_to_all | solution.py:456
  232.2 1.5 copy-start

commit v2 on v1

--- a/solution.py
+++ b/solution.py
@@ -86,29 +86,324 @@
     lax.fori_loop(0, 64, body, 0)
 
 
-def packed(ref):
-    sides = [jnp.concatenate([ref[b, :, 0], ref[b, :, 1]], axis=-1) for b in range(2)]
-    return jnp.concatenate(sides, axis=2).reshape(512, 128)
-
-
-def layer_kernel(code_ref, recv_ref, x_ref, m_ref, cot_ref, wf_ref, wb_ref, bias_ref,
-                 act_ref, own_ref, send_ref, a_ref, dt_ref, pf, dpad, dxf, tmp):
+def placed(v, other):
+    return jnp.where(other, v, swap(v))
+
+
+def shifted(v, l, row):
+    if l == 1:
+        return v
+    turned = pltpu.roll(v, 1 if l == 0 else 7, axis=0)
+    return jnp.where(row == (0 if l == 0 else 7), 0.0, turned)
+
+
+def weights_kernel(w_ref, f_ref, b_ref):
+    zero = jnp.zeros((64, 64), F32)
+
+    def fill(out_ref, s, sides):
+        c = jnp.concatenate(sides, axis=1)
+        top = c.astype(BF16)
+        low = (c - top.astype(F32)).astype(BF16)
+        v = jnp.concatenate([top, low], axis=1)
+        out_ref[s * 128:s * 128 + 128, :] = jnp.concatenate([v, v], axis=0)
+
+    for j in range(3):
+        for l in range(3):
+            w = [w_ref[i * 9 + j * 3 + l] for i in range(3)]
+            t = [w_ref[(2 - i) * 9 + (2 - j) * 3 + 2 - l].T for i in range(3)]
+            for i in range(4):
+                s = i * 9 + j * 3 + l
+                fill(f_ref, s, [w[i] if i < 3 else zero, w[i - 1] if i else zero])
+                fill(b_ref, s, [t[i] if i < 3 else zero, t[i - 1] if i else zero])
+
+
+def convolve(a_ref, w_ref):
+    slices = [(i, j, l) for i in range(4) for j in range(3) for l in range(3)]
+    acc = None
+    for s in range(0, 36, 4):
+        parts = [a_ref[l, i % 2, i // 2:i // 2 + 4, j:j + 8].reshape(512, 128) for i, j, l in slices[s:s + 4]]
+        lhs = jnp.concatenate(parts, axis=1)
+        d = jnp.dot(lhs, w_ref[s * 128:s * 128 + 512, :], preferred_element_type=F32)
+        acc = d if acc is None else acc + d
+    return (acc[:, :128] + acc[:, 128:]).reshape(4, 8, 16, 128)
+
+
+def own_forward_kernel(x_ref, m_ref, cot_ref, w_ref, bias_ref, pre_ref, mask_ref, cotm_ref, a_ref):
+    @pl.when(pl.program_id(0) == 0)
+    def _():
+        a_ref[...] = jnp.zeros_like(a_ref)
+
+    row = lax.broadcasted_iota(jnp.int32, (8, 128), 0)
+    low = jnp.logical_not(half_of((16, 128)))
+    for x in range(8):
+        cols = []
+        for b in range(2):
+            v = x_ref[b, x // 2, x % 2] * m_ref[b, x // 2, x % 2]
+            cols.append(jnp.concatenate([v, v], axis=-1))
+        for y in range(8):
+            for l in range(3):
+                v = jnp.concatenate([shifted(cols[b][y], l, row) for b in range(2)], axis=0)
+                a_ref[l, (x + 1) % 2, (x + 1) // 2, y + 1] = split_halves(v, low)
+    pre = convolve(a_ref, w_ref) + bias_ref[...]
+    for b in range(2):
+        pre_ref[b] = pre[:, :, b * 8:b * 8 + 8]
+        mask = jnp.concatenate([m_ref[b, :, 0], m_ref[b, :, 1]], axis=-1)
+        mask_ref[b] = mask
+        cotm_ref[b] = jnp.concatenate([cot_ref[b, :, 0], cot_ref[b, :, 1]], axis=-1) * mask
+
+
+def own_backward_kernel(d_ref, w_ref, own_ref, a_ref):
+    @pl.when(pl.program_id(0) == 0)
+    def _():
+        a_ref[...] = jnp.zeros_like(a_ref)
+
+    row = lax.broadcasted_iota(jnp.int32, (8, 128), 0)
+    half = half_of((8, 128))
+    low = jnp.logical_not(half_of((16, 128)))
+    for x in range(8):
+        for y in range(8):
+            cols = []
+            for b in range(2):
+                v = d_ref[b, x // 2, y]
+                cols.append(placed(v, half if x % 2 else jnp.logical_not(half)))
+            for l in range(3):
+                v = jnp.concatenate([shifted(cols[b], l, row) for b in range(2)], axis=0)
+                a_ref[l, (x + 1) % 2, (x + 1) // 2, y + 1] = split_halves(v, low)
+    out = convolve(a_ref, w_ref)
+    for b in range(2):
+        own_ref[b, :, 0] = out[:, :, b * 8:b * 8 + 8, :64]
+        own_ref[b, :, 1] = out[:, :, b * 8:b * 8 + 8, 64:]
+
+
+def unpack_code(code_ref, b, k):
+    c = code_ref[b * 26 + k]
+    return c >> 4, (c >> 1) & 7, c & 1
+
+
+def edge_rows(pos):
+    e = pos - 2
+    return pl.ds(pl.multiple_of(64 + 8 * (e >> 1), 8), 8), e & 1
+
+
+def halo_kernel(code_ref, recv_ref, own_ref, mask_ref, cot_ref, wf_ref, wb_ref,
+                act_ref, dpre_ref, send_ref, pre, px, py, zf, pz, qx, qy, qz, rx, ry, rz, tmp):
+    high8 = half_of((8, 128))
+    half8 = high8.astype(jnp.int32)
+    row = lax.broadcasted_iota(jnp.int32, (8, 128), 0)
+    low = jnp.logical_not(half_of((16, 128)))
+    spare = jnp.zeros((16, 128), BF16)
+
+    def zrow(s, x, y, b):
+        return ((s * 10 + x) * 10 + y) * 16 + b
+
+    for s in range(2):
+        for l in range(3):
+            for g in range(6):
+                py[s, l, 0, 0, g] = spare
+                py[s, l, 1, 4, g] = spare
+        for x in range(10):
+            for y in range(10):
+                r = zrow(s, x, y, 8)
+                zf[r:r + 8, :] = jnp.zeros((8, 128), F32)
+
+    def face(k, b, i):
+        o, pos, alive = unpack_code(code_ref, b, k)
+        v = recv_ref[o, i * 8:i * 8 + 8, :]
+        return placed(v, half8 == pos) * alive.astype(F32)
+
+    def edge(k, b):
+        o, pos, alive = unpack_code(code_ref, b, k)
+        rows, h = edge_rows(pos)
+        return placed(recv_ref[o, rows, :], half8 == h) * alive.astype(F32)
+
+    for k, (dx, dy, dz) in enumerate(OFFSETS):
+        xt, yt = target_coord(dx), target_coord(dy)
+        sx, sy, sz = int(dx == 1), int(dy == 1), int(dz == 1)
+        for g in range(6):
+            pair = (2 * g, 2 * g + 1)
+            if KIND[k] == 0 and not dz:
+                for i in range(8):
+                    v = [face(k, b, i) for b in pair]
+                    for l in range(3):
+                        w = split_halves(jnp.concatenate([shifted(u, l, row) for u in v], axis=0), low)
+                        if dx:
+                            px[sx, l, i + 1, g] = w
+                        else:
+                            py[sy, l, (i + 1) % 2, (i + 1) // 2, g] = w
+            elif KIND[k] == 1 and not dz:
+                v = [edge(k, b) for b in pair]
+                for l in range(3):
+                    px[sx, l, yt, g] = split_halves(jnp.concatenate([shifted(u, l, row) for u in v], axis=0), low)
+            else:
+                for b in pair:
+                    if KIND[k] == 0:
+                        for i in range(8):
+                            zf[pl.ds(zrow(sz, i + 1, 1, b), 8, stride=16), :] = face(k, b, i)
+                    elif KIND[k] == 1 and dx:
+                        zf[pl.ds(zrow(sz, xt, 1, b), 8, stride=16), :] = edge(k, b)
+                    elif KIND[k] == 1:
+                        zf[pl.ds(zrow(sz, 1, yt, b), 8, stride=160), :] = edge(k, b)
+                    else:
+                        o, pos, alive = unpack_code(code_ref, b, k)
+                        v = recv_ref[o, 72:80, :]
+                        v = jnp.where(pos == 5, v[0:1, :], v[1:2, :])
+                        r = zrow(sz, xt, yt, b)
+                        zf[r:r + 1, :] = placed(v, high8[0:1]) * alive.astype(F32)
+    for s in range(2):
+        for x in range(10):
+            for y in range(10):
+                r = zrow(s, x, y, 0)
+                pz[s, x % 2, x // 2, y] = split_halves(zf[r:r + 16, :], low)
+
+    def side_x(src, s, ii, ys, w_ref):
+        parts = [src[s, l, j:j + ys].reshape(ys * 96, 128) for j in range(3) for l in range(3)]
+        v = jnp.dot(jnp.concatenate(parts, axis=1), w_ref[ii * 1152:ii * 1152 + 1152, :], preferred_element_type=F32)
+        return v[:, :128] + v[:, 128:]
+
+    def side_y(src, s, j, w_ref):
+        acc = None
+        for h in range(2):
+            parts = [src[s, l, i, h:h + 4].reshape(384, 128) for i in range(2) for l in range(3)]
+            at = [((2 * h + i) * 9 + j * 3) * 128 for i in range(2)]
+            w = jnp.concatenate([w_ref[a:a + 384, :] for a in at], axis=0)
+            v = jnp.dot(jnp.concatenate(parts, axis=1), w, preferred_element_type=F32)
+            acc = v if acc is None else acc + v
+        return acc[:, :128] + acc[:, 128:]
+
+    def side_z(src, s, l, xs, ys, w_ref):
+        slices = [(i, j) for i in range(4) for j in range(3)]
+        acc = None
+        for n in range(0, 12, 4):
+            parts = [src[s, i % 2, i // 2:i // 2 + xs, j:j + ys].reshape(xs * ys * 16, 128) for i, j in slices[n:n + 4]]
+            at = [(i * 9 + j * 3 + l) * 128 for i, j in slices[n:n + 4]]
+            w = jnp.concatenate([w_ref[a:a + 128, :] for a in at], axis=0)
+            v = jnp.dot(jnp.concatenate(parts, axis=1), w, preferred_element_type=F32)
+            acc = v if acc is None else acc + v
+        return acc[:, :128] + acc[:, 128:]
+
+    def prow(b, xh, y, z):
+        return ((b * 4 + xh) * 8 + y) * 8 + z
+
+    pre[...] = own_ref[...]
+    for s in range(2):
+        v = side_x(px, s, 3 * s, 8, wf_ref)
+        for y in range(8):
+            for b in range(12):
+                r, q = prow(b, 3 * s, y, 0), (y * 12 + b) * 8
+                pre[r:r + 8, :] += v[q:q + 8]
+        v = side_y(py, s, 2 * s, wf_ref)
+        for xh in range(4):
+            for b in range(12):
+                r, q = prow(b, xh, 7 * s, 0), (xh * 12 + b) * 8
+                pre[r:r + 8, :] += v[q:q + 8]
+        v = side_z(pz, s, 2 * s, 4, 8, wf_ref)
+        for xh in range(4):
+            for y in range(8):
+                q = (xh * 8 + y) * 16
+                a = pl.ds(prow(0, xh, y, 7 * s), 8, stride=256)
+                pre[a, :] = pre[a, :] + v[q:q + 8]
+                a = pl.ds(prow(8, xh, y, 7 * s), 4, stride=256)
+                pre[a, :] = pre[a, :] + v[q + 8:q + 12]
+
+    def activate(n, carry):
+        a = pl.ds(pl.multiple_of(n * 128, 128), 128)
+        p = pre[a, :]
+        sig = jax.nn.sigmoid(p)
+        ps = p * sig
+        act_ref[a, :] = ps * mask_ref[a, :]
+        dpre_ref[a, :] = cot_ref[a, :] * (sig + ps * (1.0 - sig))
+        return carry
+
+    lax.fori_loop(0, 24, activate, 0)
+
+    for s in range(2):
+        for l in range(3):
+            for g in range(6):
+                for y in (0, 1, 10, 11):
+                    qx[s, l, y, g] = spare
+                qy[s, l, 0, 0, g] = spare
+                qy[s, l, 1, 4, g] = spare
+    qz[...] = jnp.zeros_like(qz)
+    wanted = [jnp.logical_not(high8), high8]
+    wanted16 = [low, jnp.logical_not(low)]
+    for s in range(2):
+        for g in range(6):
+            for y in range(8):
+                v = []
+                for b in (2 * g, 2 * g + 1):
+                    r = prow(b, 3 * s, y, 0)
+                    v.append(placed(dpre_ref[r:r + 8, :], wanted[s]))
+                for l in range(3):
+                    qx[s, l, y + 2, g] = split_halves(jnp.concatenate([shifted(u, l, row) for u in v], axis=0), low)
+            for x in range(8):
+                v = []
+                for b in (2 * g, 2 * g + 1):
+                    r = prow(b, x // 2, 7 * s, 0)
+                    v.append(placed(dpre_ref[r:r + 8, :], wanted[x % 2]))
+                for l in range(3):
+                    w = split_halves(jnp.concatenate([shifted(u, l, row) for u in v], axis=0), low)
+                    qy[s, l, (x + 1) % 2, (x + 1) // 2, g] = w
+        for xh in range(4):
+            for y in range(8):
+                first = dpre_ref[pl.ds(prow(0, xh, y, 7 * s), 8, stride=256), :]
+                last = dpre_ref[pl.ds(prow(8, xh, y, 7 * s), 4, stride=256), :]
+                v = jnp.concatenate([first, last, jnp.zeros((4, 128), F32)], axis=0)
+                for p in range(2):
+                    qz[s, p, xh + 1, y + 2] = split_halves(placed(v, wanted16[p]), low)
+    for s in range(2):
+        rx[s] = side_x(qx, s, 3 - 3 * s, 10, wb_ref)
+        ry[s] = side_y(qy, s, 2 - 2 * s, wb_ref)
+        rz[s * 800:s * 800 + 800, :] = side_z(qz, s, 2 - 2 * s, 5, 10, wb_ref)
+
+    def rzrow(s, xh, y, b):
+        return s * 800 + (xh * 10 + y) * 16 + b
+
+    send_ref[...] = jnp.zeros_like(send_ref)
+    for b in range(12):
+        for k, (dx, dy, dz) in enumerate(OFFSETS):
+            o, pos, _ = unpack_code(code_ref, b, k)
+            xt, yt = target_coord(dx), target_coord(dy)
+            sx, sy, sz = int(dx == 1), int(dy == 1), int(dz == 1)
+            if KIND[k] == 0:
+                for i in range(8):
+                    if dx:
+                        r, par = ((i + 1) * 12 + b) * 8, 1 - sx
+                        v = rx[sx, r:r + 8, :]
+                    elif dy:
+                        r, par = ((i // 2) * 12 + b) * 8, i % 2
+                        v = ry[sy, r:r + 8, :]
+                    else:
+                        par = (i + 1) % 2
+                        v = rz[pl.ds(rzrow(sz, (i + 1) // 2, 1, b), 8, stride=16), :]
+                    v = placed(v, wanted[par])
+                    a = slice(i * 8, i * 8 + 8)
+                    send_ref[o, a, :] = jnp.where(half8 == pos, v, send_ref[o, a, :])
+            elif KIND[k] == 1:
+                if not dz:
+                    r = (yt * 12 + b) * 8
+                    v = placed(rx[sx, r:r + 8, :], wanted[1 - sx])
+                elif dx:
+                    v = placed(rz[pl.ds(rzrow(sz, xt // 2, 1, b), 8, stride=16), :], wanted[xt % 2])
+                else:
+                    for q in range(2):
+                        tmp[pl.ds(q, 4, stride=2), :] = rz[pl.ds(rzrow(sz, q, yt, b), 4, stride=160), :]
+                    v = placed(tmp[...], half8 == 1 - (row & 1))
+                a, h = edge_rows(pos)
+                send_ref[o, a, :] = jnp.where(half8 == h, v, send_ref[o, a, :])
+            else:
+                r = rzrow(sz, xt // 2, yt, b)
+                v = placed(jnp.broadcast_to(rz[r:r + 1, :], (8, 128)), wanted[xt % 2])
+                spot = jnp.logical_and(row == pos - 5, high8)
+                send_ref[o, 72:80, :] = jnp.where(spot, v, send_ref[o, 72:80, :])
+
+
+def windows_kernel(code_ref, recv_ref, x_ref, m_ref, d_ref, a_ref, dt_ref, pf):
     g = pl.program_id(0)
-    high8 = lax.broadcasted_iota(jnp.int32, (8, 128), 1) >= 64
+    high8 = half_of((8, 128))
     half8 = high8.astype(jnp.int32)
-    rowi = lax.broadcasted_iota(jnp.int32, (8, 128), 0)
-
-    @pl.when(g == 0)
-    def _():
-        dpad[...] = jnp.zeros_like(dpad)
-        send_ref[...] = jnp.zeros_like(send_ref)
 
     def prow(b, x, y, z):
         return ((b * 10 + x) * 10 + y) * PITCH + z
-
-    def fetch(k, b):
-        c = code_ref[(2 * g + b) * 26 + k]
-        return c >> 4, (c >> 1) & 7, c & 1
 
     for b in range(2):
         for x in range(8):
@@ -118,39 +413,36 @@
                 r = prow(b, x + 1, y + 1, 8)
                 pf[r:r + 8, :] = v[y]
     for b in range(2):
-        for k, (a, bb, c) in enumerate(OFFSETS):
-            o, pos, alive = fetch(k, b)
+        for k, (dx, dy, dz) in enumerate(OFFSETS):
+            o, pos, alive = unpack_code(code_ref, 2 * g + b, k)
             scale = alive.astype(F32)
-            xt, yt, zt = target_coord(a), target_coord(bb), z_row(c)
+            xt, yt, zt = target_coord(dx), target_coord(dy), z_row(dz)
             if KIND[k] == 0:
                 for i in range(8):
-                    v = recv_ref[o, i * 8:i * 8 + 8, :]
-                    v = jnp.where(half8 == pos, v, swap(v)) * scale
-                    if a:
+                    v = placed(recv_ref[o, i * 8:i * 8 + 8, :], half8 == pos) * scale
+                    if dx:
                         r = prow(b, xt, i + 1, 8)
                         pf[r:r + 8, :] = v
-                    elif bb:
+                    elif dy:
                         r = prow(b, i + 1, yt, 8)
                         pf[r:r + 8, :] = v
                     else:
                         pf[pl.ds(prow(b, i + 1, 1, zt), 8, stride=PITCH), :] = v
             elif KIND[k] == 1:
-                e = pos - 2
-                v = recv_ref[o, pl.ds(pl.multiple_of(64 + 8 * (e >> 1), 8), 8), :]
-                v = jnp.where(half8 == (e & 1), v, swap(v)) * scale
-                if not c:
+                rows, h = edge_rows(pos)
+                v = placed(recv_ref[o, rows, :], half8 == h) * scale
+                if not dz:
                     r = prow(b, xt, yt, 8)
                     pf[r:r + 8, :] = v
-                elif not bb:
+                elif dx:
                     pf[pl.ds(prow(b, xt, 1, zt), 8, stride=PITCH), :] = v
                 else:
                     pf[pl.ds(prow(b, 1, yt, zt), 8, stride=10 * PITCH), :] = v
             else:
                 v = recv_ref[o, 72:80, :]
                 v = jnp.where(pos == 5, v[0:1, :], v[1:2, :])
-                v = jnp.where(high8[0:1], v, swap(v)) * scale
                 r = prow(b, xt, yt, zt)
-                pf[r:r + 1, :] = v
+                pf[r:r + 1, :] = placed(v, high8[0:1]) * scale
     low = jnp.logical_not(half_of((16, 128)))
     for l in range(3):
         for x in range(10):
@@ -158,98 +450,10 @@
                 r0, r1 = prow(0, x, y, 7 + l), prow(1, x, y, 7 + l)
                 v = jnp.concatenate([pf[r0:r0 + 8, :], pf[r1:r1 + 8, :]], axis=0)
                 a_ref[l, 0, x % 2, x // 2, y] = split_halves(v, low)
-    acc = None
-    for i in range(4):
-        for j in range(3):
-            parts = [a_ref[l, 0, i % 2, i // 2:i // 2 + 4, j:j + 8].reshape(512, 128) for l in range(3)]
-            lhs = jnp.concatenate(parts, axis=1)
-            at = (i * 3 + j) * 384
-            d = jnp.dot(lhs, wf_ref[at:at + 384, :], preferred_element_type=F32)
-            acc = d if acc is None else acc + d
-    pre = acc[:, :128] + acc[:, 128:] + bias_ref[...]
-    mask = packed(m_ref)
-    sig = jax.nn.sigmoid(pre)
-    act = (pre * sig * mask).reshape(4, 8, 16, 128)
-    for b in range(2):
-        act_ref[b, :, 0] = act[:, :, b * 8:b * 8 + 8, :64]
-        act_ref[b, :, 1] = act[:, :, b * 8:b * 8 + 8, 64:]
-    dpre = packed(cot_ref) * mask * (sig + pre * sig * (1.0 - sig))
-    lowl = jnp.logical_not(half_of((512, 128)))
-    turned = swap(dpre)
-    for p in range(2):
-        v = jnp.where(lowl, dpre, turned) if p == 0 else jnp.where(lowl, turned, dpre)
-        dpad[p, 1:5, 2:10] = split_halves(v, lowl).reshape(4, 8, 16, 128)
-    t = dpre.T
+    t = jnp.concatenate([d_ref[0], d_ref[1]], axis=2).reshape(512, 128).T
     top = t.astype(BF16)
     dt_ref[0:128, :] = top
     dt_ref[128:256, :] = (t - top.astype(F32)).astype(BF16)
-    acc = None
-    for i in range(4):
-        parts = [dpad[i % 2, i // 2:i // 2 + 5, j:j + 10].reshape(800, 128) for j in range(3)]
-        lhs = jnp.concatenate(parts, axis=1)
-        d = jnp.dot(lhs, wb_ref[i * 384:i * 384 + 384, :], preferred_element_type=F32)
-        acc = d if acc is None else acc + d
-    y3 = (acc[:, :384] + acc[:, 384:]).reshape(5, 10, 16, 384)
-
-    def drow(b, x, y, z):
-        return ((b * 5 + x) * 10 + y) * PITCH + z
-
-    zero = jnp.zeros((8, 128), F32)
-    for b in range(2):
-        for x in range(5):
-            for y in range(10):
-                v = y3[x, y, b * 8:b * 8 + 8]
-                r = drow(b, x, y, 0)
-                dxf[r:r + 8, :] = zero
-                dxf[r + 16:r + 24, :] = zero
-                dxf[r + 8:r + 16, :] = v[:, 128:256]
-                dxf[r + 7:r + 15, :] += v[:, :128]
-                dxf[r + 9:r + 17, :] += v[:, 256:]
-    for b in range(2):
-        for x in range(8):
-            for y in range(8):
-                r = drow(b, (x + 1) // 2, y + 1, 8)
-                v = dxf[r:r + 8, :]
-                own_ref[b, x // 2, x % 2, y] = v[:, :64] if (x + 1) % 2 == 0 else v[:, 64:]
-        for k, (a, bb, c) in enumerate(OFFSETS):
-            o, pos, _ = fetch(k, b)
-            xt, yt, zt = target_coord(a), target_coord(bb), z_row(c)
-            if KIND[k] == 0:
-                for i in range(8):
-                    xx = xt if a else i + 1
-                    if a:
-                        r = drow(b, xx // 2, i + 1, 8)
-                        v = dxf[r:r + 8, :]
-                    elif bb:
-                        r = drow(b, xx // 2, yt, 8)
-                        v = dxf[r:r + 8, :]
-                    else:
-                        v = dxf[pl.ds(drow(b, xx // 2, 1, zt), 8, stride=PITCH), :]
-                    v = jnp.where(half8 == xx % 2, v, swap(v))
-                    s = slice(i * 8, i * 8 + 8)
-                    send_ref[o, s, :] = jnp.where(half8 == pos, v, send_ref[o, s, :])
-            elif KIND[k] == 1:
-                par = jnp.full((8, 128), xt % 2, jnp.int32)
-                if not c:
-                    r = drow(b, xt // 2, yt, 8)
-                    v = dxf[r:r + 8, :]
-                elif not bb:
-                    v = dxf[pl.ds(drow(b, xt // 2, 1, zt), 8, stride=PITCH), :]
-                else:
-                    for q in range(2):
-                        tmp[pl.ds(q, 4, stride=2), :] = dxf[pl.ds(drow(b, q, yt, zt), 4, stride=10 * PITCH), :]
-                    v = tmp[...]
-                    par = 1 - (rowi & 1)
-                v = jnp.where(half8 == par, v, swap(v))
-                e = pos - 2
-                s = pl.ds(pl.multiple_of(64 + 8 * (e >> 1), 8), 8)
-                send_ref[o, s, :] = jnp.where(half8 == (e & 1), v, send_ref[o, s, :])
-            else:
-                r = drow(b, xt // 2, yt, zt)
-                v = jnp.broadcast_to(dxf[r:r + 1, :], (8, 128))
-                v = jnp.where(half8 == xt % 2, v, swap(v))
-                spot = jnp.logical_and(rowi == pos - 5, high8)
-                send_ref[o, 72:80, :] = jnp.where(spot, v, send_ref[o, 72:80, :])
 
 
 def kernel_grad_kernel(a_ref, dt_ref, out_ref):
@@ -330,24 +534,21 @@
     out_ref[...] = rows[...].reshape(out_ref.shape) * m_ref[...]
 
 
-def two_terms(w):
-    top = lax.reduce_precision(w, 8, 7)
-    return jnp.stack([top, w - top], axis=0)
-
-
-def layer_weights(weight):
-    w = weight.reshape(3, 3, 3, 64, 64)
-    zero = jnp.zeros((1, 3, 3, 64, 64), F32)
-    sides = jnp.stack([jnp.concatenate([w, zero]), jnp.concatenate([zero, w])])
-    f = two_terms(sides)
-    f = f.transpose(2, 3, 4, 5, 0, 1, 6)
-    f = jnp.broadcast_to(f[:, :, :, None], (4, 3, 3, 2, 64, 2, 2, 64)).reshape(36 * 128, 256).astype(BF16)
-    r = w[::-1, ::-1]
-    sides = jnp.stack([jnp.concatenate([r, zero]), jnp.concatenate([zero, r])])
-    b = two_terms(sides)
-    b = b.transpose(2, 3, 6, 0, 4, 1, 5)
-    b = jnp.broadcast_to(b[:, :, None], (4, 3, 2, 64, 2, 3, 2, 64)).reshape(12 * 128, 768).astype(BF16)
-    return f, b
+def share_out(v):
+    scene, brick = lax.axis_index("scene"), lax.axis_index("brick")
+    v = v.reshape(2, 64, 7, 128)
+    mine = lax.dynamic_index_in_dim(v, scene, 0, keepdims=False)
+    theirs = lax.dynamic_index_in_dim(v, 1 - scene, 0, keepdims=False)
+    v = mine + lax.ppermute(theirs, "scene", [(0, 1), (1, 0)])
+    for stride in (16, 4, 1):
+        v = v.reshape(4, stride, 7, 128)
+        at = (brick // stride) % 4
+        total = lax.dynamic_index_in_dim(v, at, 0, keepdims=False)
+        for d in (1, 2, 3):
+            part = lax.dynamic_index_in_dim(v, at ^ d, 0, keepdims=False)
+            total = total + lax.ppermute(part, "brick", [(n, n ^ (d * stride)) for n in range(64)])
+        v = total
+    return v.reshape(896)[:864]
 
 
 def whole(memory=pltpu.VMEM):
@@ -388,6 +589,16 @@
     code = (peer * 8 + place) * 2 + alive
     asked = lax.all_to_all(wanted, "brick", split_axis=0, concat_axis=0, tiled=True)
 
+    wf, wb = pl.pallas_call(
+        weights_kernel,
+        in_specs=[whole()],
+        out_specs=[whole(), whole()],
+        out_shape=[jax.ShapeDtypeStruct((4608, 256), BF16)] * 2,
+        compiler_params=params(),
+        cost_estimate=pl.CostEstimate(flops=0, bytes_accessed=6000000, transcendentals=0),
+        name="weights",
+    )(weight)
+
     faces, edges, corners = pl.pallas_call(
         tables_kernel,
         grid=(12,),
@@ -413,48 +624,78 @@
     )(asked, faces, edges, corners)
     recv = lax.all_to_all(out, "brick", split_axis=0, concat_axis=0, tiled=True)
 
-    wf, wb = layer_weights(weight)
     bias2 = jnp.concatenate([bias, bias]).reshape(1, 128)
     brick_block = lead_block((2, 4, 2, 8, 8, 64))
     brick_shape = jax.ShapeDtypeStruct((12, 4, 2, 8, 8, 64), F32)
-    act, own, send, windows, dpre_t = pl.pallas_call(
-        layer_kernel,
+    packed_block = lead_block((2, 4, 8, 8, 128))
+    packed_shape = jax.ShapeDtypeStruct((12, 4, 8, 8, 128), F32)
+    window_scratch = pltpu.VMEM((3, 2, 5, 10, 16, 128), BF16)
+    own_pre, mask_p, cot_p = pl.pallas_call(
+        own_forward_kernel,
+        grid=(6,),
+        in_specs=[brick_block] * 3 + [const_block((4608, 256)), const_block((1, 128))],
+        out_specs=[packed_block] * 3,
+        out_shape=[packed_shape] * 3,
+        scratch_shapes=[window_scratch],
+        compiler_params=params(),
+        cost_estimate=pl.CostEstimate(flops=2 * 3072 * 4608 * 256, bytes_accessed=15000000, transcendentals=0),
+        name="own_forward",
+    )(x, mask, cot, wf, bias2)
+
+    flat = (3072, 128)
+    act, dpre, send = pl.pallas_call(
+        halo_kernel,
+        in_specs=[whole(pltpu.SMEM)] + [whole()] * 6,
+        out_specs=[whole()] * 3,
+        out_shape=[
+            jax.ShapeDtypeStruct(flat, F32),
+            jax.ShapeDtypeStruct(flat, F32),
+            jax.ShapeDtypeStruct((64, 80, 128), F32),
+        ],
+        scratch_shapes=[
+            pltpu.VMEM(flat, F32),
+            pltpu.VMEM((2, 3, 10, 6, 16, 128), BF16),
+            pltpu.VMEM((2, 3, 2, 5, 6, 16, 128), BF16),
+            pltpu.VMEM((3200, 128), F32),
+            pltpu.VMEM((2, 2, 5, 10, 16, 128), BF16),
+            pltpu.VMEM((2, 3, 12, 6, 16, 128), BF16),
+            pltpu.VMEM((2, 3, 2, 5, 6, 16, 128), BF16),
+            pltpu.VMEM((2, 2, 6, 12, 16, 128), BF16),
+            pltpu.VMEM((2, 960, 128), F32),
+            pltpu.VMEM((2, 384, 128), F32),
+            pltpu.VMEM((1600, 128), F32),
+            pltpu.VMEM((8, 128), F32),
+        ],
+        compiler_params=params(),
+        name="halo",
+    )(code, recv, own_pre.reshape(flat), mask_p.reshape(flat), cot_p.reshape(flat), wf, wb)
+    back = lax.all_to_all(send, "brick", split_axis=0, concat_axis=0, tiled=True)
+    act = act.reshape(12, 4, 8, 8, 2, 64).transpose(0, 1, 4, 2, 3, 5)
+    dpre = dpre.reshape(12, 4, 8, 8, 128)
+
+    windows, dpre_t = pl.pallas_call(
+        windows_kernel,
         grid=(6,),
         in_specs=[
             pl.BlockSpec(memory_space=pltpu.SMEM),
             const_block((64, 80, 128)),
             brick_block,
             brick_block,
-            brick_block,
-            const_block((36 * 128, 256)),
-            const_block((12 * 128, 768)),
-            const_block((1, 128)),
+            packed_block,
         ],
         out_specs=[
-            brick_block,
-            brick_block,
-            const_block((64, 80, 128)),
             pl.BlockSpec((3, 1, 2, 5, 10, 16, 128), lambda g: (0, g, 0, 0, 0, 0, 0)),
             pl.BlockSpec((256, 512), lambda g: (0, g)),
         ],
         out_shape=[
-            brick_shape,
-            brick_shape,
-            jax.ShapeDtypeStruct((64, 80, 128), F32),
             jax.ShapeDtypeStruct((3, 6, 2, 5, 10, 16, 128), BF16),
             jax.ShapeDtypeStruct((256, 3072), BF16),
         ],
-        scratch_shapes=[
-            pltpu.VMEM((200 * PITCH, 128), F32),
-            pltpu.VMEM((2, 6, 12, 16, 128), BF16),
-            pltpu.VMEM((100 * PITCH, 128), F32),
-            pltpu.VMEM((8, 128), F32),
-        ],
-        compiler_params=params(),
-        name="layer",
-    )(code, recv, x, mask, cot, wf, wb, bias2)
-    back = lax.all_to_all(send, "brick", split_axis=0, concat_axis=0, tiled=True)
-
+        scratch_shapes=[pltpu.VMEM((200 * PITCH, 128), F32)],
+        compiler_params=params(),
+        cost_estimate=pl.CostEstimate(flops=0, bytes_accessed=30000000, transcendentals=0),
+        name="windows",
+    )(code, recv, x, mask, dpre)
     z = pl.pallas_call(
         kernel_grad_kernel,
         grid=(3,),
@@ -471,9 +712,20 @@
     kernel = z[:, :, 0:3, 0:64] + z[:, :, 1:4, 64:128]
     kernel = kernel.transpose(2, 1, 0, 4, 3).reshape(128, 864)
     kernel = jnp.pad(kernel, ((0, 0), (0, 32))).reshape(128, 7, 128)
-    shares = lax.all_to_all(kernel, ("scene", "brick"), split_axis=0, concat_axis=0, tiled=True)
     scale = 1.0 / math.sqrt(float(2 * 768 * 512))
-    share = jnp.sum(shares, axis=0).reshape(896)[:864] * scale
+    share = share_out(kernel) * scale
+
+    own = pl.pallas_call(
+        own_backward_kernel,
+        grid=(6,),
+        in_specs=[packed_block, const_block((4608, 256))],
+        out_specs=brick_block,
+        out_shape=brick_shape,
+        scratch_shapes=[window_scratch],
+        compiler_params=params(),
+        cost_estimate=pl.CostEstimate(flops=2 * 3072 * 4608 * 256, bytes_accessed=15000000, transcendentals=0),
+        name="own_backward",
+    )(dpre, wb)
 
     grad = pl.pallas_call(
         collect_kernel,

time: 251 us -> 195 us (0.78)
  local copies, waits for them, and re-layouts: 61.6 us -> 24.7 us
  blocking collectives: 22.5 us -> 0 us
  starting transfers between devices: 27.4 us -> 41.7 us
  waiting for transfers between devices: 31.2 us -> 24.4 us
  other arithmetic: 11.3 us -> 7.39 us
    all_to_all x1, waiting for transfers between devices: 31.1 us -> 0.01 us  [on_device(): lax.all_to_all(send, 'brick', split_axis=0, concat_axis=0, tiled=True)]
    convert_element_type x4 -> x0, local copies, waits for them, and re-layouts: 27.9 us -> none  [the longest x2 15.9 us: layer_weights(): jnp.broadcast_to(b[:, :, None], (4, 3, 2, 64, 2, 3, 2, 64))]
    all_to_all x1 -> x0, blocking collectives: 22.5 us -> none  [on_device(): lax.all_to_all(kernel, ('scene', 'brick'), split_axis=0, concat_axis=0, t...]
    all_to_all x1, waiting for transfers between devices: 0.01 us -> 13.9 us  [on_device(): recv = lax.all_to_all(out, 'brick', split_axis=0, concat_axis=0, tiled=True)]
    ppermute x0 -> x10, starting transfers between devices: none -> 12.6 us  [the longest x9 12.5 us: share_out(): lax.ppermute(part, 'brick', [(n, n ^ d * stride) for n in range(64)])]
    ppermute x0 -> x10, waiting for transfers between devices: none -> 10.5 us  [the longest x9 9.04 us: share_out(): lax.ppermute(part, 'brick', [(n, n ^ d * stride) for n in range(64)])]
    broadcast_in_dim x2 -> x0, local copies, waits for them, and re-layouts: 9.46 us -> none  [the longest x1 5.6 us: layer_weights(): jnp.broadcast_to(b[:, :, None], (4, 3, 2, 64, 2, 3, 2, 64))]
    reshape x1 -> x2, local copies, waits for them, and re-layouts: 0.23 us -> 5.34 us  [on_device(): act = act.reshape(12, 4, 8, 8, 2, 64).transpose(0, 1, 4, 2, 3, 5)]
  transfers between devices with their start and end apart: 3 -> 13, of which waited for: 1 -> 6; matrix products, arithmetic and copies ran while one was open for 24% -> 11% of each run, Pallas kernels for 4% -> 31%
where the time goes in v2:
time: 195 us; the launch traced here: 194 us
  Pallas kernels  94.8 us (49%)
  starting transfers between devices  41.7 us (21%)
  local copies, waits for them, and re-layouts  24.7 us (13%)
  waiting for transfers between devices  24.4 us (13%)
  other arithmetic  7.39 us (4%)
    pallas_call x1, Pallas kernels, on_device(): pl.pallas_call(halo_kernel, in_specs=[whole(pltpu.SMEM)] + [whole()] * 6,...  18.1 us
    unnamed x10, local copies, waits for them, and re-layouts  15.1 us
    all_to_all x1, waiting for transfers between devices, on_device(): recv = lax.all_to_all(out, 'brick', split_axis=0, concat_axis=0, tiled=True)  13.9 us
    ppermute x9, starting transfers between devices, share_out(): lax.ppermute(part, 'brick', [(n, n ^ d * stride) for n in range(64)])  12.5 us
    pallas_call x1, Pallas kernels, on_device(): pl.pallas_call(own_forward_kernel, grid=(6,), in_specs=[brick_block] * 3...  12.5 us
    pallas_call x1, Pallas kernels, on_device(): pl.pallas_call(collect_kernel, grid=(12,), in_specs=[pl.BlockSpec(memory_...  12.2 us
    pallas_call x1, Pallas kernels, on_device(): pl.pallas_call(own_backward_kernel, grid=(6,), in_specs=[packed_block, co...  12.1 us
    all_to_all x1, starting transfers between devices, on_device(): lax.all_to_all(wanted, 'brick', split_axis=0, concat_axis=0, tiled=True)  11.5 us
  transfers between devices with their start and end apart: 13, of which 6 were waited for; matrix products, arithmetic and copies ran while one was open for 11% of the time, Pallas kernels for 31%

profile of v2, /device:TPU:0, one launch (start us, length us, event | category | flops | bytes accessed | tf_op | source)
XLA Modules:
  0.0 193.9 jit_solution(14232594108403099576)
XLA Ops:
  0.6 0.7 reduce.2
  1.3 0.1 reshape.97
  1.4 0.8 add_reduce_fusion.1
  2.2 0.1 mul.32
  2.3 0.1 reshape.114
  2.4 0.1 convert_reduce_fusion
  2.5 0.8 add_reduce_fusion
  3.3 0.1 reshape.120
  3.3 1.3 compare_select_fusion
  4.6 0.2 select_reduce_fusion
  4.8 0.7 sub.18
  5.5 11.5 %all-to-all-start = ((s32[64,1,8]{2,1,0:T(1,128)}), s32[64,1,8]{2,1,0:T(1,128)S(1)}, u32[]{:S(2)}, u32[]{:S(2)}) async-start(s32[64,1,8]{2,1,0:T(1,128)} %bitcast), calls=%async_computation | async-start | bytes 65536 | tf_op jit(solution)/shard_map/all_to_all | solution.py:590
  17.0 0.8 convert_reduce_fusion.1
  17.8 3.4 %copy.33 = f32[1,12,512,64]{3,2,1,0:T(8,128)} copy(f32[1,12,512,64]{2,3,1,0:T(8,128)} %param.12) | data formatting | bytes 3145728 | tf_op args[0]
  21.2 0.2 convert_element_type.17
  21.4 2.2 %broadcast_in_dim.32.m_ref = f32[12,4,2,8,8,64]{5,4,3,2,1,0:T(8,128)} broadcast(f32[12,4,2,8,8]{4,3,2,1,0:T(8,128)S(1)} %convert_element_type.17), dimensions={0,1,2,3,4} | broadcast | bytes 1597440 | tf_op jit(solution)/shard_map/broadcast_in_dim | solution.py:573
  23.6 9.1 %tables.1 = (f32[72,64,128]{2,1,0:T(8,128)}, f32[144,8,128]{2,1,0:T(8,128)}, f32[96,8,128]{2,1,0:T(8,128)}) custom-call(f32[12,4,2,8,8,64]{5,4,3,2,1,0:T(8,128)} %bitcast.50, f32[12,4,2,8,8,64]{5,4,3,2,1,0:T(8,128)} %broadcast_in_dim.32.m_ref), custom_call_target="tpu_custom_call" | custom-call | tf_op jit(solution)/shard_map/tables/pallas_call | solution.py:602
  32.7 0.0 all-to-all-done
  32.7 0.6 copy-done.1
  33.3 4.5 %pack.1 = f32[64,80,128]{2,1,0:T(8,128)} custom-call(s32[64,8]{1,0:T(8,128)} %bitcast.63, f32[72,64,128]{2,1,0:T(8,128)} %get-tuple-element.16.face_ref, f32[144,8,128]{2,1,0:T(8,128)} %get-tuple-element.17.edge_ref, f32[96,8,128]{2,1,0:T(8,128)} %get-tuple-element.18.corner_ref), custom_call_target="tpu_custom_call" | custom-call | tf_op jit(solution)/shard_map/pack/pallas_call | solution.py:617
  37.9 10.5 %all-to-all-start.1 = ((f32[64,80,128]{2,1,0:T(8,128)}), f32[64,80,128]{2,1,0:T(8,128)S(1)}, u32[]{:S(2)}, u32[]{:S(2)}) async-start(f32[64,80,128]{2,1,0:T(8,128)} %pack.1), calls=%async_computation.1 | async-start | bytes 5242880 | tf_op jit(solution)/shard_map/all_to_all | solution.py:625
  48.4 0.0 copy-start.2
  48.4 3.3 %copy.34 = f32[1,12,512,64]{3,2,1,0:T(8,128)} copy(f32[1,12,512,64]{2,3,1,0:T(8,128)} %param.16) | data formatting | bytes 3145728 | tf_op args[4]
  51.6 4.1 %weights.1 = (bf16[4608,256]{1,0:T(8,128)(2,1)}, bf16[4608,256]{1,0:T(8,128)(2,1)}) custom-call(f32[27,64,64]{2,1,0:T(8,128)} %w_ref.1), custom_call_target="tpu_custom_call" | custom-call | bytes 6000000 | tf_op jit(solution)/shard_map/weights/pallas_call | solution.py:592
  55.7 0.6 maximum_bitcast_fusion.bias_ref
  56.3 12.5 %own_forward.1 = (f32[12,4,8,8,128]{4,3,2,1,0:T(8,128)}, f32[12,4,8,8,128]{4,3,2,1,0:T(8,128)}, f32[12,4,8,8,128]{4,3,2,1,0:T(8,128)}) custom-call(f32[12,4,2,8,8,64]{5,4,3,2,1,0:T(8,128)} %bitcast.51, f32[12,4,2,8,8,64]{5,4,3,2,1,0:T(8,128)} %broadcast_in_dim.32.m_ref, f32[12,4,2,8,8,64]{5,4,3,2,1,0:T(8,128)} %bitcast.55, ...), custom_call_target="tpu_custom_call" | custom-call | flops 7247757312 | bytes 15000000 | tf_op jit(solution)/shard_map/own_forward/pallas_call | solution.py:633
  68.8 13.9 %all-to-all-done.1.recv_ref = f32[64,80,128]{2,1,0:T(8,128)S(1)} async-done(((f32[64,80,128]{2,1,0:T(8,128)}), f32[64,80,128]{2,1,0:T(8,128)S(1)}, u32[]{:S(2)}, u32[]{:S(2)}) %all-to-all-start.1) | async-done | bytes 2621472 | tf_op jit(solution)/shard_map/all_to_all | solution.py:625
  82.7 1.5 copy-done
  84.2 18.1 %halo.1 = (f32[3072,128]{1,0:T(8,128)}, f32[3072,128]{1,0:T(8,128)}, f32[64,80,128]{2,1,0:T(8,128)}) custom-call(s32[312]{0:T(512)} %get-tuple-element.53.code_ref, f32[64,80,128]{2,1,0:T(8,128)} %copy-done, f32[3072,128]{1,0:T(8,128)} %bitcast.56, f32[3072,128]{1,0:T(8,128)} %bitcast.57, f32[3072,128]{1,0:T(8,128)} %bitcast.58, ...), custom_call_target="tpu_custom_call" | custom-call | tf_op jit(solution)/shard_map/halo/pallas_call | solution.py:646
  102.3 7.1 %all-to-all-start.2 = ((f32[64,80,128]{2,1,0:T(8,128)}), f32[64,80,128]{2,1,0:T(8,128)}, u32[]{:S(2)}, u32[]{:S(2)}) async-start(f32[64,80,128]{2,1,0:T(8,128)} %get-tuple-element.25), calls=%async_computation.2 | async-start | bytes 5242880 | tf_op jit(solution)/shard_map/all_to_all | solution.py:672
  109.4 10.9 %windows.1 = (bf16[3,6,2,5,10,16,128]{6,5,4,3,2,1,0:T(8,128)(2,1)}, bf16[256,3072]{1,0:T(8,128)(2,1)}) custom-call(s32[312]{0:T(512)} %get-tuple-element.53.code_ref, f32[64,80,128]{2,1,0:T(8,128)} %copy-done, f32[12,4,2,8,8,64]{5,4,3,2,1,0:T(8,128)} %bitcast.52, f32[12,4,2,8,8,64]{5,4,3,2,1,0:T(8,128)} %broadcast_in_dim.32.m_ref, f32[12,4,8,8,128]{4,3,2,1,0:T(8,128)} %bitcast.59), custom_call_target="tpu_custom_call" | custom-call | bytes 30000000 | tf_op jit(solution)/shard_map/windows/pallas_call | solution.py:676
  120.3 11.2 %kernel_grad.1 = f32[3,3,4,128,64]{4,3,2,1,0:T(8,128)} custom-call(bf16[3,6,2,5,10,16,128]{6,5,4,3,2,1,0:T(8,128)(2,1)} %get-tuple-element.27.a_ref, bf16[256,3072]{1,0:T(8,128)(2,1)} %get-tuple-element.28.dt_ref), custom_call_target="tpu_custom_call" | custom-call | flops 7247757312 | bytes 11000000 | tf_op jit(solution)/shard_map/kernel_grad/pallas_call | solution.py:699
  131.5 1.5 fusion
  133.0 0.3 copy.36
  133.3 0.3 reshape.109
  133.7 0.1 reshape_reshape.3
  133.8 0.1 collective-permute-start
  133.9 1.5 collective-permute-done
  135.5 3.0 %collective-permute-start.3 = (f32[16,7,128]{2,1,0:T(8,128)S(1)}, f32[16,7,128]{2,1,0:T(8,128)S(1)}, u32[]{:S(2)}, u32[]{:S(2)}) collective-permute-start(f32[16,7,128]{2,1,0:T(8,128)S(1)} %get-tuple-element.44), channel_id=1, source_target_pairs={{0,48},{1,49},{2,50},{3,51},{4,52},{5,53},{6,54},{7,55},{8,56},{9,... | collective-permute-start | bytes 172040 | tf_op jit(solution)/shard_map/ppermute | solution.py:549
  138.5 0.7 collective-permute-start.2
  139.1 0.5 collective-permute-start.1
  139.7 4.4 %collective-permute-done.3 = f32[16,7,128]{2,1,0:T(8,128)S(1)} collective-permute-done((f32[16,7,128]{2,1,0:T(8,128)S(1)}, f32[16,7,128]{2,1,0:T(8,128)S(1)}, u32[]{:S(2)}, u32[]{:S(2)}) %collective-permute-start.3) | collective-permute-done | bytes 57376 | tf_op jit(solution)/shard_map/ppermute | solution.py:549
  144.0 0.9 collective-permute-done.2
  145.0 0.0 collective-permute-done.1
  145.0 2.6 %collective-permute-start.6 = (f32[4,7,128]{2,1,0:T(8,128)S(1)}, f32[4,7,128]{2,1,0:T(8,128)S(1)}, u32[]{:S(2)}, u32[]{:S(2)}) collective-permute-start(f32[4,7,128]{2,1,0:T(8,128)S(1)} %get-tuple-element.47), channel_id=1, source_target_pairs={{0,12},{1,13},{2,14},{3,15},{4,8},{5,9},{6,10},{7,11},{8,4},{9,5},... | collective-permute-start | bytes 43016 | tf_op jit(solution)/shard_map/ppermute | solution.py:549
  147.7 0.6 collective-permute-start.5
  148.2 0.9 collective-permute-start.4
  149.2 0.9 collective-permute-done.6
  150.0 2.9 %collective-permute-done.5 = f32[4,7,128]{2,1,0:T(8,128)S(1)} collective-permute-done((f32[4,7,128]{2,1,0:T(8,128)S(1)}, f32[4,7,128]{2,1,0:T(8,128)S(1)}, u32[]{:S(2)}, u32[]{:S(2)}) %collective-permute-start.5) | collective-permute-done | bytes 14368 | tf_op jit(solution)/shard_map/ppermute | solution.py:549
  152.9 0.0 collective-permute-done.4
  152.9 2.5 %collective-permute-start.9 = (f32[1,7,128]{2,1,0:T(8,128)S(1)}, f32[1,7,128]{2,1,0:T(8,128)S(1)}, u32[]{:S(2)}, u32[]{:S(2)}) collective-permute-start(f32[1,7,128]{2,1,0:T(8,128)S(1)} %get-tuple-element.50), channel_id=1, source_target_pairs={{0,3},{1,2},{2,1},{3,0},{4,7},{5,6},{6,5},{7,4},{8,11},{9,10},{10,... | collective-permute-start | bytes 10760 | tf_op jit(solution)/shard_map/ppermute | solution.py:549
  155.5 0.8 collective-permute-start.8
  156.3 0.8 collective-permute-start.7
  157.1 12.1 %own_backward.1.own_ref = f32[12,4,2,8,8,64]{5,4,3,2,1,0:T(8,128)} custom-call(f32[12,4,8,8,128]{4,3,2,1,0:T(8,128)} %bitcast.60, bf16[4608,256]{1,0:T(8,128)(2,1)} %get-tuple-element.23.wb_ref.w_ref), custom_call_target="tpu_custom_call" | custom-call | flops 7247757312 | bytes 15000000 | tf_op jit(solution)/shard_map/own_backward/pallas_call | solution.py:718
  169.3 3.2 %reshape.105 = f32[12,4,8,8,2,64]{5,4,3,2,1,0:T(2,128)S(1)} reshape(f32[3072,128]{1,0:T(8,128)} %get-tuple-element.24) | data formatting | bytes 3145728 | tf_op jit(solution)/shard_map/reshape | solution.py:673
  172.5 2.1 %copy.35 = f32[12,4,8,8,2,64]{5,3,2,4,1,0:T(8,128)} copy(f32[12,4,8,8,2,64]{5,4,3,2,1,0:T(2,128)S(1)} %reshape.105) | data formatting | bytes 3145728 | tf_op jit(solution)/shard_map/reshape | solution.py:673
  174.6 3.2 %copy.37 = f32[1,12,512,64]{2,3,1,0:T(8,128)} copy(f32[1,12,512,64]{3,2,1,0:T(8,128)} %bitcast.53) | data formatting | bytes 3145728
  177.8 0.0 collective-permute-done.9
  177.8 0.0 collective-permute-done.8
  177.8 0.0 collective-permute-done.7
  177.8 0.6 slice_multiply_fusion
  178.4 0.0 all-to-all-done.2.back_ref
  178.4 12.2 %collect.1 = f32[12,4,2,8,8,64]{5,4,3,2,1,0:T(8,128)} custom-call(s32[64,8]{1,0:T(8,128)} %bitcast.64, f32[64,80,128]{2,1,0:T(8,128)} %all-to-all-done.2.back_ref, f32[12,4,2,8,8,64]{5,4,3,2,1,0:T(8,128)} %own_backward.1.own_ref, f32[12,4,2,8,8,64]{5,4,3,2,1,0:T(8,128)} %broadcast_in_dim.32.m_ref), custom_call_target="tpu_custom_call" | custom-call | tf_op jit(solution)/shard_map/collect/pallas_call | solution.py:730
  190.7 3.2 %copy.38 = f32[1,12,512,64]{2,3,1,0:T(8,128)} copy(f32[1,12,512,64]{3,2,1,0:T(8,128)} %bitcast.54) | data formatting | bytes 3145728
  (13 shorter events, 0.2 us)
Async XLA Ops:
  5.5 27.2 %all-to-all-start = ((s32[64,1,8]{2,1,0:T(1,128)}), s32[64,1,8]{2,1,0:T(1,128)S(1)}, u32[]{:S(2)}, u32[]{:S(2)}) async-start(s32[64,1,8]{2,1,0:T(1,128)} %bitcast), calls=%async_computation | async-start | bytes 65536 | tf_op jit(solution)/shard_map/all_to_all | solution.py:590
  32.7 0.6 copy-start.1
  37.9 44.9 %all-to-all-start.1 = ((f32[64,80,128]{2,1,0:T(8,128)}), f32[64,80,128]{2,1,0:T(8,128)S(1)}, u32[]{:S(2)}, u32[]{:S(2)}) async-start(f32[64,80,128]{2,1,0:T(8,128)} %pack.1), calls=%async_computation.1 | async-start | bytes 5242880 | tf_op jit(solution)/shard_map/all_to_all | solution.py:625
  48.4 7.4 %copy-start.2 = (f32[64]{0:T(128)S(1)}, f32[64]{0:T(128)}, u32[]{:S(2)}) copy-start(f32[64]{0:T(128)} %param.15) | copy-start | bytes 772
  82.7 1.5 copy-start
  102.3 76.1 %all-to-all-start.2 = ((f32[64,80,128]{2,1,0:T(8,128)}), f32[64,80,128]{2,1,0:T(8,128)}, u32[]{:S(2)}, u32[]{:S(2)}) async-start(f32[64,80,128]{2,1,0:T(8,128)} %get-tuple-element.25), calls=%async_computation.2 | async-start | bytes 5242880 | tf_op jit(solution)/shard_map/all_to_all | solution.py:672
  133.8 1.6 collective-permute-start
  135.5 8.6 %collective-permute-start.3 = (f32[16,7,128]{2,1,0:T(8,128)S(1)}, f32[16,7,128]{2,1,0:T(8,128)S(1)}, u32[]{:S(2)}, u32[]{:S(2)}) collective-permute-start(f32[16,7,128]{2,1,0:T(8,128)S(1)} %get-tuple-element.44), channel_id=1, source_target_pairs={{0,48},{1,49},{2,50},{3,51},{4,52},{5,53},{6,54},{7,55},{8,56},{9,... | collective-permute-start | bytes 172040 | tf_op jit(solution)/shard_map/ppermute | solution.py:549
  138.5 6.5 %collective-permute-start.2 = (f32[16,7,128]{2,1,0:T(8,128)S(1)}, f32[16,7,128]{2,1,0:T(8,128)S(1)}, u32[]{:S(2)}, u32[]{:S(2)}) collective-permute-start(f32[16,7,128]{2,1,0:T(8,128)S(1)} %get-tuple-element.45), channel_id=1, source_target_pairs={{0,32},{1,33},{2,34},{3,35},{4,36},{5,37},{6,38},{7,39},{8,40},{9,... | collective-permute-start | bytes 172040 | tf_op jit(solution)/shard_map/ppermute | solution.py:549
  139.1 5.8 %collective-permute-start.1 = (f32[16,7,128]{2,1,0:T(8,128)S(1)}, f32[16,7,128]{2,1,0:T(8,128)S(1)}, u32[]{:S(2)}, u32[]{:S(2)}) collective-permute-start(f32[16,7,128]{2,1,0:T(8,128)S(1)} %get-tuple-element.43), channel_id=1, source_target_pairs={{0,16},{1,17},{2,18},{3,19},{4,20},{5,21},{6,22},{7,23},{8,24},{9,... | collective-permute-start | bytes 172040 | tf_op jit(solution)/shard_map/ppermute | solution.py:549
  145.0 5.0 %collective-permute-start.6 = (f32[4,7,128]{2,1,0:T(8,128)S(1)}, f32[4,7,128]{2,1,0:T(8,128)S(1)}, u32[]{:S(2)}, u32[]{:S(2)}) collective-permute-start(f32[4,7,128]{2,1,0:T(8,128)S(1)} %get-tuple-element.47), channel_id=1, source_target_pairs={{0,12},{1,13},{2,14},{3,15},{4,8},{5,9},{6,10},{7,11},{8,4},{9,5},... | collective-permute-start | bytes 43016 | tf_op jit(solution)/shard_map/ppermute | solution.py:549
  147.7 5.2 %collective-permute-start.5 = (f32[4,7,128]{2,1,0:T(8,128)S(1)}, f32[4,7,128]{2,1,0:T(8,128)S(1)}, u32[]{:S(2)}, u32[]{:S(2)}) collective-permute-start(f32[4,7,128]{2,1,0:T(8,128)S(1)} %get-tuple-element.48), channel_id=1, source_target_pairs={{0,8},{1,9},{2,10},{3,11},{4,12},{5,13},{6,14},{7,15},{8,0},{9,1},... | collective-permute-start | bytes 43016 | tf_op jit(solution)/shard_map/ppermute | solution.py:549
  148.2 4.7 %collective-permute-start.4 = (f32[4,7,128]{2,1,0:T(8,128)S(1)}, f32[4,7,128]{2,1,0:T(8,128)S(1)}, u32[]{:S(2)}, u32[]{:S(2)}) collective-permute-start(f32[4,7,128]{2,1,0:T(8,128)S(1)} %get-tuple-element.46), channel_id=1, source_target_pairs={{0,4},{1,5},{2,6},{3,7},{4,0},{5,1},{6,2},{7,3},{8,12},{9,13},{10,... | collective-permute-start | bytes 43016 | tf_op jit(solution)/shard_map/ppermute | solution.py:549
  152.9 24.9 %collective-permute-start.9 = (f32[1,7,128]{2,1,0:T(8,128)S(1)}, f32[1,7,128]{2,1,0:T(8,128)S(1)}, u32[]{:S(2)}, u32[]{:S(2)}) collective-permute-start(f32[1,7,128]{2,1,0:T(8,128)S(1)} %get-tuple-element.50), channel_id=1, source_target_pairs={{0,3},{1,2},{2,1},{3,0},{4,7},{5,6},{6,5},{7,4},{8,11},{9,10},{10,... | collective-permute-start | bytes 10760 | tf_op jit(solution)/shard_map/ppermute | solution.py:549
  155.5 22.3 %collective-permute-start.8 = (f32[1,7,128]{2,1,0:T(8,128)S(1)}, f32[1,7,128]{2,1,0:T(8,128)S(1)}, u32[]{:S(2)}, u32[]{:S(2)}) collective-permute-start(f32[1,7,128]{2,1,0:T(8,128)S(1)} %get-tuple-element.51), channel_id=1, source_target_pairs={{0,2},{1,3},{2,0},{3,1},{4,6},{5,7},{6,4},{7,5},{8,10},{9,11},{10,... | collective-permute-start | bytes 10760 | tf_op jit(solution)/shard_map/ppermute | solution.py:549
  156.3 21.5 %collective-permute-start.7 = (f32[1,7,128]{2,1,0:T(8,128)S(1)}, f32[1,7,128]{2,1,0:T(8,128)S(1)}, u32[]{:S(2)}, u32[]{:S(2)}) collective-permute-start(f32[1,7,128]{2,1,0:T(8,128)S(1)} %get-tuple-element.49), channel_id=1, source_target_pairs={{0,1},{1,0},{2,3},{3,2},{4,5},{5,4},{6,7},{7,6},{8,9},{9,8},{10,11... | collective-permute-start | bytes 10760 | tf_op jit(solution)/shard_map/ppermute | solution.py:549

commit v3 on v2

--- a/solution.py
+++ b/solution.py
@@ -13,7 +13,6 @@
 ORDINAL = [KIND[:k].count(KIND[k]) for k in range(26)]
 PER_KIND = (6, 12, 8)
 FIRST = (0, 2, 5)
-PITCH = 24
 F32, BF16 = jnp.float32, jnp.bfloat16
 
 
@@ -23,10 +22,6 @@
 
 def target_coord(step):
     return 9 if step == 1 else 0
-
-
-def z_row(step):
-    return 16 if step == 1 else 7
 
 
 def half_of(shape):
@@ -42,32 +37,39 @@
     return jnp.where(low, top, v - top).astype(BF16)
 
 
-def tables_kernel(x_ref, m_ref, face_ref, edge_ref, corner_ref, rows):
-    x = (x_ref[...] * m_ref[...]).reshape(512, 64)
-    rows[...] = jnp.concatenate([x, x], axis=1)
-    for k, (a, b, c) in enumerate(OFFSETS):
-        n = ORDINAL[k]
-        x0, y0, z0 = source_coord(a), source_coord(b), source_coord(c)
-        if KIND[k] == 0:
-            for i in range(8):
-                if a:
-                    v = rows[x0 * 64 + i * 8:x0 * 64 + i * 8 + 8, :]
-                elif b:
-                    v = rows[i * 64 + y0 * 8:i * 64 + y0 * 8 + 8, :]
+def masked_rows(x_ref, m_ref, p):
+    return (x_ref[p] * m_ref[p].astype(F32)).T
+
+
+def tables_kernel(x_ref, m_ref, face_ref, edge_ref, corner_ref, row_ref, rows):
+    for p in range(x_ref.shape[0]):
+        x = masked_rows(x_ref, m_ref, p)
+        x = jnp.concatenate([x, x], axis=1)
+        rows[...] = x
+        row_ref[p] = x
+        for k, (a, b, c) in enumerate(OFFSETS):
+            n = ORDINAL[k]
+            x0, y0, z0 = source_coord(a), source_coord(b), source_coord(c)
+            if KIND[k] == 0:
+                for i in range(8):
+                    if a:
+                        v = rows[x0 * 64 + i * 8:x0 * 64 + i * 8 + 8, :]
+                    elif b:
+                        v = rows[i * 64 + y0 * 8:i * 64 + y0 * 8 + 8, :]
+                    else:
+                        v = rows[pl.ds(i * 64 + z0, 8, stride=8), :]
+                    face_ref[p * 6 + n, i * 8:i * 8 + 8, :] = v
+            elif KIND[k] == 1:
+                if not c:
+                    v = rows[x0 * 64 + y0 * 8:x0 * 64 + y0 * 8 + 8, :]
+                elif not b:
+                    v = rows[pl.ds(x0 * 64 + z0, 8, stride=8), :]
                 else:
-                    v = rows[pl.ds(i * 64 + z0, 8, stride=8), :]
-                face_ref[n, i * 8:i * 8 + 8, :] = v
-        elif KIND[k] == 1:
-            if not c:
-                v = rows[x0 * 64 + y0 * 8:x0 * 64 + y0 * 8 + 8, :]
-            elif not b:
-                v = rows[pl.ds(x0 * 64 + z0, 8, stride=8), :]
+                    v = rows[pl.ds(y0 * 8 + z0, 8, stride=64), :]
+                edge_ref[p * 12 + n] = v
             else:
-                v = rows[pl.ds(y0 * 8 + z0, 8, stride=64), :]
-            edge_ref[n] = v
-        else:
-            r = x0 * 64 + y0 * 8 + z0
-            corner_ref[n] = jnp.broadcast_to(rows[r:r + 1, :], (8, 128))
+                r = x0 * 64 + y0 * 8 + z0
+                corner_ref[p * 8 + n] = jnp.broadcast_to(rows[r:r + 1, :], (8, 128))
 
 
 def pack_kernel(want_ref, face_ref, edge_ref, corner_ref, out_ref):
@@ -121,35 +123,37 @@
     slices = [(i, j, l) for i in range(4) for j in range(3) for l in range(3)]
     acc = None
     for s in range(0, 36, 4):
-        parts = [a_ref[l, i % 2, i // 2:i // 2 + 4, j:j + 8].reshape(512, 128) for i, j, l in slices[s:s + 4]]
+        parts = [a_ref[l, 0, i % 2, i // 2:i // 2 + 4, j:j + 8].reshape(512, 128) for i, j, l in slices[s:s + 4]]
         lhs = jnp.concatenate(parts, axis=1)
         d = jnp.dot(lhs, w_ref[s * 128:s * 128 + 512, :], preferred_element_type=F32)
         acc = d if acc is None else acc + d
     return (acc[:, :128] + acc[:, 128:]).reshape(4, 8, 16, 128)
 
 
-def own_forward_kernel(x_ref, m_ref, cot_ref, w_ref, bias_ref, pre_ref, mask_ref, cotm_ref, a_ref):
-    @pl.when(pl.program_id(0) == 0)
-    def _():
-        a_ref[...] = jnp.zeros_like(a_ref)
-
+def clear_border(a_ref):
+    spare = jnp.zeros((16, 128), BF16)
+    for l in range(3):
+        for x in range(10):
+            for y in range(10):
+                if x in (0, 9) or y in (0, 9):
+                    a_ref[l, 0, x % 2, x // 2, y] = spare
+
+
+def own_forward_kernel(x_ref, m_ref, cot_ref, w_ref, bias_ref, pre_ref, cotm_ref, a_ref):
+    clear_border(a_ref)
     row = lax.broadcasted_iota(jnp.int32, (8, 128), 0)
     low = jnp.logical_not(half_of((16, 128)))
     for x in range(8):
-        cols = []
-        for b in range(2):
-            v = x_ref[b, x // 2, x % 2] * m_ref[b, x // 2, x % 2]
-            cols.append(jnp.concatenate([v, v], axis=-1))
         for y in range(8):
+            r = x * 64 + y * 8
             for l in range(3):
-                v = jnp.concatenate([shifted(cols[b][y], l, row) for b in range(2)], axis=0)
-                a_ref[l, (x + 1) % 2, (x + 1) // 2, y + 1] = split_halves(v, low)
+                v = jnp.concatenate([shifted(x_ref[b, r:r + 8, :], l, row) for b in range(2)], axis=0)
+                a_ref[l, 0, (x + 1) % 2, (x + 1) // 2, y + 1] = split_halves(v, low)
     pre = convolve(a_ref, w_ref) + bias_ref[...]
     for b in range(2):
         pre_ref[b] = pre[:, :, b * 8:b * 8 + 8]
-        mask = jnp.concatenate([m_ref[b, :, 0], m_ref[b, :, 1]], axis=-1)
-        mask_ref[b] = mask
-        cotm_ref[b] = jnp.concatenate([cot_ref[b, :, 0], cot_ref[b, :, 1]], axis=-1) * mask
+        c = masked_rows(cot_ref, m_ref, b).reshape(4, 2, 8, 8, 64)
+        cotm_ref[b] = jnp.concatenate([c[:, 0], c[:, 1]], axis=-1)
 
 
 def own_backward_kernel(d_ref, w_ref, own_ref, a_ref):
@@ -164,17 +168,26 @@
         for y in range(8):
             cols = []
             for b in range(2):
-                v = d_ref[b, x // 2, y]
-                cols.append(placed(v, half if x % 2 else jnp.logical_not(half)))
+                cols.append(placed(d_ref[b, x // 2, y], half if x % 2 else jnp.logical_not(half)))
             for l in range(3):
                 v = jnp.concatenate([shifted(cols[b], l, row) for b in range(2)], axis=0)
-                a_ref[l, (x + 1) % 2, (x + 1) // 2, y + 1] = split_halves(v, low)
+                a_ref[l, 0, (x + 1) % 2, (x + 1) // 2, y + 1] = split_halves(v, low)
     out = convolve(a_ref, w_ref)
     for b in range(2):
         own_ref[b, :, 0] = out[:, :, b * 8:b * 8 + 8, :64]
         own_ref[b, :, 1] = out[:, :, b * 8:b * 8 + 8, 64:]
 
 
+def activated_kernel(act_ref, m_ref, out_ref):
+    for b in range(2):
+        mask = m_ref[b].astype(F32)
+        for h in range(2):
+            t = act_ref[b, 2 * h:2 * h + 2].reshape(128, 128).T
+            v = jnp.concatenate([t[:64, :64], t[64:, :64], t[:64, 64:], t[64:, 64:]], axis=1)
+            a = slice(h * 256, h * 256 + 256)
+            out_ref[b, :, a] = v * mask[:, a]
+
+
 def unpack_code(code_ref, b, k):
     c = code_ref[b * 26 + k]
     return c >> 4, (c >> 1) & 7, c & 1
@@ -185,8 +198,8 @@
     return pl.ds(pl.multiple_of(64 + 8 * (e >> 1), 8), 8), e & 1
 
 
-def halo_kernel(code_ref, recv_ref, own_ref, mask_ref, cot_ref, wf_ref, wb_ref,
-                act_ref, dpre_ref, send_ref, pre, px, py, zf, pz, qx, qy, qz, rx, ry, rz, tmp):
+def halo_kernel(code_ref, recv_ref, own_ref, cot_ref, wf_ref, wb_ref,
+                act_ref, dpre_ref, send_ref, px, py, pz, pre, zf, qx, qy, qz, rx, ry, rz, tmp):
     high8 = half_of((8, 128))
     half8 = high8.astype(jnp.int32)
     row = lax.broadcasted_iota(jnp.int32, (8, 128), 0)
@@ -310,7 +323,7 @@
         p = pre[a, :]
         sig = jax.nn.sigmoid(p)
         ps = p * sig
-        act_ref[a, :] = ps * mask_ref[a, :]
+        act_ref[a, :] = ps
         dpre_ref[a, :] = cot_ref[a, :] * (sig + ps * (1.0 - sig))
         return carry
 
@@ -397,76 +410,70 @@
                 send_ref[o, 72:80, :] = jnp.where(spot, v, send_ref[o, 72:80, :])
 
 
-def windows_kernel(code_ref, recv_ref, x_ref, m_ref, d_ref, a_ref, dt_ref, pf):
-    g = pl.program_id(0)
-    high8 = half_of((8, 128))
-    half8 = high8.astype(jnp.int32)
-
-    def prow(b, x, y, z):
-        return ((b * 10 + x) * 10 + y) * PITCH + z
-
-    for b in range(2):
-        for x in range(8):
-            v = x_ref[b, x // 2, x % 2] * m_ref[b, x // 2, x % 2]
-            v = jnp.concatenate([v, v], axis=-1)
+def turned_terms(out_ref, at, v):
+    t = v.T
+    n = t.shape[1]
+    top = t.astype(BF16)
+    out_ref[0:128, at:at + n] = top
+    out_ref[128:256, at:at + n] = (t - top.astype(F32)).astype(BF16)
+
+
+def kernel_grad_kernel(a_ref, px_ref, py_ref, pz_ref, d_ref, out_ref, dt, dx, dy, dz):
+    l = pl.program_id(0)
+
+    @pl.when(l == 0)
+    def _():
+        for g in range(6):
+            v = jnp.concatenate([d_ref[2 * g], d_ref[2 * g + 1]], axis=2)
+            turned_terms(dt, g * 512, v.reshape(512, 128))
+        flat = d_ref.reshape(3072, 128)
+        for s in range(2):
             for y in range(8):
-                r = prow(b, x + 1, y + 1, 8)
-                pf[r:r + 8, :] = v[y]
-    for b in range(2):
-        for k, (dx, dy, dz) in enumerate(OFFSETS):
-            o, pos, alive = unpack_code(code_ref, 2 * g + b, k)
-            scale = alive.astype(F32)
-            xt, yt, zt = target_coord(dx), target_coord(dy), z_row(dz)
-            if KIND[k] == 0:
-                for i in range(8):
-                    v = placed(recv_ref[o, i * 8:i * 8 + 8, :], half8 == pos) * scale
-                    if dx:
-                        r = prow(b, xt, i + 1, 8)
-                        pf[r:r + 8, :] = v
-                    elif dy:
-                        r = prow(b, i + 1, yt, 8)
-                        pf[r:r + 8, :] = v
-                    else:
-                        pf[pl.ds(prow(b, i + 1, 1, zt), 8, stride=PITCH), :] = v
-            elif KIND[k] == 1:
-                rows, h = edge_rows(pos)
-                v = placed(recv_ref[o, rows, :], half8 == h) * scale
-                if not dz:
-                    r = prow(b, xt, yt, 8)
-                    pf[r:r + 8, :] = v
-                elif dx:
-                    pf[pl.ds(prow(b, xt, 1, zt), 8, stride=PITCH), :] = v
-                else:
-                    pf[pl.ds(prow(b, 1, yt, zt), 8, stride=10 * PITCH), :] = v
-            else:
-                v = recv_ref[o, 72:80, :]
-                v = jnp.where(pos == 5, v[0:1, :], v[1:2, :])
-                r = prow(b, xt, yt, zt)
-                pf[r:r + 1, :] = placed(v, high8[0:1]) * scale
-    low = jnp.logical_not(half_of((16, 128)))
-    for l in range(3):
-        for x in range(10):
-            for y in range(10):
-                r0, r1 = prow(0, x, y, 7 + l), prow(1, x, y, 7 + l)
-                v = jnp.concatenate([pf[r0:r0 + 8, :], pf[r1:r1 + 8, :]], axis=0)
-                a_ref[l, 0, x % 2, x // 2, y] = split_halves(v, low)
-    t = jnp.concatenate([d_ref[0], d_ref[1]], axis=2).reshape(512, 128).T
-    top = t.astype(BF16)
-    dt_ref[0:128, :] = top
-    dt_ref[128:256, :] = (t - top.astype(F32)).astype(BF16)
-
-
-def kernel_grad_kernel(a_ref, dt_ref, out_ref):
-    d = dt_ref[...]
+                v = jnp.concatenate([d_ref[b, 3 * s, y] for b in range(12)], axis=0)
+                if y % 4 == 0:
+                    held = []
+                held.append(v)
+                if y % 4 == 3:
+                    turned_terms(dx.at[s], (y - 3) * 96, jnp.concatenate(held, axis=0))
+            v = [d_ref[b, xh, 7 * s] for xh in range(4) for b in range(12)]
+            turned_terms(dy.at[s], 0, jnp.concatenate(v, axis=0))
+            v = []
+            for n in range(32):
+                r = n * 8 + 7 * s
+                v.append(flat[pl.ds(r, 8, stride=256), :])
+                v.append(flat[pl.ds(r + 2048, 4, stride=256), :])
+                v.append(jnp.zeros((4, 128), F32))
+            turned_terms(dz.at[s], 0, jnp.concatenate(v, axis=0))
+
+    def product(d, parts):
+        s = jnp.dot(d, jnp.concatenate(parts, axis=1), preferred_element_type=F32)
+        s = s[:128] + s[128:]
+        out = []
+        for q in range(len(parts)):
+            v = s[:, q * 128:q * 128 + 128]
+            out.append((v + swap(v))[:, :64])
+        return out
+
     for j in range(3):
         for h in range(2):
             parts = [a_ref[0, :, q, h:h + 4, j:j + 8].reshape(3072, 128) for q in range(2)]
-            s = jnp.dot(d, jnp.concatenate(parts, axis=1), preferred_element_type=F32)
-            s = s[:128] + s[128:]
-            for q in range(2):
-                v = s[:, q * 128:q * 128 + 128]
-                v = v + swap(v)
-                out_ref[0, j, 2 * h + q] = v[:, :64]
+            for q, v in enumerate(product(dt[...], parts)):
+                out_ref[0, j, 2 * h + q] = v
+    for s in range(2):
+        parts = [px_ref[s, 0, j:j + 8].reshape(768, 128) for j in range(3)]
+        for j, v in enumerate(product(dx[s], parts)):
+            out_ref[0, j, 3 * s] += v
+        parts = [py_ref[s, 0, i % 2, i // 2:i // 2 + 4].reshape(384, 128) for i in range(4)]
+        for i, v in enumerate(product(dy[s], parts)):
+            out_ref[0, 2 * s, i] += v
+
+    @pl.when(l != 1)
+    def _():
+        s = l // 2
+        for j in range(3):
+            parts = [pz_ref[s, i % 2, i // 2:i // 2 + 4, j:j + 8].reshape(512, 128) for i in range(4)]
+            for i, v in enumerate(product(dz[s], parts)):
+                out_ref[0, j, i] += v
 
 
 def collect_kernel(want_ref, back_ref, own_ref, m_ref, out_ref, faces, edges, corners, rows):
@@ -504,51 +511,52 @@
     def fold(v):
         return (v + swap(v))[:, :64]
 
-    rows[...] = own_ref[...].reshape(512, 64)
-    for k, (a, b, c) in enumerate(OFFSETS):
-        n = g * PER_KIND[KIND[k]] + ORDINAL[k]
-        x0, y0, z0 = source_coord(a), source_coord(b), source_coord(c)
-        if KIND[k] == 0:
-            for i in range(8):
-                v = fold(faces[n, i * 8:i * 8 + 8, :])
-                if a:
-                    s = slice(x0 * 64 + i * 8, x0 * 64 + i * 8 + 8)
-                elif b:
-                    s = slice(i * 64 + y0 * 8, i * 64 + y0 * 8 + 8)
+    bricks = own_ref.shape[0]
+    for p in range(bricks):
+        rows[...] = own_ref[p].reshape(512, 64)
+        for k, (a, b, c) in enumerate(OFFSETS):
+            n = (g * bricks + p) * PER_KIND[KIND[k]] + ORDINAL[k]
+            x0, y0, z0 = source_coord(a), source_coord(b), source_coord(c)
+            if KIND[k] == 0:
+                for i in range(8):
+                    v = fold(faces[n, i * 8:i * 8 + 8, :])
+                    if a:
+                        s = slice(x0 * 64 + i * 8, x0 * 64 + i * 8 + 8)
+                    elif b:
+                        s = slice(i * 64 + y0 * 8, i * 64 + y0 * 8 + 8)
+                    else:
+                        s = pl.ds(i * 64 + z0, 8, stride=8)
+                    rows[s, :] = rows[s, :] + v
+            elif KIND[k] == 1:
+                v = fold(edges[n])
+                if not c:
+                    s = slice(x0 * 64 + y0 * 8, x0 * 64 + y0 * 8 + 8)
+                elif not b:
+                    s = pl.ds(x0 * 64 + z0, 8, stride=8)
                 else:
-                    s = pl.ds(i * 64 + z0, 8, stride=8)
+                    s = pl.ds(y0 * 8 + z0, 8, stride=64)
                 rows[s, :] = rows[s, :] + v
-        elif KIND[k] == 1:
-            v = fold(edges[n])
-            if not c:
-                s = slice(x0 * 64 + y0 * 8, x0 * 64 + y0 * 8 + 8)
-            elif not b:
-                s = pl.ds(x0 * 64 + z0, 8, stride=8)
             else:
-                s = pl.ds(y0 * 8 + z0, 8, stride=64)
-            rows[s, :] = rows[s, :] + v
-        else:
-            r = x0 * 64 + y0 * 8 + z0
-            v = fold(corners[n])
-            rows[r:r + 1, :] = rows[r:r + 1, :] + (v[0:1] + v[1:2])
-    out_ref[...] = rows[...].reshape(out_ref.shape) * m_ref[...]
-
-
-def share_out(v):
-    scene, brick = lax.axis_index("scene"), lax.axis_index("brick")
+                r = x0 * 64 + y0 * 8 + z0
+                v = fold(corners[n])
+                rows[r:r + 1, :] = rows[r:r + 1, :] + (v[0:1] + v[1:2])
+        out_ref[p] = rows[...].T * m_ref[p].astype(F32)
+
+
+def swap_scenes(v):
+    scene = lax.axis_index("scene")
     v = v.reshape(2, 64, 7, 128)
     mine = lax.dynamic_index_in_dim(v, scene, 0, keepdims=False)
     theirs = lax.dynamic_index_in_dim(v, 1 - scene, 0, keepdims=False)
-    v = mine + lax.ppermute(theirs, "scene", [(0, 1), (1, 0)])
-    for stride in (16, 4, 1):
-        v = v.reshape(4, stride, 7, 128)
-        at = (brick // stride) % 4
-        total = lax.dynamic_index_in_dim(v, at, 0, keepdims=False)
-        for d in (1, 2, 3):
-            part = lax.dynamic_index_in_dim(v, at ^ d, 0, keepdims=False)
-            total = total + lax.ppermute(part, "brick", [(n, n ^ (d * stride)) for n in range(64)])
-        v = total
-    return v.reshape(896)[:864]
+    return mine + lax.ppermute(theirs, "scene", [(0, 1), (1, 0)])
+
+
+def sum_stage(v, stride):
+    at = (lax.axis_index("brick") // stride) % 4
+    v = v.reshape(4, stride, 7, 128)
+    sent = [lax.ppermute(lax.dynamic_index_in_dim(v, at ^ d, 0, keepdims=False), "brick",
+                         [(n, n ^ (d * stride)) for n in range(64)]) for d in (1, 2, 3)]
+    return lax.dynamic_index_in_dim(v, at, 0, keepdims=False), sent
 
 
 def whole(memory=pltpu.VMEM):
@@ -563,14 +571,14 @@
     return pl.BlockSpec(shape, lambda g: (g,) + (0,) * (len(shape) - 1))
 
 
-def params():
-    return pltpu.CompilerParams(vmem_limit_bytes=56 * 1024 * 1024)
+def params(mib):
+    return pltpu.CompilerParams(vmem_limit_bytes=mib * 1024 * 1024)
 
 
 def on_device(features, voxel_mask, weight, bias, cotangent, owner, slot, live):
-    x = features.reshape(12, 4, 2, 8, 8, 64)
-    cot = cotangent.reshape(12, 4, 2, 8, 8, 64)
-    mask = jnp.broadcast_to(voxel_mask[0].astype(F32)[:, :, None], (12, 512, 64)).reshape(12, 4, 2, 8, 8, 64)
+    x = features[0].transpose(0, 2, 1)
+    cot = cotangent[0].transpose(0, 2, 1)
+    mask = voxel_mask.reshape(12, 1, 512)
 
     peer = owner.reshape(312)
     alive = live.reshape(312)
@@ -594,23 +602,29 @@
         in_specs=[whole()],
         out_specs=[whole(), whole()],
         out_shape=[jax.ShapeDtypeStruct((4608, 256), BF16)] * 2,
-        compiler_params=params(),
+        compiler_params=params(16),
         cost_estimate=pl.CostEstimate(flops=0, bytes_accessed=6000000, transcendentals=0),
         name="weights",
     )(weight)
 
-    faces, edges, corners = pl.pallas_call(
+    faces, edges, corners, rows = pl.pallas_call(
         tables_kernel,
-        grid=(12,),
-        in_specs=[lead_block((1, 4, 2, 8, 8, 64))] * 2,
-        out_specs=[lead_block((6, 64, 128)), lead_block((12, 8, 128)), lead_block((8, 8, 128))],
+        grid=(3,),
+        in_specs=[lead_block((4, 64, 512)), lead_block((4, 1, 512))],
+        out_specs=[
+            lead_block((24, 64, 128)),
+            lead_block((48, 8, 128)),
+            lead_block((32, 8, 128)),
+            lead_block((4, 512, 128)),
+        ],
         out_shape=[
             jax.ShapeDtypeStruct((72, 64, 128), F32),
             jax.ShapeDtypeStruct((144, 8, 128), F32),
             jax.ShapeDtypeStruct((96, 8, 128), F32),
+            jax.ShapeDtypeStruct((12, 512, 128), F32),
         ],
         scratch_shapes=[pltpu.VMEM((512, 128), F32)],
-        compiler_params=params(),
+        compiler_params=params(16),
         name="tables",
     )(x, mask)
 
@@ -619,45 +633,51 @@
         in_specs=[whole(pltpu.SMEM), whole(), whole(), whole()],
         out_specs=whole(),
         out_shape=jax.ShapeDtypeStruct((64, 80, 128), F32),
-        compiler_params=params(),
+        compiler_params=params(16),
         name="pack",
     )(asked, faces, edges, corners)
     recv = lax.all_to_all(out, "brick", split_axis=0, concat_axis=0, tiled=True)
 
     bias2 = jnp.concatenate([bias, bias]).reshape(1, 128)
+    turned_block = lead_block((2, 64, 512))
+    turned_shape = jax.ShapeDtypeStruct((12, 64, 512), F32)
+    mask_block = lead_block((2, 1, 512))
     brick_block = lead_block((2, 4, 2, 8, 8, 64))
     brick_shape = jax.ShapeDtypeStruct((12, 4, 2, 8, 8, 64), F32)
     packed_block = lead_block((2, 4, 8, 8, 128))
     packed_shape = jax.ShapeDtypeStruct((12, 4, 8, 8, 128), F32)
-    window_scratch = pltpu.VMEM((3, 2, 5, 10, 16, 128), BF16)
-    own_pre, mask_p, cot_p = pl.pallas_call(
+    own_pre, cot_p, windows = pl.pallas_call(
         own_forward_kernel,
         grid=(6,),
-        in_specs=[brick_block] * 3 + [const_block((4608, 256)), const_block((1, 128))],
-        out_specs=[packed_block] * 3,
-        out_shape=[packed_shape] * 3,
-        scratch_shapes=[window_scratch],
-        compiler_params=params(),
+        in_specs=[lead_block((2, 512, 128)), mask_block, turned_block, const_block((4608, 256)), const_block((1, 128))],
+        out_specs=[
+            packed_block,
+            packed_block,
+            pl.BlockSpec((3, 1, 2, 5, 10, 16, 128), lambda g: (0, g, 0, 0, 0, 0, 0)),
+        ],
+        out_shape=[packed_shape, packed_shape, jax.ShapeDtypeStruct((3, 6, 2, 5, 10, 16, 128), BF16)],
+        compiler_params=params(24),
         cost_estimate=pl.CostEstimate(flops=2 * 3072 * 4608 * 256, bytes_accessed=15000000, transcendentals=0),
         name="own_forward",
-    )(x, mask, cot, wf, bias2)
+    )(rows, mask, cot, wf, bias2)
 
     flat = (3072, 128)
-    act, dpre, send = pl.pallas_call(
+    side_x, side_y, side_z = (2, 3, 10, 6, 16, 128), (2, 3, 2, 5, 6, 16, 128), (2, 2, 5, 10, 16, 128)
+    act, dpre, send, px, py, pz = pl.pallas_call(
         halo_kernel,
-        in_specs=[whole(pltpu.SMEM)] + [whole()] * 6,
-        out_specs=[whole()] * 3,
+        in_specs=[whole(pltpu.SMEM)] + [whole()] * 5,
+        out_specs=[whole()] * 6,
         out_shape=[
             jax.ShapeDtypeStruct(flat, F32),
             jax.ShapeDtypeStruct(flat, F32),
             jax.ShapeDtypeStruct((64, 80, 128), F32),
+            jax.ShapeDtypeStruct(side_x, BF16),
+            jax.ShapeDtypeStruct(side_y, BF16),
+            jax.ShapeDtypeStruct(side_z, BF16),
         ],
         scratch_shapes=[
             pltpu.VMEM(flat, F32),
-            pltpu.VMEM((2, 3, 10, 6, 16, 128), BF16),
-            pltpu.VMEM((2, 3, 2, 5, 6, 16, 128), BF16),
             pltpu.VMEM((3200, 128), F32),
-            pltpu.VMEM((2, 2, 5, 10, 16, 128), BF16),
             pltpu.VMEM((2, 3, 12, 6, 16, 128), BF16),
             pltpu.VMEM((2, 3, 2, 5, 6, 16, 128), BF16),
             pltpu.VMEM((2, 2, 6, 12, 16, 128), BF16),
@@ -666,54 +686,43 @@
             pltpu.VMEM((1600, 128), F32),
             pltpu.VMEM((8, 128), F32),
         ],
-        compiler_params=params(),
+        compiler_params=params(40),
         name="halo",
-    )(code, recv, own_pre.reshape(flat), mask_p.reshape(flat), cot_p.reshape(flat), wf, wb)
+    )(code, recv, own_pre.reshape(flat), cot_p.reshape(flat), wf, wb)
     back = lax.all_to_all(send, "brick", split_axis=0, concat_axis=0, tiled=True)
-    act = act.reshape(12, 4, 8, 8, 2, 64).transpose(0, 1, 4, 2, 3, 5)
-    dpre = dpre.reshape(12, 4, 8, 8, 128)
-
-    windows, dpre_t = pl.pallas_call(
-        windows_kernel,
-        grid=(6,),
-        in_specs=[
-            pl.BlockSpec(memory_space=pltpu.SMEM),
-            const_block((64, 80, 128)),
-            brick_block,
-            brick_block,
-            packed_block,
-        ],
-        out_specs=[
-            pl.BlockSpec((3, 1, 2, 5, 10, 16, 128), lambda g: (0, g, 0, 0, 0, 0, 0)),
-            pl.BlockSpec((256, 512), lambda g: (0, g)),
-        ],
-        out_shape=[
-            jax.ShapeDtypeStruct((3, 6, 2, 5, 10, 16, 128), BF16),
-            jax.ShapeDtypeStruct((256, 3072), BF16),
-        ],
-        scratch_shapes=[pltpu.VMEM((200 * PITCH, 128), F32)],
-        compiler_params=params(),
-        cost_estimate=pl.CostEstimate(flops=0, bytes_accessed=30000000, transcendentals=0),
-        name="windows",
-    )(code, recv, x, mask, dpre)
+    act = act.reshape(packed_shape.shape)
+    dpre = dpre.reshape(packed_shape.shape)
+
     z = pl.pallas_call(
         kernel_grad_kernel,
         grid=(3,),
         in_specs=[
             pl.BlockSpec((1, 6, 2, 5, 10, 16, 128), lambda l: (l, 0, 0, 0, 0, 0, 0)),
-            const_block((256, 3072)),
+            pl.BlockSpec((2, 1, 10, 6, 16, 128), lambda l: (0, l, 0, 0, 0, 0)),
+            pl.BlockSpec((2, 1, 2, 5, 6, 16, 128), lambda l: (0, l, 0, 0, 0, 0, 0)),
+            const_block(side_z),
+            const_block(packed_shape.shape),
         ],
         out_specs=lead_block((1, 3, 4, 128, 64)),
         out_shape=jax.ShapeDtypeStruct((3, 3, 4, 128, 64), F32),
-        compiler_params=params(),
-        cost_estimate=pl.CostEstimate(flops=2 * 256 * 3072 * 4608, bytes_accessed=11000000, transcendentals=0),
+        scratch_shapes=[
+            pltpu.VMEM((256, 3072), BF16),
+            pltpu.VMEM((2, 256, 768), BF16),
+            pltpu.VMEM((2, 256, 384), BF16),
+            pltpu.VMEM((2, 256, 512), BF16),
+        ],
+        compiler_params=params(40),
+        cost_estimate=pl.CostEstimate(flops=0, bytes_accessed=1000, transcendentals=0),
         name="kernel_grad",
-    )(windows, dpre_t)
+    )(windows, px, py, pz, dpre)
     kernel = z[:, :, 0:3, 0:64] + z[:, :, 1:4, 64:128]
     kernel = kernel.transpose(2, 1, 0, 4, 3).reshape(128, 864)
     kernel = jnp.pad(kernel, ((0, 0), (0, 32))).reshape(128, 7, 128)
     scale = 1.0 / math.sqrt(float(2 * 768 * 512))
-    share = share_out(kernel) * scale
+    act, kernel = lax.optimization_barrier((act, kernel))
+    total = swap_scenes(kernel)
+    dpre, total = lax.optimization_barrier((dpre, total))
+    kept, sent = sum_stage(total, 16)
 
     own = pl.pallas_call(
         own_backward_kernel,
@@ -721,34 +730,52 @@
         in_specs=[packed_block, const_block((4608, 256))],
         out_specs=brick_block,
         out_shape=brick_shape,
-        scratch_shapes=[window_scratch],
-        compiler_params=params(),
-        cost_estimate=pl.CostEstimate(flops=2 * 3072 * 4608 * 256, bytes_accessed=15000000, transcendentals=0),
+        scratch_shapes=[pltpu.VMEM((3, 1, 2, 5, 10, 16, 128), BF16)],
+        compiler_params=params(24),
+        cost_estimate=pl.CostEstimate(flops=0, bytes_accessed=1000, transcendentals=0),
         name="own_backward",
     )(dpre, wb)
+    activated = pl.pallas_call(
+        activated_kernel,
+        grid=(6,),
+        in_specs=[packed_block, mask_block],
+        out_specs=turned_block,
+        out_shape=turned_shape,
+        compiler_params=params(8),
+        cost_estimate=pl.CostEstimate(flops=0, bytes_accessed=1000, transcendentals=0),
+        name="activated",
+    )(act, mask)
+
+    total = kept + sent[0] + sent[1] + sent[2]
+    own, total, activated = lax.optimization_barrier((own, total, activated))
+    kept, sent = sum_stage(total, 4)
+    total = kept + sent[0] + sent[1] + sent[2]
+    back, total = lax.optimization_barrier((back, total))
+    kept, sent = sum_stage(total, 1)
 
     grad = pl.pallas_call(
         collect_kernel,
-        grid=(12,),
+        grid=(4,),
         in_specs=[
             pl.BlockSpec(memory_space=pltpu.SMEM),
             const_block((64, 80, 128)),
-            lead_block((1, 4, 2, 8, 8, 64)),
-            lead_block((1, 4, 2, 8, 8, 64)),
-        ],
-        out_specs=lead_block((1, 4, 2, 8, 8, 64)),
-        out_shape=brick_shape,
+            lead_block((3, 4, 2, 8, 8, 64)),
+            lead_block((3, 1, 512)),
+        ],
+        out_specs=lead_block((3, 64, 512)),
+        out_shape=turned_shape,
         scratch_shapes=[
             pltpu.VMEM((73, 64, 128), F32),
             pltpu.VMEM((145, 8, 128), F32),
             pltpu.VMEM((97, 8, 128), F32),
             pltpu.VMEM((512, 64), F32),
         ],
-        compiler_params=params(),
+        compiler_params=params(24),
         name="collect",
     )(asked, back, own, mask)
-    shape = features.shape
-    return act.reshape(shape), grad.reshape(shape), share
+    grad, kept = lax.optimization_barrier((grad, kept))
+    share = (kept + sent[0] + sent[1] + sent[2]).reshape(896)[:864] * scale
+    return activated.transpose(0, 2, 1)[None], grad.transpose(0, 2, 1)[None], share
 
 
 def solution(mesh):

time: 195 us -> 170 us (0.87)
  Pallas kernels: 94.8 us -> 65 us
  local copies, waits for them, and re-layouts: 24.7 us -> 33.3 us
    pallas_call x5, Pallas kernels: 62.9 us -> 36.7 us  [the longest x1 15.4 us: on_device(): pl.pallas_call(halo_kernel, in_specs=[whole(pltpu.SMEM)] + [whole()] * 5,...]
    unnamed x10 -> x53, local copies, waits for them, and re-layouts: 15.1 us -> 29.2 us
    reshape x2 -> x0, local copies, waits for them, and re-layouts: 5.34 us -> none  [on_device(): act = act.reshape(12, 4, 8, 8, 2, 64).transpose(0, 1, 4, 2, 3, 5)]
    ppermute x10, waiting for transfers between devices: 10.5 us -> 5.86 us  [the longest x9 4.43 us: sum_stage(): lax.ppermute(lax.dynamic_index_in_dim(v, at ^ d, 0, keepdims=False), 'bri...]
    all_to_all x1, waiting for transfers between devices: 0.01 us -> 3.54 us  [on_device(): lax.all_to_all(wanted, 'brick', split_axis=0, concat_axis=0, tiled=True)]
    pallas_call x1, Pallas kernels: 4.08 us -> 0.77 us  [on_device(): pl.pallas_call(weights_kernel, in_specs=[whole()], out_specs=[whole(), wh...]
    all_to_all x1, starting transfers between devices: 10.5 us -> 7.36 us  [on_device(): recv = lax.all_to_all(out, 'brick', split_axis=0, concat_axis=0, tiled=True)]
    pallas_call x1, Pallas kernels: 11.2 us -> 14.3 us  [on_device(): pl.pallas_call(kernel_grad_kernel, grid=(3,), in_specs=[pl.BlockSpec((1,...]
  transfers between devices with their start and end apart: 13 -> 13, of which waited for: 6 -> 5; matrix products, arithmetic and copies ran while one was open for 11% -> 4% of each run, Pallas kernels for 31% -> 27%
where the time goes in v3:
time: 170 us; the launch traced here: 169 us
  Pallas kernels  65 us (38%)
  starting transfers between devices  40.1 us (24%)
  local copies, waits for them, and re-layouts  33.3 us (20%)
  waiting for transfers between devices  23.6 us (14%)
  other arithmetic  5.85 us (3%)
    unnamed x53, local copies, waits for them, and re-layouts  29.2 us
    pallas_call x1, Pallas kernels, on_device(): pl.pallas_call(halo_kernel, in_specs=[whole(pltpu.SMEM)] + [whole()] * 5,...  15.4 us
    ppermute x9, starting transfers between devices, sum_stage(): lax.ppermute(lax.dynamic_index_in_dim(v, at ^ d, 0, keepdims=False), 'bri...  14.3 us
    pallas_call x1, Pallas kernels, on_device(): pl.pallas_call(kernel_grad_kernel, grid=(3,), in_specs=[pl.BlockSpec((1,...  14.3 us
    all_to_all x1, waiting for transfers between devices, on_device(): recv = lax.all_to_all(out, 'brick', split_axis=0, concat_axis=0, tiled=True)  14.3 us
    all_to_all x1, starting transfers between devices, on_device(): lax.all_to_all(wanted, 'brick', split_axis=0, concat_axis=0, tiled=True)  11.5 us
    pallas_call x1, Pallas kernels, on_device(): pl.pallas_call(own_backward_kernel, grid=(6,), in_specs=[packed_block, co...  9.48 us
    pallas_call x1, Pallas kernels, on_device(): pl.pallas_call(own_forward_kernel, grid=(6,), in_specs=[lead_block((2, 51...  9.19 us
  transfers between devices with their start and end apart: 13, of which 5 were waited for; matrix products, arithmetic and copies ran while one was open for 4% of the time, Pallas kernels for 27%

profile of v3, /device:TPU:0, one launch (start us, length us, event | category | flops | bytes accessed | tf_op | source)
XLA Modules:
  0.0 168.9 jit_solution(13021127251272826739)
XLA Ops:
  0.6 0.8 add_reduce_fusion.1
  1.4 0.1 reshape.97
  1.5 0.1 convert_reduce_fusion
  1.7 0.7 reduce.2
  2.4 0.1 reshape.82
  2.5 0.8 add_reduce_fusion
  3.3 0.7 compare_select_fusion
  4.0 0.2 select_reduce_fusion
  4.2 0.7 sub.18
  4.9 11.5 %all-to-all-start = ((s32[64,1,8]{2,1,0:T(1,128)}), s32[64,1,8]{2,1,0:T(1,128)S(1)}, u32[]{:S(2)}, u32[]{:S(2)}) async-start(s32[64,1,8]{2,1,0:T(1,128)} %bitcast), calls=%async_computation | async-start | bytes 65536 | tf_op jit(solution)/shard_map/all_to_all | solution.py:598
  16.4 1.4 copy-done.7
  17.8 0.7 copy-done.19
  18.6 2.2 %tables.1 = (f32[72,64,128]{2,1,0:T(8,128)S(1)}, f32[144,8,128]{2,1,0:T(8,128)S(1)}, f32[96,8,128]{2,1,0:T(8,128)S(1)}, f32[12,512,128]{2,1,0:T(8,128)S(1)}) custom-call(f32[12,64,512]{2,1,0:T(8,128)S(1)} %bitcast.60, s32[12,1,512]{2,1,0:T(1,128)S(1)} %bitcast.66), custom_call_target="tpu_custom_call" | custom-call | tf_op jit(solution)/shard_map/tables/pallas_call | solution.py:610
  20.7 1.6 copy-done.21
  22.4 3.5 %all-to-all-done = s32[64,1,8]{2,1,0:T(1,128)S(1)} async-done(((s32[64,1,8]{2,1,0:T(1,128)}), s32[64,1,8]{2,1,0:T(1,128)S(1)}, u32[]{:S(2)}, u32[]{:S(2)}) %all-to-all-start) | async-done | bytes 2080 | tf_op jit(solution)/shard_map/all_to_all | solution.py:598
  25.9 3.7 %pack.1 = f32[64,80,128]{2,1,0:T(8,128)} custom-call(s32[64,8]{1,0:T(8,128)S(1)} %bitcast.64, f32[72,64,128]{2,1,0:T(8,128)S(1)} %get-tuple-element.29.face_ref, f32[144,8,128]{2,1,0:T(8,128)S(1)} %get-tuple-element.30.edge_ref, f32[96,8,128]{2,1,0:T(8,128)S(1)} %get-tuple-element.31.corner_ref), custom_call_target="tpu_custom_call" | custom-call | tf_op jit(solution)/shard_map/pack/pallas_call | solution.py:631
  29.6 7.4 %all-to-all-start.1 = ((f32[64,80,128]{2,1,0:T(8,128)}), f32[64,80,128]{2,1,0:T(8,128)}, u32[]{:S(2)}, u32[]{:S(2)}) async-start(f32[64,80,128]{2,1,0:T(8,128)} %pack.1), calls=%async_computation.1 | async-start | bytes 5242880 | tf_op jit(solution)/shard_map/all_to_all | solution.py:639
  37.0 0.8 weights.1
  37.8 1.4 copy-done
  39.2 1.9 %copy-done.22 = f32[12,512,128]{2,1,0:T(8,128)S(1)} copy-done((f32[12,512,128]{2,1,0:T(8,128)S(1)}, f32[12,512,128]{2,1,0:T(8,128)}, u32[]{:S(2)}) %copy-start.22) | copy-done | bytes 3145752
  41.1 9.2 %own_forward.1 = (f32[12,4,8,8,128]{4,3,2,1,0:T(8,128)S(1)}, f32[12,4,8,8,128]{4,3,2,1,0:T(8,128)S(1)}, bf16[3,6,2,5,10,16,128]{6,5,4,3,2,1,0:T(8,128)(2,1)S(1)}) custom-call(f32[12,512,128]{2,1,0:T(8,128)S(1)} %copy-done.22, s32[12,1,512]{2,1,0:T(1,128)S(1)} %bitcast.67, f32[12,64,512]{2,1,0:T(8,128)S(1)} %bitcast.70, ...), custom_call_target="tpu_custom_call" | custom-call | flops 7247757312 | bytes 15000000 | tf_op jit(solution)/shard_map/own_forward/pallas_call | solution.py:649
  50.3 2.9 %copy-done.2 = bf16[3,6,2,5,10,16,128]{6,5,4,3,2,1,0:T(8,128)(2,1)} copy-done((bf16[3,6,2,5,10,16,128]{6,5,4,3,2,1,0:T(8,128)(2,1)}, bf16[3,6,2,5,10,16,128]{6,5,4,3,2,1,0:T(8,128)(2,1)S(1)}, u32[]{:S(2)}) %copy-start.2) | copy-done | bytes 7372824
  53.3 1.4 copy-done.5
  54.6 1.1 copy-done.8
  55.8 1.1 copy-done.10
  56.9 14.3 %all-to-all-done.1.recv_ref = f32[64,80,128]{2,1,0:T(8,128)} async-done(((f32[64,80,128]{2,1,0:T(8,128)}), f32[64,80,128]{2,1,0:T(8,128)}, u32[]{:S(2)}, u32[]{:S(2)}) %all-to-all-start.1) | async-done | bytes 2621472 | tf_op jit(solution)/shard_map/all_to_all | solution.py:639
  71.2 1.7 copy-done.6
  72.9 1.4 copy-done.9
  74.3 1.4 copy-done.11
  75.7 15.4 %halo.1 = (f32[3072,128]{1,0:T(8,128)S(1)}, f32[3072,128]{1,0:T(8,128)S(1)}, f32[64,80,128]{2,1,0:T(8,128)}, bf16[2,3,10,6,16,128]{5,4,3,2,1,0:T(8,128)(2,1)S(1)...) custom-call(s32[312]{0:T(512)S(1)} %get-tuple-element.68.code_ref, ...), custom_call_target="tpu_custom_call" | custom-call | tf_op jit(solution)/shard_map/halo/pallas_call | solution.py:666
  91.0 1.1 copy-done.12
  92.1 1.1 copy-done.14
  93.3 0.9 copy-done.17
  94.1 6.9 %all-to-all-start.2 = ((f32[64,80,128]{2,1,0:T(8,128)}), f32[64,80,128]{2,1,0:T(8,128)}, u32[]{:S(2)}, u32[]{:S(2)}) async-start(f32[64,80,128]{2,1,0:T(8,128)} %get-tuple-element.48), calls=%async_computation.2 | async-start | bytes 5242880 | tf_op jit(solution)/shard_map/all_to_all | solution.py:692
  101.1 1.4 copy-done.13
  102.4 1.4 copy-done.15
  103.8 1.1 copy-done.18
  104.9 14.3 %kernel_grad.1 = f32[3,3,4,128,64]{4,3,2,1,0:T(8,128)S(1)} custom-call(bf16[3,6,2,5,10,16,128]{6,5,4,3,2,1,0:T(8,128)(2,1)} %copy-done.2, bf16[2,3,10,6,16,128]{5,4,3,2,1,0:T(8,128)(2,1)S(1)} %copy-done.13, bf16[2,3,2,5,6,16,128]{6,5,4,3,2,1,0:T(8,128)(2,1)S(1)} %copy-done.15, bf16[2,2,5,10,16,128]{5,4,3,2,1,0:T(8,128)(2,1)S(1)} %copy-done.18, ...), custom_call_target="tpu_custom_call" | custom-call | bytes 1000 | tf_op jit(solution)/shard_map/kernel_grad/pallas_call | solution.py:696
  119.2 1.1 fusion
  120.3 1.5 copy.28
  121.8 0.3 reshape.90
  122.1 1.0 copy.31
  123.0 1.0 pad.4.clone
  124.1 0.2 copy.30
  124.3 0.1 collective-permute-start
  124.4 1.4 collective-permute-done
  125.9 1.6 collective-permute-start.1
  127.5 2.9 %collective-permute-start.2 = (f32[16,7,128]{2,0,1:T(8,128)S(1)}, f32[16,7,128]{2,0,1:T(8,128)S(1)}, u32[]{:S(2)}, u32[]{:S(2)}) collective-permute-start(f32[16,7,128]{2,0,1:T(8,128)S(1)} %get-tuple-element.59), channel_id=1, source_target_pairs={{0,32},{1,33},{2,34},{3,35},{4,36},{5,37},{6,38},{7,39},{8,40},{9,... | collective-permute-start | bytes 172040 | tf_op jit(solution)/shard_map/ppermute | solution.py:557
  130.4 0.3 collective-permute-start.3
  130.7 3.2 %activated.1 = f32[12,64,512]{2,1,0:T(8,128)} custom-call(f32[12,4,8,8,128]{4,3,2,1,0:T(8,128)S(1)} %bitcast.61, s32[12,1,512]{2,1,0:T(1,128)S(1)} %bitcast.68), custom_call_target="tpu_custom_call" | custom-call | bytes 1000 | tf_op jit(solution)/shard_map/activated/pallas_call | solution.py:738
  133.9 1.7 copy-done.1
  135.6 1.4 copy-done.4
  137.0 9.5 %own_backward.1.own_ref = f32[12,4,2,8,8,64]{5,4,3,2,1,0:T(8,128)S(1)} custom-call(f32[12,4,8,8,128]{4,3,2,1,0:T(8,128)S(1)} %bitcast.59, bf16[4608,256]{1,0:T(8,128)(2,1)S(1)} %copy-done.1), custom_call_target="tpu_custom_call" | custom-call | bytes 1000 | tf_op jit(solution)/shard_map/own_backward/pallas_call | solution.py:727
  146.5 0.8 fusion.3
  147.4 1.6 collective-permute-start.4
  148.9 2.7 %collective-permute-start.5 = (f32[4,7,128]{2,0,1:T(4,128)S(1)}, f32[4,7,128]{2,0,1:T(4,128)S(1)}, u32[]{:S(2)}, u32[]{:S(2)}) collective-permute-start(f32[4,7,128]{2,0,1:T(4,128)S(1)} %get-tuple-element.62), channel_id=1, source_target_pairs={{0,8},{1,9},{2,10},{3,11},{4,12},{5,13},{6,14},{7,15},{8,0},{9,1},... | collective-permute-start | bytes 43016 | tf_op jit(solution)/shard_map/ppermute | solution.py:557
  151.6 0.5 collective-permute-start.6
  152.1 2.0 %collective-permute-done.5 = f32[4,7,128]{2,0,1:T(4,128)S(1)} collective-permute-done((f32[4,7,128]{2,0,1:T(4,128)S(1)}, f32[4,7,128]{2,0,1:T(4,128)S(1)}, u32[]{:S(2)}, u32[]{:S(2)}) %collective-permute-start.5) | collective-permute-done | bytes 14368 | tf_op jit(solution)/shard_map/ppermute | solution.py:557
  154.1 2.4 %collective-permute-done.6 = f32[4,7,128]{2,0,1:T(4,128)S(1)} collective-permute-done((f32[4,7,128]{2,0,1:T(4,128)S(1)}, f32[4,7,128]{2,0,1:T(4,128)S(1)}, u32[]{:S(2)}, u32[]{:S(2)}) %collective-permute-start.6) | collective-permute-done | bytes 14368 | tf_op jit(solution)/shard_map/ppermute | solution.py:557
  156.6 1.5 collective-permute-start.7
  158.1 2.7 %collective-permute-start.8 = (f32[1,7,128]{2,0,1:T(1,128)S(1)}, f32[1,7,128]{2,0,1:T(1,128)S(1)}, u32[]{:S(2)}, u32[]{:S(2)}) collective-permute-start(f32[1,7,128]{2,0,1:T(1,128)S(1)} %get-tuple-element.65), channel_id=1, source_target_pairs={{0,2},{1,3},{2,0},{3,1},{4,6},{5,7},{6,4},{7,5},{8,10},{9,11},{10,... | collective-permute-start | bytes 10760 | tf_op jit(solution)/shard_map/ppermute | solution.py:557
  160.8 0.6 collective-permute-start.9
  161.4 6.9 %collect.1 = f32[12,64,512]{2,1,0:T(8,128)} custom-call(s32[64,8]{1,0:T(8,128)S(1)} %bitcast.65, f32[64,80,128]{2,1,0:T(8,128)} %all-to-all-done.2.back_ref, f32[12,4,2,8,8,64]{5,4,3,2,1,0:T(8,128)S(1)} %own_backward.1.own_ref, s32[12,1,512]{2,1,0:T(1,128)S(1)} %bitcast.69), custom_call_target="tpu_custom_call" | custom-call | tf_op jit(solution)/shard_map/collect/pallas_call | solution.py:756
  168.3 0.6 slice_multiply_fusion
  (51 shorter events, 0.5 us)
Async XLA Ops:
  4.9 21.0 %all-to-all-start = ((s32[64,1,8]{2,1,0:T(1,128)}), s32[64,1,8]{2,1,0:T(1,128)S(1)}, u32[]{:S(2)}, u32[]{:S(2)}) async-start(s32[64,1,8]{2,1,0:T(1,128)} %bitcast), calls=%async_computation | async-start | bytes 65536 | tf_op jit(solution)/shard_map/all_to_all | solution.py:598
  16.4 1.4 copy-start.7
  17.8 0.7 copy-start.19
  20.7 1.6 copy-start.21
  29.6 7.4 %copy-start.16 = (f32[27,64,64]{2,1,0:T(8,128)S(1)}, f32[27,64,64]{2,1,0:T(8,128)}, u32[]{:S(2)}) copy-start(f32[27,64,64]{2,1,0:T(8,128)} %w_ref.1) | copy-start | bytes 1327108
  29.6 9.6 %copy-start.25 = (f32[64]{0:T(128)S(1)}, f32[64]{0:T(128)}, u32[]{:S(2)}) copy-start(f32[64]{0:T(128)} %param.15) | copy-start | bytes 772
  29.6 9.6 %copy-start.20 = (s32[1,12,512]{2,0,1:T(1,128)S(1)}, s32[1,12,512]{2,0,1:T(1,128)}, u32[]{:S(2)}) copy-start(s32[1,12,512]{2,0,1:T(1,128)} %param.13) | copy-start | bytes 73732
  29.6 9.6 %copy-start.23 = (f32[1,12,512,64]{2,3,1,0:T(8,128)S(1)}, f32[1,12,512,64]{2,3,1,0:T(8,128)}, u32[]{:S(2)}) copy-start(f32[1,12,512,64]{2,3,1,0:T(8,128)} %param.16) | copy-start | bytes 4718596
  29.6 41.6 %all-to-all-start.1 = ((f32[64,80,128]{2,1,0:T(8,128)}), f32[64,80,128]{2,1,0:T(8,128)}, u32[]{:S(2)}, u32[]{:S(2)}) async-start(f32[64,80,128]{2,1,0:T(8,128)} %pack.1), calls=%async_computation.1 | async-start | bytes 5242880 | tf_op jit(solution)/shard_map/all_to_all | solution.py:639
  37.8 1.4 copy-start
  39.2 1.9 %copy-start.22 = (f32[12,512,128]{2,1,0:T(8,128)S(1)}, f32[12,512,128]{2,1,0:T(8,128)}, u32[]{:S(2)}) copy-start(f32[12,512,128]{2,1,0:T(8,128)} %copy-done.21) | copy-start | bytes 9437188
  50.3 2.9 %copy-start.2 = (bf16[3,6,2,5,10,16,128]{6,5,4,3,2,1,0:T(8,128)(2,1)}, bf16[3,6,2,5,10,16,128]{6,5,4,3,2,1,0:T(8,128)(2,1)S(1)}, u32[]{:S(2)}) copy-start(bf16[3,6,2,5,10,16,128]{6,5,4,3,2,1,0:T(8,128)(2,1)S(1)} %get-tuple-element.39.a_ref) | copy-start | bytes 22118404
  53.3 1.4 copy-start.5
  54.6 1.1 copy-start.8
  55.8 1.1 copy-start.10
  71.2 1.7 copy-start.6
  72.8 1.4 copy-start.9
  74.3 1.4 copy-start.11
  91.0 1.1 copy-start.12
  92.1 1.1 copy-start.14
  93.2 0.9 copy-start.17
  94.1 6.9 %copy-start.3 = (f32[3072,128]{1,0:T(8,128)}, f32[3072,128]{1,0:T(8,128)S(1)}, u32[]{:S(2)}) copy-start(f32[3072,128]{1,0:T(8,128)S(1)} %get-tuple-element.37) | copy-start | bytes 4718596
  94.1 62.4 %all-to-all-start.2 = ((f32[64,80,128]{2,1,0:T(8,128)}), f32[64,80,128]{2,1,0:T(8,128)}, u32[]{:S(2)}, u32[]{:S(2)}) async-start(f32[64,80,128]{2,1,0:T(8,128)} %get-tuple-element.48), calls=%async_computation.2 | async-start | bytes 5242880 | tf_op jit(solution)/shard_map/all_to_all | solution.py:692
  101.0 1.4 copy-start.13
  102.4 1.4 copy-start.15
  103.8 1.1 copy-start.18
  124.3 1.6 collective-permute-start
  125.9 4.8 %copy-start.24 = (f32[64,7,128]{2,0,1:T(8,128)}, f32[64,7,128]{2,0,1:T(8,128)S(1)}, u32[]{:S(2)}) copy-start(f32[64,7,128]{2,0,1:T(8,128)S(1)} %bitcast_add_fusion) | copy-start | bytes 688132
  125.9 20.5 %collective-permute-start.1 = (f32[16,7,128]{2,0,1:T(8,128)S(1)}, f32[16,7,128]{2,0,1:T(8,128)S(1)}, u32[]{:S(2)}, u32[]{:S(2)}) collective-permute-start(f32[16,7,128]{2,0,1:T(8,128)S(1)} %get-tuple-element.57), channel_id=1, source_target_pairs={{0,16},{1,17},{2,18},{3,19},{4,20},{5,21},{6,22},{7,23},{8,24},{9,... | collective-permute-start | bytes 172040 | tf_op jit(solution)/shard_map/ppermute | solution.py:557
  127.5 18.9 %collective-permute-start.2 = (f32[16,7,128]{2,0,1:T(8,128)S(1)}, f32[16,7,128]{2,0,1:T(8,128)S(1)}, u32[]{:S(2)}, u32[]{:S(2)}) collective-permute-start(f32[16,7,128]{2,0,1:T(8,128)S(1)} %get-tuple-element.59), channel_id=1, source_target_pairs={{0,32},{1,33},{2,34},{3,35},{4,36},{5,37},{6,38},{7,39},{8,40},{9,... | collective-permute-start | bytes 172040 | tf_op jit(solution)/shard_map/ppermute | solution.py:557
  130.4 16.1 %collective-permute-start.3 = (f32[16,7,128]{2,0,1:T(8,128)S(1)}, f32[16,7,128]{2,0,1:T(8,128)S(1)}, u32[]{:S(2)}, u32[]{:S(2)}) collective-permute-start(f32[16,7,128]{2,0,1:T(8,128)S(1)} %get-tuple-element.58), channel_id=1, source_target_pairs={{0,48},{1,49},{2,50},{3,51},{4,52},{5,53},{6,54},{7,55},{8,56},{9,... | collective-permute-start | bytes 172040 | tf_op jit(solution)/shard_map/ppermute | solution.py:557
  133.9 1.7 copy-start.1
  135.6 1.4 copy-start.4
  147.4 4.8 %collective-permute-start.4 = (f32[4,7,128]{2,0,1:T(4,128)S(1)}, f32[4,7,128]{2,0,1:T(4,128)S(1)}, u32[]{:S(2)}, u32[]{:S(2)}) collective-permute-start(f32[4,7,128]{2,0,1:T(4,128)S(1)} %get-tuple-element.60), channel_id=1, source_target_pairs={{0,4},{1,5},{2,6},{3,7},{4,0},{5,1},{6,2},{7,3},{8,12},{9,13},{10,... | collective-permute-start | bytes 43016 | tf_op jit(solution)/shard_map/ppermute | solution.py:557
  148.9 5.2 %collective-permute-start.5 = (f32[4,7,128]{2,0,1:T(4,128)S(1)}, f32[4,7,128]{2,0,1:T(4,128)S(1)}, u32[]{:S(2)}, u32[]{:S(2)}) collective-permute-start(f32[4,7,128]{2,0,1:T(4,128)S(1)} %get-tuple-element.62), channel_id=1, source_target_pairs={{0,8},{1,9},{2,10},{3,11},{4,12},{5,13},{6,14},{7,15},{8,0},{9,1},... | collective-permute-start | bytes 43016 | tf_op jit(solution)/shard_map/ppermute | solution.py:557
  151.6 4.9 %collective-permute-start.6 = (f32[4,7,128]{2,0,1:T(4,128)S(1)}, f32[4,7,128]{2,0,1:T(4,128)S(1)}, u32[]{:S(2)}, u32[]{:S(2)}) collective-permute-start(f32[4,7,128]{2,0,1:T(4,128)S(1)} %get-tuple-element.61), channel_id=1, source_target_pairs={{0,12},{1,13},{2,14},{3,15},{4,8},{5,9},{6,10},{7,11},{8,4},{9,5},... | collective-permute-start | bytes 43016 | tf_op jit(solution)/shard_map/ppermute | solution.py:557
  156.6 11.7 %collective-permute-start.7 = (f32[1,7,128]{2,0,1:T(1,128)S(1)}, f32[1,7,128]{2,0,1:T(1,128)S(1)}, u32[]{:S(2)}, u32[]{:S(2)}) collective-permute-start(f32[1,7,128]{2,0,1:T(1,128)S(1)} %get-tuple-element.63), channel_id=1, source_target_pairs={{0,1},{1,0},{2,3},{3,2},{4,5},{5,4},{6,7},{7,6},{8,9},{9,8},{10,11... | collective-permute-start | bytes 10760 | tf_op jit(solution)/shard_map/ppermute | solution.py:557
  158.1 10.1 %collective-permute-start.8 = (f32[1,7,128]{2,0,1:T(1,128)S(1)}, f32[1,7,128]{2,0,1:T(1,128)S(1)}, u32[]{:S(2)}, u32[]{:S(2)}) collective-permute-start(f32[1,7,128]{2,0,1:T(1,128)S(1)} %get-tuple-element.65), channel_id=1, source_target_pairs={{0,2},{1,3},{2,0},{3,1},{4,6},{5,7},{6,4},{7,5},{8,10},{9,11},{10,... | collective-permute-start | bytes 10760 | tf_op jit(solution)/shard_map/ppermute | solution.py:557
  160.8 7.4 %collective-permute-start.9 = (f32[1,7,128]{2,0,1:T(1,128)S(1)}, f32[1,7,128]{2,0,1:T(1,128)S(1)}, u32[]{:S(2)}, u32[]{:S(2)}) collective-permute-start(f32[1,7,128]{2,0,1:T(1,128)S(1)} %get-tuple-element.64), channel_id=1, source_target_pairs={{0,3},{1,2},{2,1},{3,0},{4,7},{5,6},{6,5},{7,4},{8,11},{9,10},{10,... | collective-permute-start | bytes 10760 | tf_op jit(solution)/shard_map/ppermute | solution.py:557

commit v4 on v3

--- a/solution.py
+++ b/solution.py
@@ -198,8 +198,16 @@
     return pl.ds(pl.multiple_of(64 + 8 * (e >> 1), 8), 8), e & 1
 
 
-def halo_kernel(code_ref, recv_ref, own_ref, cot_ref, wf_ref, wb_ref,
-                act_ref, dpre_ref, send_ref, px, py, pz, pre, zf, qx, qy, qz, rx, ry, rz, tmp):
+def halo_kernel(code_ref, recv_ref, own_hbm, cot_hbm, wf_hbm, wb_hbm,
+                act_hbm, dpre_hbm, send_ref, px_hbm, py_hbm, pz_hbm,
+                pre, cot_ref, wf_ref, wb_ref, act_ref, dpre_ref, px, py, pz,
+                zf, qx, qy, qz, rx, ry, rz, tmp, sems):
+    arriving = [pltpu.make_async_copy(a, b, sems.at[n]) for n, (a, b) in enumerate(
+        [(own_hbm, pre), (wf_hbm, wf_ref), (cot_hbm, cot_ref), (wb_hbm, wb_ref)])]
+    leaving = [pltpu.make_async_copy(a, b, sems.at[4 + n]) for n, (a, b) in enumerate(
+        [(px, px_hbm), (py, py_hbm), (pz, pz_hbm), (act_ref, act_hbm), (dpre_ref, dpre_hbm)])]
+    for c in arriving:
+        c.start()
     high8 = half_of((8, 128))
     half8 = high8.astype(jnp.int32)
     row = lax.broadcasted_iota(jnp.int32, (8, 128), 0)
@@ -297,7 +305,10 @@
     def prow(b, xh, y, z):
         return ((b * 4 + xh) * 8 + y) * 8 + z
 
-    pre[...] = own_ref[...]
+    for c in leaving[:3]:
+        c.start()
+    arriving[0].wait()
+    arriving[1].wait()
     for s in range(2):
         v = side_x(px, s, 3 * s, 8, wf_ref)
         for y in range(8):
@@ -327,7 +338,10 @@
         dpre_ref[a, :] = cot_ref[a, :] * (sig + ps * (1.0 - sig))
         return carry
 
+    arriving[2].wait()
     lax.fori_loop(0, 24, activate, 0)
+    leaving[3].start()
+    leaving[4].start()
 
     for s in range(2):
         for l in range(3):
@@ -363,6 +377,7 @@
                 v = jnp.concatenate([first, last, jnp.zeros((4, 128), F32)], axis=0)
                 for p in range(2):
                     qz[s, p, xh + 1, y + 2] = split_halves(placed(v, wanted16[p]), low)
+    arriving[3].wait()
     for s in range(2):
         rx[s] = side_x(qx, s, 3 - 3 * s, 10, wb_ref)
         ry[s] = side_y(qy, s, 2 - 2 * s, wb_ref)
@@ -408,6 +423,8 @@
                 v = placed(jnp.broadcast_to(rz[r:r + 1, :], (8, 128)), wanted[xt % 2])
                 spot = jnp.logical_and(row == pos - 5, high8)
                 send_ref[o, 72:80, :] = jnp.where(spot, v, send_ref[o, 72:80, :])
+    for c in leaving:
+        c.wait()
 
 
 def turned_terms(out_ref, at, v):
@@ -418,7 +435,7 @@
     out_ref[128:256, at:at + n] = (t - top.astype(F32)).astype(BF16)
 
 
-def kernel_grad_kernel(a_ref, px_ref, py_ref, pz_ref, d_ref, out_ref, dt, dx, dy, dz):
+def kernel_grad_kernel(a_ref, px_ref, py_ref, pz_ref, d_ref, out_ref, dt, dx, dy, dz, sums):
     l = pl.program_id(0)
 
     @pl.when(l == 0)
@@ -458,14 +475,14 @@
         for h in range(2):
             parts = [a_ref[0, :, q, h:h + 4, j:j + 8].reshape(3072, 128) for q in range(2)]
             for q, v in enumerate(product(dt[...], parts)):
-                out_ref[0, j, 2 * h + q] = v
+                sums[j, 2 * h + q] = v
     for s in range(2):
         parts = [px_ref[s, 0, j:j + 8].reshape(768, 128) for j in range(3)]
         for j, v in enumerate(product(dx[s], parts)):
-            out_ref[0, j, 3 * s] += v
+            sums[j, 3 * s] += v
         parts = [py_ref[s, 0, i % 2, i // 2:i // 2 + 4].reshape(384, 128) for i in range(4)]
         for i, v in enumerate(product(dy[s], parts)):
-            out_ref[0, 2 * s, i] += v
+            sums[2 * s, i] += v
 
     @pl.when(l != 1)
     def _():
@@ -473,7 +490,11 @@
         for j in range(3):
             parts = [pz_ref[s, i % 2, i // 2:i // 2 + 4, j:j + 8].reshape(512, 128) for i in range(4)]
             for i, v in enumerate(product(dz[s], parts)):
-                out_ref[0, j, i] += v
+                sums[j, i] += v
+
+    for i in range(3):
+        for j in range(3):
+            out_ref[i, j, 0] = (sums[j, i, 0:64] + sums[j, i + 1, 64:128]).T
 
 
 def collect_kernel(want_ref, back_ref, own_ref, m_ref, out_ref, faces, edges, corners, rows):
@@ -545,18 +566,20 @@
 
 def swap_scenes(v):
     scene = lax.axis_index("scene")
-    v = v.reshape(2, 64, 7, 128)
-    mine = lax.dynamic_index_in_dim(v, scene, 0, keepdims=False)
-    theirs = lax.dynamic_index_in_dim(v, 1 - scene, 0, keepdims=False)
+    mine = lax.dynamic_slice_in_dim(v, scene * 864, 864, 0)
+    theirs = lax.dynamic_slice_in_dim(v, (1 - scene) * 864, 864, 0)
     return mine + lax.ppermute(theirs, "scene", [(0, 1), (1, 0)])
 
 
 def sum_stage(v, stride):
     at = (lax.axis_index("brick") // stride) % 4
-    v = v.reshape(4, stride, 7, 128)
-    sent = [lax.ppermute(lax.dynamic_index_in_dim(v, at ^ d, 0, keepdims=False), "brick",
-                         [(n, n ^ (d * stride)) for n in range(64)]) for d in (1, 2, 3)]
-    return lax.dynamic_index_in_dim(v, at, 0, keepdims=False), sent
+    n = v.shape[0] // 4
+
+    def quarter(k):
+        return lax.dynamic_slice_in_dim(v, k * n, n, 0)
+
+    sent = [lax.ppermute(quarter(at ^ d), "brick", [(m, m ^ (d * stride)) for m in range(64)]) for d in (1, 2, 3)]
+    return quarter(at), sent
 
 
 def whole(memory=pltpu.VMEM):
@@ -569,6 +592,14 @@
 
 def lead_block(shape):
     return pl.BlockSpec(shape, lambda g: (g,) + (0,) * (len(shape) - 1))
+
+
+def in_hbm(x):
+    return pltpu.with_memory_space_constraint(x, pltpu.HBM)
+
+
+def hbm_out(shape, kind):
+    return pltpu.HBM(shape, kind)
 
 
 def params(mib):
@@ -601,7 +632,7 @@
         weights_kernel,
         in_specs=[whole()],
         out_specs=[whole(), whole()],
-        out_shape=[jax.ShapeDtypeStruct((4608, 256), BF16)] * 2,
+        out_shape=[hbm_out((4608, 256), BF16)] * 2,
         compiler_params=params(16),
         cost_estimate=pl.CostEstimate(flops=0, bytes_accessed=6000000, transcendentals=0),
         name="weights",
@@ -621,7 +652,7 @@
             jax.ShapeDtypeStruct((72, 64, 128), F32),
             jax.ShapeDtypeStruct((144, 8, 128), F32),
             jax.ShapeDtypeStruct((96, 8, 128), F32),
-            jax.ShapeDtypeStruct((12, 512, 128), F32),
+            hbm_out((12, 512, 128), F32),
         ],
         scratch_shapes=[pltpu.VMEM((512, 128), F32)],
         compiler_params=params(16),
@@ -655,28 +686,41 @@
             packed_block,
             pl.BlockSpec((3, 1, 2, 5, 10, 16, 128), lambda g: (0, g, 0, 0, 0, 0, 0)),
         ],
-        out_shape=[packed_shape, packed_shape, jax.ShapeDtypeStruct((3, 6, 2, 5, 10, 16, 128), BF16)],
+        out_shape=[
+            hbm_out(packed_shape.shape, F32),
+            hbm_out(packed_shape.shape, F32),
+            hbm_out((3, 6, 2, 5, 10, 16, 128), BF16),
+        ],
         compiler_params=params(24),
         cost_estimate=pl.CostEstimate(flops=2 * 3072 * 4608 * 256, bytes_accessed=15000000, transcendentals=0),
         name="own_forward",
-    )(rows, mask, cot, wf, bias2)
+    )(in_hbm(rows), mask, in_hbm(cot), in_hbm(wf), bias2)
 
     flat = (3072, 128)
     side_x, side_y, side_z = (2, 3, 10, 6, 16, 128), (2, 3, 2, 5, 6, 16, 128), (2, 2, 5, 10, 16, 128)
+    held = pl.BlockSpec(memory_space=pl.ANY)
     act, dpre, send, px, py, pz = pl.pallas_call(
         halo_kernel,
-        in_specs=[whole(pltpu.SMEM)] + [whole()] * 5,
-        out_specs=[whole()] * 6,
+        in_specs=[whole(pltpu.SMEM), whole()] + [held] * 4,
+        out_specs=[held, held, whole(), held, held, held],
         out_shape=[
-            jax.ShapeDtypeStruct(flat, F32),
-            jax.ShapeDtypeStruct(flat, F32),
+            hbm_out(flat, F32),
+            hbm_out(flat, F32),
             jax.ShapeDtypeStruct((64, 80, 128), F32),
-            jax.ShapeDtypeStruct(side_x, BF16),
-            jax.ShapeDtypeStruct(side_y, BF16),
-            jax.ShapeDtypeStruct(side_z, BF16),
+            hbm_out(side_x, BF16),
+            hbm_out(side_y, BF16),
+            hbm_out(side_z, BF16),
         ],
         scratch_shapes=[
             pltpu.VMEM(flat, F32),
+            pltpu.VMEM(flat, F32),
+            pltpu.VMEM((4608, 256), BF16),
+            pltpu.VMEM((4608, 256), BF16),
+            pltpu.VMEM(flat, F32),
+            pltpu.VMEM(flat, F32),
+            pltpu.VMEM(side_x, BF16),
+            pltpu.VMEM(side_y, BF16),
+            pltpu.VMEM(side_z, BF16),
             pltpu.VMEM((3200, 128), F32),
             pltpu.VMEM((2, 3, 12, 6, 16, 128), BF16),
             pltpu.VMEM((2, 3, 2, 5, 6, 16, 128), BF16),
@@ -685,10 +729,11 @@
             pltpu.VMEM((2, 384, 128), F32),
             pltpu.VMEM((1600, 128), F32),
             pltpu.VMEM((8, 128), F32),
-        ],
-        compiler_params=params(40),
+            pltpu.SemaphoreType.DMA((9,)),
+        ],
+        compiler_params=params(44),
         name="halo",
-    )(code, recv, own_pre.reshape(flat), cot_p.reshape(flat), wf, wb)
+    )(code, recv, in_hbm(own_pre.reshape(flat)), in_hbm(cot_p.reshape(flat)), in_hbm(wf), in_hbm(wb))
     back = lax.all_to_all(send, "brick", split_axis=0, concat_axis=0, tiled=True)
     act = act.reshape(packed_shape.shape)
     dpre = dpre.reshape(packed_shape.shape)
@@ -703,21 +748,20 @@
             const_block(side_z),
             const_block(packed_shape.shape),
         ],
-        out_specs=lead_block((1, 3, 4, 128, 64)),
-        out_shape=jax.ShapeDtypeStruct((3, 3, 4, 128, 64), F32),
+        out_specs=pl.BlockSpec((3, 3, 1, 64, 64), lambda l: (0, 0, l, 0, 0)),
+        out_shape=jax.ShapeDtypeStruct((3, 3, 3, 64, 64), F32),
         scratch_shapes=[
             pltpu.VMEM((256, 3072), BF16),
             pltpu.VMEM((2, 256, 768), BF16),
             pltpu.VMEM((2, 256, 384), BF16),
             pltpu.VMEM((2, 256, 512), BF16),
+            pltpu.VMEM((3, 4, 128, 64), F32),
         ],
         compiler_params=params(40),
         cost_estimate=pl.CostEstimate(flops=0, bytes_accessed=1000, transcendentals=0),
         name="kernel_grad",
-    )(windows, px, py, pz, dpre)
-    kernel = z[:, :, 0:3, 0:64] + z[:, :, 1:4, 64:128]
-    kernel = kernel.transpose(2, 1, 0, 4, 3).reshape(128, 864)
-    kernel = jnp.pad(kernel, ((0, 0), (0, 32))).reshape(128, 7, 128)
+    )(in_hbm(windows), in_hbm(px), in_hbm(py), in_hbm(pz), in_hbm(dpre))
+    kernel = z.reshape(1728, 64)
     scale = 1.0 / math.sqrt(float(2 * 768 * 512))
     act, kernel = lax.optimization_barrier((act, kernel))
     total = swap_scenes(kernel)
@@ -734,7 +778,7 @@
         compiler_params=params(24),
         cost_estimate=pl.CostEstimate(flops=0, bytes_accessed=1000, transcendentals=0),
         name="own_backward",
-    )(dpre, wb)
+    )(in_hbm(dpre), in_hbm(wb))
     activated = pl.pallas_call(
         activated_kernel,
         grid=(6,),
@@ -744,10 +788,11 @@
         compiler_params=params(8),
         cost_estimate=pl.CostEstimate(flops=0, bytes_accessed=1000, transcendentals=0),
         name="activated",
-    )(act, mask)
+    )(in_hbm(act), mask)
 
     total = kept + sent[0] + sent[1] + sent[2]
     own, total, activated = lax.optimization_barrier((own, total, activated))
+    total = jnp.pad(total.reshape(16, 864), ((0, 0), (0, 32))).reshape(16, 7, 128)
     kept, sent = sum_stage(total, 4)
     total = kept + sent[0] + sent[1] + sent[2]
     back, total = lax.optimization_barrier((back, total))

time: 170 us -> 160 us (0.941)
  local copies, waits for them, and re-layouts: 33.3 us -> 6.4 us
  Pallas kernels: 65 us -> 78.5 us
  waiting for transfers between devices: 23.6 us -> 28.5 us
    unnamed x53 -> x16, local copies, waits for them, and re-layouts: 29.2 us -> 4.4 us
    all_to_all x1, waiting for transfers between devices: 14.3 us -> 18.4 us  [on_device(): recv = lax.all_to_all(out, 'brick', split_axis=0, concat_axis=0, tiled=True)]
    pallas_call x1, Pallas kernels: 9.19 us -> 12.4 us  [on_device(): pl.pallas_call(own_forward_kernel, grid=(6,), in_specs=[lead_block((2, 51...]
    pallas_call x1, Pallas kernels: 0.77 us -> 2.9 us  [on_device(): pl.pallas_call(weights_kernel, in_specs=[whole()], out_specs=[whole(), wh...]
    pallas_call x1, Pallas kernels: 3.17 us -> 5.19 us  [on_device(): pl.pallas_call(activated_kernel, grid=(6,), in_specs=[packed_block, mask_...]
    pallas_call x1, Pallas kernels: 9.48 us -> 11.3 us  [on_device(): pl.pallas_call(own_backward_kernel, grid=(6,), in_specs=[packed_block, co...]
  transfers between devices with their start and end apart: 13 -> 13, of which waited for: 5 -> 5; matrix products, arithmetic and copies ran while one was open for 4% -> 1% of each run, Pallas kernels for 27% -> 36%
where the time goes in v4:
time: 160 us; the launch traced here: 159 us
  Pallas kernels  78.5 us (49%)
  starting transfers between devices  39.2 us (25%)
  waiting for transfers between devices  28.5 us (18%)
  local copies, waits for them, and re-layouts  6.4 us (4%)
  other arithmetic  4.94 us (3%)
    all_to_all x1, waiting for transfers between devices, on_device(): recv = lax.all_to_all(out, 'brick', split_axis=0, concat_axis=0, tiled=True)  18.4 us
    pallas_call x1, Pallas kernels, on_device(): pl.pallas_call(halo_kernel, in_specs=[whole(pltpu.SMEM), whole()] + [held...  17 us
    pallas_call x1, Pallas kernels, on_device(): pl.pallas_call(kernel_grad_kernel, grid=(3,), in_specs=[pl.BlockSpec((1,...  15.8 us
    ppermute x9, starting transfers between devices, sum_stage(): lax.ppermute(quarter(at ^ d), 'brick', [(m, m ^ d * stride) for m in rang...  14.3 us
    pallas_call x1, Pallas kernels, on_device(): pl.pallas_call(own_forward_kernel, grid=(6,), in_specs=[lead_block((2, 51...  12.4 us
    all_to_all x1, starting transfers between devices, on_device(): lax.all_to_all(wanted, 'brick', split_axis=0, concat_axis=0, tiled=True)  11.5 us
    pallas_call x1, Pallas kernels, on_device(): pl.pallas_call(own_backward_kernel, grid=(6,), in_specs=[packed_block, co...  11.3 us
    all_to_all x1, starting transfers between devices, on_device(): lax.all_to_all(send, 'brick', split_axis=0, concat_axis=0, tiled=True)  6.88 us
  transfers between devices with their start and end apart: 13, of which 5 were waited for; matrix products, arithmetic and copies ran while one was open for 1% of the time, Pallas kernels for 36%

profile of v4, /device:TPU:0, one launch (start us, length us, event | category | flops | bytes accessed | tf_op | source)
XLA Modules:
  0.0 158.5 jit_solution(16840459115488776366)
XLA Ops:
  0.6 0.8 add_reduce_fusion.1
  1.4 0.1 reshape.80
  1.5 0.1 convert_reduce_fusion
  1.6 0.1 mul.62
  1.7 0.7 reduce.2
  2.4 0.1 reshape.67
  2.5 0.8 add_reduce_fusion
  3.3 0.1 reshape.86
  3.3 0.7 compare_select_fusion
  4.0 0.2 select_reduce_fusion
  4.2 0.7 sub.18
  4.9 11.5 %all-to-all-start = ((s32[64,1,8]{2,1,0:T(1,128)}), s32[64,1,8]{2,1,0:T(1,128)S(1)}, u32[]{:S(2)}, u32[]{:S(2)}) async-start(s32[64,1,8]{2,1,0:T(1,128)} %bitcast), calls=%async_computation | async-start | bytes 65536 | tf_op jit(solution)/shard_map/all_to_all | solution.py:629
  16.4 0.0 copy-start.1
  16.4 1.4 copy-done.1
  17.8 0.0 copy-start.3
  17.8 0.7 copy-done.3
  18.6 3.4 %tables.1 = (f32[72,64,128]{2,1,0:T(8,128)S(1)}, f32[144,8,128]{2,1,0:T(8,128)S(1)}, f32[96,8,128]{2,1,0:T(8,128)S(1)}, f32[12,512,128]{2,1,0:T(8,128)}) custom-call(f32[12,64,512]{2,1,0:T(8,128)S(1)} %bitcast.26, s32[12,1,512]{2,1,0:T(1,128)S(1)} %bitcast.29), custom_call_target="tpu_custom_call" | custom-call | tf_op jit(solution)/shard_map/tables/pallas_call | solution.py:641
  21.9 4.0 %all-to-all-done = s32[64,1,8]{2,1,0:T(1,128)S(1)} async-done(((s32[64,1,8]{2,1,0:T(1,128)}), s32[64,1,8]{2,1,0:T(1,128)S(1)}, u32[]{:S(2)}, u32[]{:S(2)}) %all-to-all-start) | async-done | bytes 2080 | tf_op jit(solution)/shard_map/all_to_all | solution.py:629
  25.9 3.7 %pack.1 = f32[64,80,128]{2,1,0:T(8,128)} custom-call(s32[64,8]{1,0:T(8,128)S(1)} %bitcast.27, f32[72,64,128]{2,1,0:T(8,128)S(1)} %get-tuple-element.29.face_ref, f32[144,8,128]{2,1,0:T(8,128)S(1)} %get-tuple-element.30.edge_ref, f32[96,8,128]{2,1,0:T(8,128)S(1)} %get-tuple-element.31.corner_ref), custom_call_target="tpu_custom_call" | custom-call | tf_op jit(solution)/shard_map/pack/pallas_call | solution.py:662
  29.6 6.5 %all-to-all-start.1 = ((f32[64,80,128]{2,1,0:T(8,128)}), f32[64,80,128]{2,1,0:T(8,128)S(1)}, u32[]{:S(2)}, u32[]{:S(2)}) async-start(f32[64,80,128]{2,1,0:T(8,128)} %pack.1), calls=%async_computation.1 | async-start | bytes 5242880 | tf_op jit(solution)/shard_map/all_to_all | solution.py:670
  36.1 0.0 copy-done.2
  36.1 2.9 %weights.1 = (bf16[4608,256]{1,0:T(8,128)(2,1)}, bf16[4608,256]{1,0:T(8,128)(2,1)}) custom-call(f32[27,64,64]{2,1,0:T(8,128)S(1)} %copy-done.2), custom_call_target="tpu_custom_call" | custom-call | bytes 6000000 | tf_op jit(solution)/shard_map/weights/pallas_call | solution.py:631
  39.0 0.0 copy-done.7
  39.0 0.1 maximum_bitcast_fusion.bias_ref
  39.1 0.7 copy-done.4
  39.9 12.4 %own_forward.1 = (f32[12,4,8,8,128]{4,3,2,1,0:T(8,128)}, f32[12,4,8,8,128]{4,3,2,1,0:T(8,128)}, bf16[3,6,2,5,10,16,128]{6,5,4,3,2,1,0:T(8,128)(2,1)}) custom-call(f32[12,512,128]{2,1,0:T(8,128)} %get-tuple-element.32.x_ref, s32[12,1,512]{2,1,0:T(1,128)S(1)} %bitcast.30, f32[12,64,512]{2,1,0:T(8,128)} %bitcast.40, ...), custom_call_target="tpu_custom_call" | custom-call | flops 7247757312 | bytes 15000000 | tf_op jit(solution)/shard_map/own_forward/pallas_call | solution.py:680
  52.2 18.4 %all-to-all-done.1.recv_ref = f32[64,80,128]{2,1,0:T(8,128)S(1)} async-done(((f32[64,80,128]{2,1,0:T(8,128)}), f32[64,80,128]{2,1,0:T(8,128)S(1)}, u32[]{:S(2)}, u32[]{:S(2)}) %all-to-all-start.1) | async-done | bytes 2621472 | tf_op jit(solution)/shard_map/all_to_all | solution.py:670
  70.6 17.0 %halo.1 = (f32[3072,128]{1,0:T(8,128)}, f32[3072,128]{1,0:T(8,128)}, f32[64,80,128]{2,1,0:T(8,128)S(1)}, bf16[2,3,10,6,16,128]{5,4,3,2,1,0:T(8,128)(2,1)}, bf16[...) custom-call(s32[312]{0:T(512)S(1)} %get-tuple-element.68.code_ref, ...), custom_call_target="tpu_custom_call" | custom-call | tf_op jit(solution)/shard_map/halo/pallas_call | solution.py:702
  87.6 0.0 copy-start
  87.7 1.5 copy-done
  89.1 6.9 %all-to-all-start.2 = ((f32[64,80,128]{2,1,0:T(8,128)}), f32[64,80,128]{2,1,0:T(8,128)}, u32[]{:S(2)}, u32[]{:S(2)}) async-start(f32[64,80,128]{2,1,0:T(8,128)} %copy-done), calls=%async_computation.2 | async-start | bytes 5242880 | tf_op jit(solution)/shard_map/all_to_all | solution.py:737
  96.0 15.8 %kernel_grad.1 = f32[3,3,3,64,64]{4,3,2,1,0:T(8,128)S(1)} custom-call(bf16[3,6,2,5,10,16,128]{6,5,4,3,2,1,0:T(8,128)(2,1)} %get-tuple-element.39.a_ref, bf16[2,3,10,6,16,128]{5,4,3,2,1,0:T(8,128)(2,1)} %get-tuple-element.40.px_ref, bf16[2,3,2,5,6,16,128]{6,5,4,3,2,1,0:T(8,128)(2,1)} %get-tuple-element.41.py_ref, ...), custom_call_target="tpu_custom_call" | custom-call | bytes 1000 | tf_op jit(solution)/shard_map/kernel_grad/pallas_call | solution.py:741
  111.8 0.0 copy-start.5
  111.9 0.1 collective-permute-start
  112.0 1.7 %collective-permute-done = f32[864,64]{1,0:T(8,128)S(1)} collective-permute-done((f32[864,64]{1,0:T(8,128)S(1)}, f32[864,64]{1,0:T(8,128)S(1)}, u32[]{:S(2)}, u32[]{:S(2)}) %collective-permute-start) | collective-permute-done | bytes 221216 | tf_op jit(solution)/shard_map/ppermute | solution.py:571
  113.8 0.0 copy-start.6
  113.8 0.8 constant_dynamic-slice_fusion.9
  114.6 1.5 collective-permute-start.1
  116.1 2.9 %collective-permute-start.2 = (f32[216,64]{1,0:T(8,128)}, f32[216,64]{1,0:T(8,128)S(1)}, u32[]{:S(2)}, u32[]{:S(2)}) collective-permute-start(f32[216,64]{1,0:T(8,128)} %get-tuple-element.59), channel_id=1, source_target_pairs={{0,32},{1,33},{2,34},{3,35},{4,36},{5,37},{6,38},{7,39},{8,40},{9,... | collective-permute-start | bytes 165896 | tf_op jit(solution)/shard_map/ppermute | solution.py:581
  119.0 0.3 collective-permute-start.3
  119.3 0.0 copy-done.6
  119.3 0.0 copy-done.5
  119.3 5.2 %activated.1 = f32[12,64,512]{2,1,0:T(8,128)} custom-call(f32[12,4,8,8,128]{4,3,2,1,0:T(8,128)} %bitcast.35, s32[12,1,512]{2,1,0:T(1,128)S(1)} %bitcast.31), custom_call_target="tpu_custom_call" | custom-call | bytes 1000 | tf_op jit(solution)/shard_map/activated/pallas_call | solution.py:782
  124.5 11.3 %own_backward.1.own_ref = f32[12,4,2,8,8,64]{5,4,3,2,1,0:T(8,128)S(1)} custom-call(f32[12,4,8,8,128]{4,3,2,1,0:T(8,128)} %bitcast.34, bf16[4608,256]{1,0:T(8,128)(2,1)} %get-tuple-element.36.wb_hbm.w_ref), custom_call_target="tpu_custom_call" | custom-call | bytes 1000 | tf_op jit(solution)/shard_map/own_backward/pallas_call | solution.py:771
  135.8 0.0 collective-permute-done.1
  135.8 0.0 collective-permute-done.2
  135.9 0.0 collective-permute-done.3
  135.9 1.0 add_add_fusion
  136.9 0.1 reshape.76
  137.0 1.6 collective-permute-start.4
  138.6 2.7 %collective-permute-start.5 = (f32[4,7,128]{2,1,0:T(8,128)S(1)}, f32[4,7,128]{2,1,0:T(8,128)S(1)}, u32[]{:S(2)}, u32[]{:S(2)}) collective-permute-start(f32[4,7,128]{2,1,0:T(8,128)S(1)} %get-tuple-element.62), channel_id=1, source_target_pairs={{0,8},{1,9},{2,10},{3,11},{4,12},{5,13},{6,14},{7,15},{8,0},{9,1},... | collective-permute-start | bytes 43016 | tf_op jit(solution)/shard_map/ppermute | solution.py:581
  141.3 0.5 collective-permute-start.6
  141.8 0.0 collective-permute-done.4
  141.8 2.0 %collective-permute-done.5 = f32[4,7,128]{2,1,0:T(8,128)S(1)} collective-permute-done((f32[4,7,128]{2,1,0:T(8,128)S(1)}, f32[4,7,128]{2,1,0:T(8,128)S(1)}, u32[]{:S(2)}, u32[]{:S(2)}) %collective-permute-start.5) | collective-permute-done | bytes 14368 | tf_op jit(solution)/shard_map/ppermute | solution.py:581
  143.8 2.4 %collective-permute-done.6 = f32[4,7,128]{2,1,0:T(8,128)S(1)} collective-permute-done((f32[4,7,128]{2,1,0:T(8,128)S(1)}, f32[4,7,128]{2,1,0:T(8,128)S(1)}, u32[]{:S(2)}, u32[]{:S(2)}) %collective-permute-start.6) | collective-permute-done | bytes 14368 | tf_op jit(solution)/shard_map/ppermute | solution.py:581
  146.2 0.0 all-to-all-done.2.back_ref
  146.3 1.6 collective-permute-start.7
  147.8 2.7 %collective-permute-start.8 = (f32[1,7,128]{2,1,0:T(8,128)S(1)}, f32[1,7,128]{2,1,0:T(8,128)S(1)}, u32[]{:S(2)}, u32[]{:S(2)}) collective-permute-start(f32[1,7,128]{2,1,0:T(8,128)S(1)} %get-tuple-element.65), channel_id=1, source_target_pairs={{0,2},{1,3},{2,0},{3,1},{4,6},{5,7},{6,4},{7,5},{8,10},{9,11},{10,... | collective-permute-start | bytes 10760 | tf_op jit(solution)/shard_map/ppermute | solution.py:581
  150.5 0.5 collective-permute-start.9
  151.0 6.9 %collect.1 = f32[12,64,512]{2,1,0:T(8,128)} custom-call(s32[64,8]{1,0:T(8,128)S(1)} %bitcast.28, f32[64,80,128]{2,1,0:T(8,128)} %all-to-all-done.2.back_ref, f32[12,4,2,8,8,64]{5,4,3,2,1,0:T(8,128)S(1)} %own_backward.1.own_ref, s32[12,1,512]{2,1,0:T(1,128)S(1)} %bitcast.32), custom_call_target="tpu_custom_call" | custom-call | tf_op jit(solution)/shard_map/collect/pallas_call | solution.py:801
  157.9 0.0 collective-permute-done.7
  157.9 0.0 collective-permute-done.8
  157.9 0.0 collective-permute-done.9
  157.9 0.6 slice_multiply_fusion
  (12 shorter events, 0.2 us)
Async XLA Ops:
  4.9 21.0 %all-to-all-start = ((s32[64,1,8]{2,1,0:T(1,128)}), s32[64,1,8]{2,1,0:T(1,128)S(1)}, u32[]{:S(2)}, u32[]{:S(2)}) async-start(s32[64,1,8]{2,1,0:T(1,128)} %bitcast), calls=%async_computation | async-start | bytes 65536 | tf_op jit(solution)/shard_map/all_to_all | solution.py:629
  16.4 1.4 copy-start.1
  17.8 0.7 copy-start.3
  29.6 6.5 %copy-start.2 = (f32[27,64,64]{2,1,0:T(8,128)S(1)}, f32[27,64,64]{2,1,0:T(8,128)}, u32[]{:S(2)}) copy-start(f32[27,64,64]{2,1,0:T(8,128)} %w_ref.1) | copy-start | bytes 1327108
  29.6 9.4 %copy-start.7 = (f32[64]{0:T(128)S(1)}, f32[64]{0:T(128)}, u32[]{:S(2)}) copy-start(f32[64]{0:T(128)} %param.15) | copy-start | bytes 772
  29.6 41.0 %all-to-all-start.1 = ((f32[64,80,128]{2,1,0:T(8,128)}), f32[64,80,128]{2,1,0:T(8,128)S(1)}, u32[]{:S(2)}, u32[]{:S(2)}) async-start(f32[64,80,128]{2,1,0:T(8,128)} %pack.1), calls=%async_computation.1 | async-start | bytes 5242880 | tf_op jit(solution)/shard_map/all_to_all | solution.py:670
  39.1 0.7 copy-start.4
  87.6 1.5 copy-start
  89.1 57.1 %all-to-all-start.2 = ((f32[64,80,128]{2,1,0:T(8,128)}), f32[64,80,128]{2,1,0:T(8,128)}, u32[]{:S(2)}, u32[]{:S(2)}) async-start(f32[64,80,128]{2,1,0:T(8,128)} %copy-done), calls=%async_computation.2 | async-start | bytes 5242880 | tf_op jit(solution)/shard_map/all_to_all | solution.py:737
  111.8 7.5 %copy-start.5 = (s32[1,12,512]{2,0,1:T(1,128)S(1)}, s32[1,12,512]{2,0,1:T(1,128)}, u32[]{:S(2)}) copy-start(s32[1,12,512]{2,0,1:T(1,128)} %param.13) | copy-start | bytes 73732
  111.9 1.9 %collective-permute-start = (f32[864,64]{1,0:T(8,128)S(1)}, f32[864,64]{1,0:T(8,128)S(1)}, u32[]{:S(2)}, u32[]{:S(2)}) collective-permute-start(f32[864,64]{1,0:T(8,128)S(1)} %constant_dynamic-slice_fusion.10), channel_id=1, source_target_pairs={{0,64},{64,0},{1,65},{65,1},{2,66},{66,2},{3,67},{67,3},{4,68},{68... | collective-permute-start | bytes 663560 | tf_op jit(solution)/shard_map/ppermute | solution.py:571
  113.8 5.5 %copy-start.6 = (f32[864,64]{1,0:T(8,128)}, f32[864,64]{1,0:T(8,128)S(1)}, u32[]{:S(2)}) copy-start(f32[864,64]{1,0:T(8,128)S(1)} %dynamic-slice_add_fusion) | copy-start | bytes 663556
  114.6 21.2 %collective-permute-start.1 = (f32[216,64]{1,0:T(8,128)}, f32[216,64]{1,0:T(8,128)S(1)}, u32[]{:S(2)}, u32[]{:S(2)}) collective-permute-start(f32[216,64]{1,0:T(8,128)} %get-tuple-element.57), channel_id=1, source_target_pairs={{0,16},{1,17},{2,18},{3,19},{4,20},{5,21},{6,22},{7,23},{8,24},{9,... | collective-permute-start | bytes 165896 | tf_op jit(solution)/shard_map/ppermute | solution.py:581
  116.1 19.7 %collective-permute-start.2 = (f32[216,64]{1,0:T(8,128)}, f32[216,64]{1,0:T(8,128)S(1)}, u32[]{:S(2)}, u32[]{:S(2)}) collective-permute-start(f32[216,64]{1,0:T(8,128)} %get-tuple-element.59), channel_id=1, source_target_pairs={{0,32},{1,33},{2,34},{3,35},{4,36},{5,37},{6,38},{7,39},{8,40},{9,... | collective-permute-start | bytes 165896 | tf_op jit(solution)/shard_map/ppermute | solution.py:581
  119.0 16.9 %collective-permute-start.3 = (f32[216,64]{1,0:T(8,128)S(1)}, f32[216,64]{1,0:T(8,128)}, u32[]{:S(2)}, u32[]{:S(2)}) collective-permute-start(f32[216,64]{1,0:T(8,128)S(1)} %get-tuple-element.58), channel_id=1, source_target_pairs={{0,48},{1,49},{2,50},{3,51},{4,52},{5,53},{6,54},{7,55},{8,56},{9,... | collective-permute-start | bytes 165896 | tf_op jit(solution)/shard_map/ppermute | solution.py:581
  137.0 4.8 %collective-permute-start.4 = (f32[4,7,128]{2,1,0:T(8,128)S(1)}, f32[4,7,128]{2,1,0:T(8,128)S(1)}, u32[]{:S(2)}, u32[]{:S(2)}) collective-permute-start(f32[4,7,128]{2,1,0:T(8,128)S(1)} %get-tuple-element.60), channel_id=1, source_target_pairs={{0,4},{1,5},{2,6},{3,7},{4,0},{5,1},{6,2},{7,3},{8,12},{9,13},{10,... | collective-permute-start | bytes 43016 | tf_op jit(solution)/shard_map/ppermute | solution.py:581
  138.6 5.2 %collective-permute-start.5 = (f32[4,7,128]{2,1,0:T(8,128)S(1)}, f32[4,7,128]{2,1,0:T(8,128)S(1)}, u32[]{:S(2)}, u32[]{:S(2)}) collective-permute-start(f32[4,7,128]{2,1,0:T(8,128)S(1)} %get-tuple-element.62), channel_id=1, source_target_pairs={{0,8},{1,9},{2,10},{3,11},{4,12},{5,13},{6,14},{7,15},{8,0},{9,1},... | collective-permute-start | bytes 43016 | tf_op jit(solution)/shard_map/ppermute | solution.py:581
  141.3 4.9 %collective-permute-start.6 = (f32[4,7,128]{2,1,0:T(8,128)S(1)}, f32[4,7,128]{2,1,0:T(8,128)S(1)}, u32[]{:S(2)}, u32[]{:S(2)}) collective-permute-start(f32[4,7,128]{2,1,0:T(8,128)S(1)} %get-tuple-element.61), channel_id=1, source_target_pairs={{0,12},{1,13},{2,14},{3,15},{4,8},{5,9},{6,10},{7,11},{8,4},{9,5},... | collective-permute-start | bytes 43016 | tf_op jit(solution)/shard_map/ppermute | solution.py:581
  146.3 11.7 %collective-permute-start.7 = (f32[1,7,128]{2,1,0:T(8,128)S(1)}, f32[1,7,128]{2,1,0:T(8,128)S(1)}, u32[]{:S(2)}, u32[]{:S(2)}) collective-permute-start(f32[1,7,128]{2,1,0:T(8,128)S(1)} %get-tuple-element.63), channel_id=1, source_target_pairs={{0,1},{1,0},{2,3},{3,2},{4,5},{5,4},{6,7},{7,6},{8,9},{9,8},{10,11... | collective-permute-start | bytes 10760 | tf_op jit(solution)/shard_map/ppermute | solution.py:581
  147.8 10.1 %collective-permute-start.8 = (f32[1,7,128]{2,1,0:T(8,128)S(1)}, f32[1,7,128]{2,1,0:T(8,128)S(1)}, u32[]{:S(2)}, u32[]{:S(2)}) collective-permute-start(f32[1,7,128]{2,1,0:T(8,128)S(1)} %get-tuple-element.65), channel_id=1, source_target_pairs={{0,2},{1,3},{2,0},{3,1},{4,6},{5,7},{6,4},{7,5},{8,10},{9,11},{10,... | collective-permute-start | bytes 10760 | tf_op jit(solution)/shard_map/ppermute | solution.py:581
  150.5 7.4 %collective-permute-start.9 = (f32[1,7,128]{2,1,0:T(8,128)S(1)}, f32[1,7,128]{2,1,0:T(8,128)S(1)}, u32[]{:S(2)}, u32[]{:S(2)}) collective-permute-start(f32[1,7,128]{2,1,0:T(8,128)S(1)} %get-tuple-element.64), channel_id=1, source_target_pairs={{0,3},{1,2},{2,1},{3,0},{4,7},{5,6},{6,5},{7,4},{8,11},{9,10},{10,... | collective-permute-start | bytes 10760 | tf_op jit(solution)/shard_map/ppermute | solution.py:581

commit v5 on v4

--- a/solution.py
+++ b/solution.py
@@ -156,7 +156,7 @@
         cotm_ref[b] = jnp.concatenate([c[:, 0], c[:, 1]], axis=-1)
 
 
-def own_backward_kernel(d_ref, w_ref, own_ref, a_ref):
+def own_backward_kernel(d_ref, act_ref, m_ref, w_ref, own_ref, out_ref, a_ref):
     @pl.when(pl.program_id(0) == 0)
     def _():
         a_ref[...] = jnp.zeros_like(a_ref)
@@ -176,16 +176,16 @@
     for b in range(2):
         own_ref[b, :, 0] = out[:, :, b * 8:b * 8 + 8, :64]
         own_ref[b, :, 1] = out[:, :, b * 8:b * 8 + 8, 64:]
-
-
-def activated_kernel(act_ref, m_ref, out_ref):
-    for b in range(2):
         mask = m_ref[b].astype(F32)
         for h in range(2):
             t = act_ref[b, 2 * h:2 * h + 2].reshape(128, 128).T
             v = jnp.concatenate([t[:64, :64], t[64:, :64], t[:64, 64:], t[64:, 64:]], axis=1)
             a = slice(h * 256, h * 256 + 256)
             out_ref[b, :, a] = v * mask[:, a]
+
+
+def rest_kernel(d_ref, act_ref, m_ref, w_ref, own_held, out_held, own_ref, out_ref, a_ref):
+    own_backward_kernel(d_ref, act_ref, m_ref, w_ref, own_ref, out_ref, a_ref)
 
 
 def unpack_code(code_ref, b, k):
@@ -706,7 +706,7 @@
         out_shape=[
             hbm_out(flat, F32),
             hbm_out(flat, F32),
-            jax.ShapeDtypeStruct((64, 80, 128), F32),
+            hbm_out((64, 80, 128), F32),
             hbm_out(side_x, BF16),
             hbm_out(side_y, BF16),
             hbm_out(side_z, BF16),
@@ -763,37 +763,35 @@
     )(in_hbm(windows), in_hbm(px), in_hbm(py), in_hbm(pz), in_hbm(dpre))
     kernel = z.reshape(1728, 64)
     scale = 1.0 / math.sqrt(float(2 * 768 * 512))
-    act, kernel = lax.optimization_barrier((act, kernel))
     total = swap_scenes(kernel)
     dpre, total = lax.optimization_barrier((dpre, total))
     kept, sent = sum_stage(total, 16)
 
-    own = pl.pallas_call(
-        own_backward_kernel,
-        grid=(6,),
-        in_specs=[packed_block, const_block((4608, 256))],
-        out_specs=brick_block,
-        out_shape=brick_shape,
-        scratch_shapes=[pltpu.VMEM((3, 1, 2, 5, 10, 16, 128), BF16)],
-        compiler_params=params(24),
-        cost_estimate=pl.CostEstimate(flops=0, bytes_accessed=1000, transcendentals=0),
-        name="own_backward",
-    )(in_hbm(dpre), in_hbm(wb))
-    activated = pl.pallas_call(
-        activated_kernel,
-        grid=(6,),
-        in_specs=[packed_block, mask_block],
-        out_specs=turned_block,
-        out_shape=turned_shape,
-        compiler_params=params(8),
-        cost_estimate=pl.CostEstimate(flops=0, bytes_accessed=1000, transcendentals=0),
-        name="activated",
-    )(in_hbm(act), mask)
-
+    def own_backward(body, first, d, extra):
+        def block(shape):
+            return pl.BlockSpec(shape, lambda g: (g + first,) + (0,) * (len(shape) - 1))
+
+        packed2, brick2, turned2 = block((2, 4, 8, 8, 128)), block((2, 4, 2, 8, 8, 64)), block((2, 64, 512))
+        return pl.pallas_call(
+            body,
+            grid=(3,),
+            in_specs=[packed2, packed2, block((2, 1, 512)), const_block((4608, 256))] + [held] * len(extra),
+            out_specs=[brick2, turned2],
+            out_shape=[hbm_out(brick_shape.shape, F32), hbm_out(turned_shape.shape, F32)],
+            scratch_shapes=[pltpu.VMEM((3, 1, 2, 5, 10, 16, 128), BF16)],
+            input_output_aliases={4 + n: n for n in range(len(extra))},
+            compiler_params=params(24),
+            cost_estimate=pl.CostEstimate(flops=0, bytes_accessed=1000, transcendentals=0),
+            name="own_backward",
+        )(in_hbm(d), in_hbm(act), mask, in_hbm(wb), *extra)
+
+    own, activated = own_backward(own_backward_kernel, 0, dpre, [])
     total = kept + sent[0] + sent[1] + sent[2]
     own, total, activated = lax.optimization_barrier((own, total, activated))
     total = jnp.pad(total.reshape(16, 864), ((0, 0), (0, 32))).reshape(16, 7, 128)
     kept, sent = sum_stage(total, 4)
+    own, activated = own_backward(rest_kernel, 3, dpre, [in_hbm(own), in_hbm(activated)])
+    own, activated, kept = lax.optimization_barrier((own, activated, kept))
     total = kept + sent[0] + sent[1] + sent[2]
     back, total = lax.optimization_barrier((back, total))
     kept, sent = sum_stage(total, 1)
@@ -817,7 +815,7 @@
         ],
         compiler_params=params(24),
         name="collect",
-    )(asked, back, own, mask)
+    )(asked, back, in_hbm(own), mask)
     grad, kept = lax.optimization_barrier((grad, kept))
     share = (kept + sent[0] + sent[1] + sent[2]).reshape(896)[:864] * scale
     return activated.transpose(0, 2, 1)[None], grad.transpose(0, 2, 1)[None], share

time: 160 us -> 161 us (level)
  transfers between devices with their start and end apart: 13 -> 13, of which waited for: 5 -> 4; matrix products, arithmetic and copies ran while one was open for 1% -> 2% of each run, Pallas kernels for 36% -> 36%
where the time goes in v5:
time: 161 us; the launch traced here: 160 us
  Pallas kernels  79 us (49%)
  starting transfers between devices  39.6 us (25%)
  waiting for transfers between devices  28.7 us (18%)
  other arithmetic  5.9 us (4%)
  local copies, waits for them, and re-layouts  5.52 us (3%)
    all_to_all x1, waiting for transfers between devices, on_device(): recv = lax.all_to_all(out, 'brick', split_axis=0, concat_axis=0, tiled=True)  19.1 us
    pallas_call x1, Pallas kernels, on_device(): pl.pallas_call(halo_kernel, in_specs=[whole(pltpu.SMEM), whole()] + [held...  18.6 us
    pallas_call x1, Pallas kernels, on_device(): pl.pallas_call(kernel_grad_kernel, grid=(3,), in_specs=[pl.BlockSpec((1,...  15.8 us
    pallas_call x2, Pallas kernels, own_backward(): pl.pallas_call(body, grid=(3,), in_specs=[packed2, packed2, block((2, 1,...  15.2 us
    ppermute x9, starting transfers between devices, sum_stage(): lax.ppermute(quarter(at ^ d), 'brick', [(m, m ^ d * stride) for m in rang...  14.9 us
    pallas_call x1, Pallas kernels, on_device(): pl.pallas_call(own_forward_kernel, grid=(6,), in_specs=[lead_block((2, 51...  12.4 us
    all_to_all x1, starting transfers between devices, on_device(): lax.all_to_all(wanted, 'brick', split_axis=0, concat_axis=0, tiled=True)  11.5 us
    pallas_call x1, Pallas kernels, on_device(): pl.pallas_call(collect_kernel, grid=(4,), in_specs=[pl.BlockSpec(memory_s...  7.02 us
  transfers between devices with their start and end apart: 13, of which 4 were waited for; matrix products, arithmetic and copies ran while one was open for 2% of the time, Pallas kernels for 36%

profile of v5, /device:TPU:0, one launch (start us, length us, event | category | flops | bytes accessed | tf_op | source)
XLA Modules:
  0.0 159.6 jit_solution(3246588311430389166)
XLA Ops:
  0.6 0.8 add_reduce_fusion.1
  1.4 0.1 reshape.80
  1.5 0.1 convert_reduce_fusion
  1.6 0.1 mul.62
  1.7 0.7 reduce.2
  2.4 0.1 reshape.67
  2.5 0.8 add_reduce_fusion
  3.3 0.1 reshape.86
  3.3 0.7 compare_select_fusion
  4.0 0.2 select_reduce_fusion
  4.2 0.7 sub.18
  4.9 11.5 %all-to-all-start = ((s32[64,1,8]{2,1,0:T(1,128)}), s32[64,1,8]{2,1,0:T(1,128)S(1)}, u32[]{:S(2)}, u32[]{:S(2)}) async-start(s32[64,1,8]{2,1,0:T(1,128)} %bitcast), calls=%async_computation | async-start | bytes 65536 | tf_op jit(solution)/shard_map/all_to_all | solution.py:629
  16.4 0.0 copy-start
  16.4 1.4 copy-done
  17.8 0.0 copy-start.2
  17.8 0.7 copy-done.2
  18.6 3.4 %tables.1 = (f32[72,64,128]{2,1,0:T(8,128)S(1)}, f32[144,8,128]{2,1,0:T(8,128)S(1)}, f32[96,8,128]{2,1,0:T(8,128)S(1)}, f32[12,512,128]{2,1,0:T(8,128)}) custom-call(f32[12,64,512]{2,1,0:T(8,128)S(1)} %bitcast.26, s32[12,1,512]{2,1,0:T(1,128)S(1)} %bitcast.27), custom_call_target="tpu_custom_call" | custom-call | tf_op jit(solution)/shard_map/tables/pallas_call | solution.py:641
  22.0 3.9 %all-to-all-done = s32[64,1,8]{2,1,0:T(1,128)S(1)} async-done(((s32[64,1,8]{2,1,0:T(1,128)}), s32[64,1,8]{2,1,0:T(1,128)S(1)}, u32[]{:S(2)}, u32[]{:S(2)}) %all-to-all-start) | async-done | bytes 2080 | tf_op jit(solution)/shard_map/all_to_all | solution.py:629
  25.9 3.7 %pack.1 = f32[64,80,128]{2,1,0:T(8,128)} custom-call(s32[64,8]{1,0:T(8,128)S(1)} %bitcast.32, f32[72,64,128]{2,1,0:T(8,128)S(1)} %get-tuple-element.34.face_ref, f32[144,8,128]{2,1,0:T(8,128)S(1)} %get-tuple-element.35.edge_ref, f32[96,8,128]{2,1,0:T(8,128)S(1)} %get-tuple-element.36.corner_ref), custom_call_target="tpu_custom_call" | custom-call | tf_op jit(solution)/shard_map/pack/pallas_call | solution.py:662
  29.6 0.0 copy-start.4
  29.6 0.6 copy-done.4
  30.2 6.6 %all-to-all-start.1 = ((f32[64,80,128]{2,1,0:T(8,128)}), f32[64,80,128]{2,1,0:T(8,128)S(1)}, u32[]{:S(2)}, u32[]{:S(2)}) async-start(f32[64,80,128]{2,1,0:T(8,128)} %pack.1), calls=%async_computation.1 | async-start | bytes 5242880 | tf_op jit(solution)/shard_map/all_to_all | solution.py:670
  36.8 0.0 copy-done.1
  36.8 2.9 %weights.1 = (bf16[4608,256]{1,0:T(8,128)(2,1)}, bf16[4608,256]{1,0:T(8,128)(2,1)}) custom-call(f32[27,64,64]{2,1,0:T(8,128)S(1)} %copy-done.1), custom_call_target="tpu_custom_call" | custom-call | bytes 6000000 | tf_op jit(solution)/shard_map/weights/pallas_call | solution.py:631
  39.7 0.0 copy-done.7
  39.7 0.1 maximum_bitcast_fusion.bias_ref
  39.8 0.0 copy-done.3
  39.8 12.4 %own_forward.1 = (f32[12,4,8,8,128]{4,3,2,1,0:T(8,128)}, f32[12,4,8,8,128]{4,3,2,1,0:T(8,128)}, bf16[3,6,2,5,10,16,128]{6,5,4,3,2,1,0:T(8,128)(2,1)}) custom-call(f32[12,512,128]{2,1,0:T(8,128)} %get-tuple-element.37.x_ref, s32[12,1,512]{2,1,0:T(1,128)S(1)} %bitcast.28, f32[12,64,512]{2,1,0:T(8,128)} %bitcast.43, ...), custom_call_target="tpu_custom_call" | custom-call | flops 7247757312 | bytes 15000000 | tf_op jit(solution)/shard_map/own_forward/pallas_call | solution.py:680
  52.2 19.1 %all-to-all-done.1.recv_ref = f32[64,80,128]{2,1,0:T(8,128)S(1)} async-done(((f32[64,80,128]{2,1,0:T(8,128)}), f32[64,80,128]{2,1,0:T(8,128)S(1)}, u32[]{:S(2)}, u32[]{:S(2)}) %all-to-all-start.1) | async-done | bytes 2621472 | tf_op jit(solution)/shard_map/all_to_all | solution.py:670
  71.3 18.6 %halo.1 = (f32[3072,128]{1,0:T(8,128)}, f32[3072,128]{1,0:T(8,128)}, f32[64,80,128]{2,1,0:T(8,128)}, bf16[2,3,10,6,16,128]{5,4,3,2,1,0:T(8,128)(2,1)}, bf16[2,3,...) custom-call(s32[312]{0:T(512)S(1)} %get-tuple-element.79.code_ref, ...), custom_call_target="tpu_custom_call" | custom-call | tf_op jit(solution)/shard_map/halo/pallas_call | solution.py:702
  89.9 6.7 %all-to-all-start.2 = ((f32[64,80,128]{2,1,0:T(8,128)}), f32[64,80,128]{2,1,0:T(8,128)S(1)}, u32[]{:S(2)}, u32[]{:S(2)}) async-start(f32[64,80,128]{2,1,0:T(8,128)} %get-tuple-element.58), calls=%async_computation.2 | async-start | bytes 5242880 | tf_op jit(solution)/shard_map/all_to_all | solution.py:737
  96.6 15.8 %kernel_grad.1 = f32[3,3,3,64,64]{4,3,2,1,0:T(8,128)S(1)} custom-call(bf16[3,6,2,5,10,16,128]{6,5,4,3,2,1,0:T(8,128)(2,1)} %get-tuple-element.43.a_ref, bf16[2,3,10,6,16,128]{5,4,3,2,1,0:T(8,128)(2,1)} %get-tuple-element.44.px_ref, bf16[2,3,2,5,6,16,128]{6,5,4,3,2,1,0:T(8,128)(2,1)} %get-tuple-element.45.py_ref, ...), custom_call_target="tpu_custom_call" | custom-call | bytes 1000 | tf_op jit(solution)/shard_map/kernel_grad/pallas_call | solution.py:741
  112.4 0.8 constant_dynamic-slice_fusion.11
  113.2 0.0 collective-permute-start
  113.2 2.1 %collective-permute-done = f32[864,64]{1,0:T(8,128)} collective-permute-done((f32[864,64]{1,0:T(8,128)}, f32[864,64]{1,0:T(8,128)}, u32[]{:S(2)}, u32[]{:S(2)}) %collective-permute-start) | collective-permute-done | bytes 221216 | tf_op jit(solution)/shard_map/ppermute | solution.py:571
  115.3 1.1 dynamic-slice_add_fusion
  116.4 0.0 copy-start.6
  116.4 0.8 copy-done.6
  117.2 1.7 %collective-permute-start.1 = (f32[216,64]{1,0:T(8,128)S(1)}, f32[216,64]{1,0:T(8,128)S(1)}, u32[]{:S(2)}, u32[]{:S(2)}) collective-permute-start(f32[216,64]{1,0:T(8,128)S(1)} %get-tuple-element.67), channel_id=1, source_target_pairs={{0,16},{1,17},{2,18},{3,19},{4,20},{5,21},{6,22},{7,23},{8,24},{9,... | collective-permute-start | bytes 165896 | tf_op jit(solution)/shard_map/ppermute | solution.py:581
  118.8 2.9 %collective-permute-start.2 = (f32[216,64]{1,0:T(8,128)S(1)}, f32[216,64]{1,0:T(8,128)S(1)}, u32[]{:S(2)}, u32[]{:S(2)}) collective-permute-start(f32[216,64]{1,0:T(8,128)S(1)} %get-tuple-element.69), channel_id=1, source_target_pairs={{0,32},{1,33},{2,34},{3,35},{4,36},{5,37},{6,38},{7,39},{8,40},{9,... | collective-permute-start | bytes 165896 | tf_op jit(solution)/shard_map/ppermute | solution.py:581
  121.7 0.2 collective-permute-start.3
  121.9 7.6 %own_backward.2 = (f32[12,4,2,8,8,64]{5,4,3,2,1,0:T(8,128)}, f32[12,64,512]{2,1,0:T(8,128)}) custom-call(f32[12,4,8,8,128]{4,3,2,1,0:T(8,128)} %bitcast.35, f32[12,4,8,8,128]{4,3,2,1,0:T(8,128)} %bitcast.37, s32[12,1,512]{2,1,0:T(1,128)S(1)} %bitcast.29, bf16[4608,256]{1,0:T(8,128)(2,1)} %get-tuple-element.41.wb_hbm.w_ref), custom_call_target="tpu_custom_call" | custom-call | bytes 1000 | tf_op jit(solution)/shard_map/own_backward/pallas_call | solution.py:775
  129.5 0.0 collective-permute-done.1
  129.5 3.5 %collective-permute-done.2 = f32[216,64]{1,0:T(8,128)S(1)} collective-permute-done((f32[216,64]{1,0:T(8,128)S(1)}, f32[216,64]{1,0:T(8,128)S(1)}, u32[]{:S(2)}, u32[]{:S(2)}) %collective-permute-start.2) | collective-permute-done | bytes 55328 | tf_op jit(solution)/shard_map/ppermute | solution.py:581
  133.1 0.0 collective-permute-done.3
  133.1 0.9 add_add_fusion
  134.0 0.1 reshape.76
  134.1 1.1 collective-permute-start.4
  135.2 4.2 %collective-permute-start.5 = (f32[4,7,128]{2,1,0:T(8,128)S(1)}, f32[4,7,128]{2,1,0:T(8,128)S(1)}, u32[]{:S(2)}, u32[]{:S(2)}) collective-permute-start(f32[4,7,128]{2,1,0:T(8,128)S(1)} %get-tuple-element.72), channel_id=1, source_target_pairs={{0,8},{1,9},{2,10},{3,11},{4,12},{5,13},{6,14},{7,15},{8,0},{9,1},... | collective-permute-start | bytes 43016 | tf_op jit(solution)/shard_map/ppermute | solution.py:581
  139.5 0.0 collective-permute-start.6
  139.5 7.6 %own_backward.3 = (f32[12,4,2,8,8,64]{5,4,3,2,1,0:T(8,128)}, f32[12,64,512]{2,1,0:T(8,128)}) custom-call(f32[12,4,8,8,128]{4,3,2,1,0:T(8,128)} %bitcast.36, f32[12,4,8,8,128]{4,3,2,1,0:T(8,128)} %bitcast.38, s32[12,1,512]{2,1,0:T(1,128)S(1)} %bitcast.30, ...), custom_call_target="tpu_custom_call", output_to_operand_aliasing={{0}: (4, {}), {1}: (5, {})} | custom-call | bytes 1000 | tf_op jit(solution)/shard_map/own_backward/pallas_call | solution.py:775
  147.1 0.0 collective-permute-done.4
  147.1 0.0 collective-permute-done.5
  147.1 0.0 collective-permute-done.6
  147.1 0.0 all-to-all-done.2.back_ref
  147.2 0.1 collective-permute-start.7
  147.3 2.1 %collective-permute-start.8 = (f32[1,7,128]{2,1,0:T(8,128)S(1)}, f32[1,7,128]{2,1,0:T(8,128)S(1)}, u32[]{:S(2)}, u32[]{:S(2)}) collective-permute-start(f32[1,7,128]{2,1,0:T(8,128)S(1)} %get-tuple-element.76), channel_id=1, source_target_pairs={{0,2},{1,3},{2,0},{3,1},{4,6},{5,7},{6,4},{7,5},{8,10},{9,11},{10,... | collective-permute-start | bytes 10760 | tf_op jit(solution)/shard_map/ppermute | solution.py:581
  149.4 2.6 %collective-permute-start.9 = (f32[1,7,128]{2,1,0:T(8,128)S(1)}, f32[1,7,128]{2,1,0:T(8,128)S(1)}, u32[]{:S(2)}, u32[]{:S(2)}) collective-permute-start(f32[1,7,128]{2,1,0:T(8,128)S(1)} %get-tuple-element.75), channel_id=1, source_target_pairs={{0,3},{1,2},{2,1},{3,0},{4,7},{5,6},{6,5},{7,4},{8,11},{9,10},{10,... | collective-permute-start | bytes 10760 | tf_op jit(solution)/shard_map/ppermute | solution.py:581
  151.9 0.0 copy-done.5
  151.9 7.0 %collect.1 = f32[12,64,512]{2,1,0:T(8,128)} custom-call(s32[64,8]{1,0:T(8,128)S(1)} %bitcast.33, f32[64,80,128]{2,1,0:T(8,128)S(1)} %all-to-all-done.2.back_ref, f32[12,4,2,8,8,64]{5,4,3,2,1,0:T(8,128)} %get-tuple-element.61.own_ref, s32[12,1,512]{2,1,0:T(1,128)S(1)} %bitcast.31), custom_call_target="tpu_custom_call" | custom-call | tf_op jit(solution)/shard_map/collect/pallas_call | solution.py:799
  159.0 0.0 collective-permute-done.7
  159.0 0.0 collective-permute-done.8
  159.0 0.0 collective-permute-done.9
  159.0 0.6 slice_multiply_fusion
  (12 shorter events, 0.1 us)
Async XLA Ops:
  4.9 21.0 %all-to-all-start = ((s32[64,1,8]{2,1,0:T(1,128)}), s32[64,1,8]{2,1,0:T(1,128)S(1)}, u32[]{:S(2)}, u32[]{:S(2)}) async-start(s32[64,1,8]{2,1,0:T(1,128)} %bitcast), calls=%async_computation | async-start | bytes 65536 | tf_op jit(solution)/shard_map/all_to_all | solution.py:629
  16.4 1.4 copy-start
  17.8 0.7 copy-start.2
  29.6 0.6 copy-start.4
  30.2 6.6 %copy-start.1 = (f32[27,64,64]{2,1,0:T(8,128)S(1)}, f32[27,64,64]{2,1,0:T(8,128)}, u32[]{:S(2)}) copy-start(f32[27,64,64]{2,1,0:T(8,128)} %w_ref.1) | copy-start | bytes 1327108
  30.2 9.5 %copy-start.7 = (f32[64]{0:T(128)S(1)}, f32[64]{0:T(128)}, u32[]{:S(2)}) copy-start(f32[64]{0:T(128)} %param.15) | copy-start | bytes 772
  30.2 9.6 %copy-start.3 = (s32[1,12,512]{2,0,1:T(1,128)S(1)}, s32[1,12,512]{2,0,1:T(1,128)}, u32[]{:S(2)}) copy-start(s32[1,12,512]{2,0,1:T(1,128)} %param.13) | copy-start | bytes 73732
  30.2 41.1 %all-to-all-start.1 = ((f32[64,80,128]{2,1,0:T(8,128)}), f32[64,80,128]{2,1,0:T(8,128)S(1)}, u32[]{:S(2)}, u32[]{:S(2)}) async-start(f32[64,80,128]{2,1,0:T(8,128)} %pack.1), calls=%async_computation.1 | async-start | bytes 5242880 | tf_op jit(solution)/shard_map/all_to_all | solution.py:670
  89.9 57.2 %all-to-all-start.2 = ((f32[64,80,128]{2,1,0:T(8,128)}), f32[64,80,128]{2,1,0:T(8,128)S(1)}, u32[]{:S(2)}, u32[]{:S(2)}) async-start(f32[64,80,128]{2,1,0:T(8,128)} %get-tuple-element.58), calls=%async_computation.2 | async-start | bytes 5242880 | tf_op jit(solution)/shard_map/all_to_all | solution.py:737
  113.2 2.1 %collective-permute-start = (f32[864,64]{1,0:T(8,128)}, f32[864,64]{1,0:T(8,128)}, u32[]{:S(2)}, u32[]{:S(2)}) collective-permute-start(f32[864,64]{1,0:T(8,128)} %constant_dynamic-slice_fusion.11), channel_id=1, source_target_pairs={{0,64},{64,0},{1,65},{65,1},{2,66},{66,2},{3,67},{67,3},{4,68},{68... | collective-permute-start | bytes 663560 | tf_op jit(solution)/shard_map/ppermute | solution.py:571
  116.4 0.8 copy-start.6
  117.2 12.4 %collective-permute-start.1 = (f32[216,64]{1,0:T(8,128)S(1)}, f32[216,64]{1,0:T(8,128)S(1)}, u32[]{:S(2)}, u32[]{:S(2)}) collective-permute-start(f32[216,64]{1,0:T(8,128)S(1)} %get-tuple-element.67), channel_id=1, source_target_pairs={{0,16},{1,17},{2,18},{3,19},{4,20},{5,21},{6,22},{7,23},{8,24},{9,... | collective-permute-start | bytes 165896 | tf_op jit(solution)/shard_map/ppermute | solution.py:581
  118.8 14.2 %collective-permute-start.2 = (f32[216,64]{1,0:T(8,128)S(1)}, f32[216,64]{1,0:T(8,128)S(1)}, u32[]{:S(2)}, u32[]{:S(2)}) collective-permute-start(f32[216,64]{1,0:T(8,128)S(1)} %get-tuple-element.69), channel_id=1, source_target_pairs={{0,32},{1,33},{2,34},{3,35},{4,36},{5,37},{6,38},{7,39},{8,40},{9,... | collective-permute-start | bytes 165896 | tf_op jit(solution)/shard_map/ppermute | solution.py:581
  121.7 11.4 %collective-permute-start.3 = (f32[216,64]{1,0:T(8,128)S(1)}, f32[216,64]{1,0:T(8,128)S(1)}, u32[]{:S(2)}, u32[]{:S(2)}) collective-permute-start(f32[216,64]{1,0:T(8,128)S(1)} %get-tuple-element.68), channel_id=1, source_target_pairs={{0,48},{1,49},{2,50},{3,51},{4,52},{5,53},{6,54},{7,55},{8,56},{9,... | collective-permute-start | bytes 165896 | tf_op jit(solution)/shard_map/ppermute | solution.py:581
  134.1 12.9 %collective-permute-start.4 = (f32[4,7,128]{2,1,0:T(8,128)S(1)}, f32[4,7,128]{2,1,0:T(8,128)S(1)}, u32[]{:S(2)}, u32[]{:S(2)}) collective-permute-start(f32[4,7,128]{2,1,0:T(8,128)S(1)} %get-tuple-element.70), channel_id=1, source_target_pairs={{0,4},{1,5},{2,6},{3,7},{4,0},{5,1},{6,2},{7,3},{8,12},{9,13},{10,... | collective-permute-start | bytes 43016 | tf_op jit(solution)/shard_map/ppermute | solution.py:581
  135.2 11.9 %collective-permute-start.5 = (f32[4,7,128]{2,1,0:T(8,128)S(1)}, f32[4,7,128]{2,1,0:T(8,128)S(1)}, u32[]{:S(2)}, u32[]{:S(2)}) collective-permute-start(f32[4,7,128]{2,1,0:T(8,128)S(1)} %get-tuple-element.72), channel_id=1, source_target_pairs={{0,8},{1,9},{2,10},{3,11},{4,12},{5,13},{6,14},{7,15},{8,0},{9,1},... | collective-permute-start | bytes 43016 | tf_op jit(solution)/shard_map/ppermute | solution.py:581
  139.5 7.6 %collective-permute-start.6 = (f32[4,7,128]{2,1,0:T(8,128)S(1)}, f32[4,7,128]{2,1,0:T(8,128)S(1)}, u32[]{:S(2)}, u32[]{:S(2)}) collective-permute-start(f32[4,7,128]{2,1,0:T(8,128)S(1)} %get-tuple-element.71), channel_id=1, source_target_pairs={{0,12},{1,13},{2,14},{3,15},{4,8},{5,9},{6,10},{7,11},{8,4},{9,5},... | collective-permute-start | bytes 43016 | tf_op jit(solution)/shard_map/ppermute | solution.py:581
  139.5 12.5 %copy-start.5 = (s32[64,1,8]{2,1,0:T(1,128)S(1)}, s32[64,1,8]{2,1,0:T(1,128)}, u32[]{:S(2)}) copy-start(s32[64,1,8]{2,1,0:T(1,128)} %copy-done.4) | copy-start | bytes 6148
  147.2 11.8 %collective-permute-start.7 = (f32[1,7,128]{2,1,0:T(8,128)S(1)}, f32[1,7,128]{2,1,0:T(8,128)S(1)}, u32[]{:S(2)}, u32[]{:S(2)}) collective-permute-start(f32[1,7,128]{2,1,0:T(8,128)S(1)} %get-tuple-element.74), channel_id=1, source_target_pairs={{0,1},{1,0},{2,3},{3,2},{4,5},{5,4},{6,7},{7,6},{8,9},{9,8},{10,11... | collective-permute-start | bytes 10760 | tf_op jit(solution)/shard_map/ppermute | solution.py:581
  147.3 11.7 %collective-permute-start.8 = (f32[1,7,128]{2,1,0:T(8,128)S(1)}, f32[1,7,128]{2,1,0:T(8,128)S(1)}, u32[]{:S(2)}, u32[]{:S(2)}) collective-permute-start(f32[1,7,128]{2,1,0:T(8,128)S(1)} %get-tuple-element.76), channel_id=1, source_target_pairs={{0,2},{1,3},{2,0},{3,1},{4,6},{5,7},{6,4},{7,5},{8,10},{9,11},{10,... | collective-permute-start | bytes 10760 | tf_op jit(solution)/shard_map/ppermute | solution.py:581
  149.4 9.6 %collective-permute-start.9 = (f32[1,7,128]{2,1,0:T(8,128)S(1)}, f32[1,7,128]{2,1,0:T(8,128)S(1)}, u32[]{:S(2)}, u32[]{:S(2)}) collective-permute-start(f32[1,7,128]{2,1,0:T(8,128)S(1)} %get-tuple-element.75), channel_id=1, source_target_pairs={{0,3},{1,2},{2,1},{3,0},{4,7},{5,6},{6,5},{7,4},{8,11},{9,10},{10,... | collective-permute-start | bytes 10760 | tf_op jit(solution)/shard_map/ppermute | solution.py:581

commit v6 on v4

--- a/solution.py
+++ b/solution.py
@@ -793,10 +793,9 @@
     total = kept + sent[0] + sent[1] + sent[2]
     own, total, activated = lax.optimization_barrier((own, total, activated))
     total = jnp.pad(total.reshape(16, 864), ((0, 0), (0, 32))).reshape(16, 7, 128)
-    kept, sent = sum_stage(total, 4)
-    total = kept + sent[0] + sent[1] + sent[2]
     back, total = lax.optimization_barrier((back, total))
-    kept, sent = sum_stage(total, 1)
+    layers = [[16 * n + m for m in range(16)] for n in range(4)]
+    shares = lax.all_to_all(total, "brick", split_axis=0, concat_axis=0, tiled=True, axis_index_groups=layers)
 
     grad = pl.pallas_call(
         collect_kernel,
@@ -818,8 +817,7 @@
         compiler_params=params(24),
         name="collect",
     )(asked, back, own, mask)
-    grad, kept = lax.optimization_barrier((grad, kept))
-    share = (kept + sent[0] + sent[1] + sent[2]).reshape(896)[:864] * scale
+    share = jnp.sum(shares, axis=0).reshape(896)[:864] * scale
     return activated.transpose(0, 2, 1)[None], grad.transpose(0, 2, 1)[None], share
 
 

time: 160 us -> 154 us (0.963)
  waiting for transfers between devices: 28.5 us -> 24.8 us
  starting transfers between devices: 39.2 us -> 36.5 us
    ppermute x9 -> x3, starting transfers between devices: 14.3 us -> 4.7 us  [sum_stage(): lax.ppermute(quarter(at ^ d), 'brick', [(m, m ^ d * stride) for m in rang...]
    all_to_all x0 -> x1, starting transfers between devices: none -> 6.8 us  [on_device(): lax.all_to_all(total, 'brick', split_axis=0, concat_axis=0, tiled=True, a...]
    ppermute x9 -> x3, waiting for transfers between devices: 4.44 us -> 0.01 us  [sum_stage(): lax.ppermute(quarter(at ^ d), 'brick', [(m, m ^ d * stride) for m in rang...]
  transfers between devices with their start and end apart: 13 -> 8, of which waited for: 5 -> 4; matrix products, arithmetic and copies ran while one was open for 1% -> 2% of each run, Pallas kernels for 36% -> 38%
where the time goes in v6:
time: 154 us; the launch traced here: 153 us
  Pallas kernels  78.6 us (51%)
  starting transfers between devices  36.5 us (24%)
  waiting for transfers between devices  24.8 us (16%)
  local copies, waits for them, and re-layouts  7.03 us (5%)
  other arithmetic  4.95 us (3%)
    all_to_all x1, waiting for transfers between devices, on_device(): recv = lax.all_to_all(out, 'brick', split_axis=0, concat_axis=0, tiled=True)  18.4 us
    pallas_call x1, Pallas kernels, on_device(): pl.pallas_call(halo_kernel, in_specs=[whole(pltpu.SMEM), whole()] + [held...  17 us
    pallas_call x1, Pallas kernels, on_device(): pl.pallas_call(kernel_grad_kernel, grid=(3,), in_specs=[pl.BlockSpec((1,...  15.8 us
    pallas_call x1, Pallas kernels, on_device(): pl.pallas_call(own_forward_kernel, grid=(6,), in_specs=[lead_block((2, 51...  12.4 us
    all_to_all x1, starting transfers between devices, on_device(): lax.all_to_all(wanted, 'brick', split_axis=0, concat_axis=0, tiled=True)  11.5 us
    pallas_call x1, Pallas kernels, on_device(): pl.pallas_call(own_backward_kernel, grid=(6,), in_specs=[packed_block, co...  11.3 us
    pallas_call x1, Pallas kernels, on_device(): pl.pallas_call(collect_kernel, grid=(4,), in_specs=[pl.BlockSpec(memory_s...  6.9 us
    all_to_all x1, starting transfers between devices, on_device(): lax.all_to_all(send, 'brick', split_axis=0, concat_axis=0, tiled=True)  6.87 us
  transfers between devices with their start and end apart: 8, of which 4 were waited for; matrix products, arithmetic and copies ran while one was open for 2% of the time, Pallas kernels for 38%

profile of v6, /device:TPU:0, one launch (start us, length us, event | category | flops | bytes accessed | tf_op | source)
XLA Modules:
  0.0 152.7 jit_solution(5681098248899605444)
XLA Ops:
  0.6 0.8 add_reduce_fusion.1
  1.4 0.1 reshape.80
  1.5 0.1 convert_reduce_fusion
  1.6 0.1 mul.50
  1.7 0.7 reduce.2
  2.4 0.1 reshape.67
  2.5 0.8 add_reduce_fusion
  3.3 0.1 reshape.86
  3.3 0.7 compare_select_fusion
  4.0 0.2 select_reduce_fusion
  4.2 0.7 sub.14
  4.9 11.5 %all-to-all-start = ((s32[64,1,8]{2,1,0:T(1,128)}), s32[64,1,8]{2,1,0:T(1,128)S(1)}, u32[]{:S(2)}, u32[]{:S(2)}) async-start(s32[64,1,8]{2,1,0:T(1,128)} %bitcast), calls=%async_computation | async-start | bytes 65536 | tf_op jit(solution)/shard_map/all_to_all | solution.py:629
  16.4 0.0 copy-start.1
  16.4 1.4 copy-done.1
  17.8 0.0 copy-start.3
  17.8 0.7 copy-done.3
  18.6 3.4 %tables.1 = (f32[72,64,128]{2,1,0:T(8,128)S(1)}, f32[144,8,128]{2,1,0:T(8,128)S(1)}, f32[96,8,128]{2,1,0:T(8,128)S(1)}, f32[12,512,128]{2,1,0:T(8,128)}) custom-call(f32[12,64,512]{2,1,0:T(8,128)S(1)} %bitcast.25, s32[12,1,512]{2,1,0:T(1,128)S(1)} %bitcast.28), custom_call_target="tpu_custom_call" | custom-call | tf_op jit(solution)/shard_map/tables/pallas_call | solution.py:641
  22.0 3.9 %all-to-all-done = s32[64,1,8]{2,1,0:T(1,128)S(1)} async-done(((s32[64,1,8]{2,1,0:T(1,128)}), s32[64,1,8]{2,1,0:T(1,128)S(1)}, u32[]{:S(2)}, u32[]{:S(2)}) %all-to-all-start) | async-done | bytes 2080 | tf_op jit(solution)/shard_map/all_to_all | solution.py:629
  25.9 3.7 %pack.1 = f32[64,80,128]{2,1,0:T(8,128)} custom-call(s32[64,8]{1,0:T(8,128)S(1)} %bitcast.26, f32[72,64,128]{2,1,0:T(8,128)S(1)} %get-tuple-element.27.face_ref, f32[144,8,128]{2,1,0:T(8,128)S(1)} %get-tuple-element.28.edge_ref, f32[96,8,128]{2,1,0:T(8,128)S(1)} %get-tuple-element.29.corner_ref), custom_call_target="tpu_custom_call" | custom-call | tf_op jit(solution)/shard_map/pack/pallas_call | solution.py:662
  29.6 0.0 copy-start.2
  29.6 0.0 copy-start.7
  29.6 6.5 %all-to-all-start.1 = ((f32[64,80,128]{2,1,0:T(8,128)}), f32[64,80,128]{2,1,0:T(8,128)S(1)}, u32[]{:S(2)}, u32[]{:S(2)}) async-start(f32[64,80,128]{2,1,0:T(8,128)} %pack.1), calls=%async_computation.1 | async-start | bytes 5242880 | tf_op jit(solution)/shard_map/all_to_all | solution.py:670
  36.1 0.0 copy-done.2
  36.2 2.9 %weights.1 = (bf16[4608,256]{1,0:T(8,128)(2,1)}, bf16[4608,256]{1,0:T(8,128)(2,1)}) custom-call(f32[27,64,64]{2,1,0:T(8,128)S(1)} %copy-done.2), custom_call_target="tpu_custom_call" | custom-call | bytes 6000000 | tf_op jit(solution)/shard_map/weights/pallas_call | solution.py:631
  39.1 0.0 copy-done.7
  39.1 0.1 maximum_bitcast_fusion.bias_ref
  39.1 0.0 copy-start.4
  39.1 0.7 copy-done.4
  39.9 12.4 %own_forward.1 = (f32[12,4,8,8,128]{4,3,2,1,0:T(8,128)}, f32[12,4,8,8,128]{4,3,2,1,0:T(8,128)}, bf16[3,6,2,5,10,16,128]{6,5,4,3,2,1,0:T(8,128)(2,1)}) custom-call(f32[12,512,128]{2,1,0:T(8,128)} %get-tuple-element.30.x_ref, s32[12,1,512]{2,1,0:T(1,128)S(1)} %bitcast.29, f32[12,64,512]{2,1,0:T(8,128)} %bitcast.40, ...), custom_call_target="tpu_custom_call" | custom-call | flops 7247757312 | bytes 15000000 | tf_op jit(solution)/shard_map/own_forward/pallas_call | solution.py:680
  52.3 18.4 %all-to-all-done.1.recv_ref = f32[64,80,128]{2,1,0:T(8,128)S(1)} async-done(((f32[64,80,128]{2,1,0:T(8,128)}), f32[64,80,128]{2,1,0:T(8,128)S(1)}, u32[]{:S(2)}, u32[]{:S(2)}) %all-to-all-start.1) | async-done | bytes 2621472 | tf_op jit(solution)/shard_map/all_to_all | solution.py:670
  70.7 17.0 %halo.1 = (f32[3072,128]{1,0:T(8,128)}, f32[3072,128]{1,0:T(8,128)}, f32[64,80,128]{2,1,0:T(8,128)S(1)}, bf16[2,3,10,6,16,128]{5,4,3,2,1,0:T(8,128)(2,1)}, bf16[...) custom-call(s32[312]{0:T(512)S(1)} %get-tuple-element.57.code_ref, ...), custom_call_target="tpu_custom_call" | custom-call | tf_op jit(solution)/shard_map/halo/pallas_call | solution.py:702
  87.7 0.0 copy-start
  87.7 1.5 %copy-done = f32[64,80,128]{2,1,0:T(8,128)} copy-done((f32[64,80,128]{2,1,0:T(8,128)}, f32[64,80,128]{2,1,0:T(8,128)S(1)}, u32[]{:S(2)}) %copy-start) | copy-done | bytes 2621464
  89.2 6.9 %all-to-all-start.2 = ((f32[64,80,128]{2,1,0:T(8,128)}), f32[64,80,128]{2,1,0:T(8,128)}, u32[]{:S(2)}, u32[]{:S(2)}) async-start(f32[64,80,128]{2,1,0:T(8,128)} %copy-done), calls=%async_computation.2 | async-start | bytes 5242880 | tf_op jit(solution)/shard_map/all_to_all | solution.py:737
  96.1 15.8 %kernel_grad.1 = f32[3,3,3,64,64]{4,3,2,1,0:T(8,128)S(1)} custom-call(bf16[3,6,2,5,10,16,128]{6,5,4,3,2,1,0:T(8,128)(2,1)} %get-tuple-element.37.a_ref, bf16[2,3,10,6,16,128]{5,4,3,2,1,0:T(8,128)(2,1)} %get-tuple-element.38.px_ref, bf16[2,3,2,5,6,16,128]{6,5,4,3,2,1,0:T(8,128)(2,1)} %get-tuple-element.39.py_ref, ...), custom_call_target="tpu_custom_call" | custom-call | bytes 1000 | tf_op jit(solution)/shard_map/kernel_grad/pallas_call | solution.py:741
  111.9 0.0 copy-start.5
  111.9 0.1 collective-permute-start
  112.1 1.7 %collective-permute-done = f32[864,64]{1,0:T(8,128)S(1)} collective-permute-done((f32[864,64]{1,0:T(8,128)S(1)}, f32[864,64]{1,0:T(8,128)S(1)}, u32[]{:S(2)}, u32[]{:S(2)}) %collective-permute-start) | collective-permute-done | bytes 221216 | tf_op jit(solution)/shard_map/ppermute | solution.py:571
  113.8 0.0 copy-start.6
  113.9 0.8 constant_dynamic-slice_fusion.2
  114.7 1.5 collective-permute-start.1
  116.2 2.9 %collective-permute-start.2 = (f32[216,64]{1,0:T(8,128)}, f32[216,64]{1,0:T(8,128)S(1)}, u32[]{:S(2)}, u32[]{:S(2)}) collective-permute-start(f32[216,64]{1,0:T(8,128)} %get-tuple-element.55), channel_id=1, source_target_pairs={{0,32},{1,33},{2,34},{3,35},{4,36},{5,37},{6,38},{7,39},{8,40},{9,... | collective-permute-start | bytes 165896 | tf_op jit(solution)/shard_map/ppermute | solution.py:581
  119.0 0.3 collective-permute-start.3
  119.4 0.0 copy-done.6
  119.4 0.0 copy-done.5
  119.4 5.2 %activated.1 = f32[12,64,512]{2,1,0:T(8,128)} custom-call(f32[12,4,8,8,128]{4,3,2,1,0:T(8,128)} %bitcast.34, s32[12,1,512]{2,1,0:T(1,128)S(1)} %bitcast.30), custom_call_target="tpu_custom_call" | custom-call | bytes 1000 | tf_op jit(solution)/shard_map/activated/pallas_call | solution.py:782
  124.6 11.3 %own_backward.1.own_ref = f32[12,4,2,8,8,64]{5,4,3,2,1,0:T(8,128)S(1)} custom-call(f32[12,4,8,8,128]{4,3,2,1,0:T(8,128)} %bitcast.33, bf16[4608,256]{1,0:T(8,128)(2,1)} %get-tuple-element.34.wb_hbm.w_ref), custom_call_target="tpu_custom_call" | custom-call | bytes 1000 | tf_op jit(solution)/shard_map/own_backward/pallas_call | solution.py:771
  135.9 0.0 collective-permute-done.1
  135.9 0.0 collective-permute-done.2
  135.9 0.0 collective-permute-done.3
  135.9 1.0 add_add_fusion
  136.9 0.1 reshape.76
  137.0 0.6 reshape.77
  137.6 0.0 all-to-all-done.2.back_ref
  137.6 6.8 %all-to-all-start.3 = ((f32[16,7,128]{2,1,0:T(8,128)}), f32[16,7,128]{2,1,0:T(8,128)S(1)}, u32[]{:S(2)}, u32[]{:S(2)}) async-start(f32[16,7,128]{2,1,0:T(8,128)} %reshape.77), calls=%async_computation.3 | async-start | bytes 131072 | tf_op jit(solution)/shard_map/all_to_all | solution.py:798
  144.5 6.9 %collect.1 = f32[12,64,512]{2,1,0:T(8,128)} custom-call(s32[64,8]{1,0:T(8,128)S(1)} %bitcast.27, f32[64,80,128]{2,1,0:T(8,128)} %all-to-all-done.2.back_ref, f32[12,4,2,8,8,64]{5,4,3,2,1,0:T(8,128)S(1)} %own_backward.1.own_ref, s32[12,1,512]{2,1,0:T(1,128)S(1)} %bitcast.31), custom_call_target="tpu_custom_call" | custom-call | tf_op jit(solution)/shard_map/collect/pallas_call | solution.py:800
  151.4 0.8 all-to-all-done.3
  152.1 0.6 slice_multiply_fusion
  (5 shorter events, 0.1 us)
Async XLA Ops:
  4.9 21.0 %all-to-all-start = ((s32[64,1,8]{2,1,0:T(1,128)}), s32[64,1,8]{2,1,0:T(1,128)S(1)}, u32[]{:S(2)}, u32[]{:S(2)}) async-start(s32[64,1,8]{2,1,0:T(1,128)} %bitcast), calls=%async_computation | async-start | bytes 65536 | tf_op jit(solution)/shard_map/all_to_all | solution.py:629
  16.4 1.4 copy-start.1
  17.8 0.7 copy-start.3
  29.6 6.6 %copy-start.2 = (f32[27,64,64]{2,1,0:T(8,128)S(1)}, f32[27,64,64]{2,1,0:T(8,128)}, u32[]{:S(2)}) copy-start(f32[27,64,64]{2,1,0:T(8,128)} %w_ref.1) | copy-start | bytes 1327108
  29.6 9.5 %copy-start.7 = (f32[64]{0:T(128)S(1)}, f32[64]{0:T(128)}, u32[]{:S(2)}) copy-start(f32[64]{0:T(128)} %param.15) | copy-start | bytes 772
  29.6 41.1 %all-to-all-start.1 = ((f32[64,80,128]{2,1,0:T(8,128)}), f32[64,80,128]{2,1,0:T(8,128)S(1)}, u32[]{:S(2)}, u32[]{:S(2)}) async-start(f32[64,80,128]{2,1,0:T(8,128)} %pack.1), calls=%async_computation.1 | async-start | bytes 5242880 | tf_op jit(solution)/shard_map/all_to_all | solution.py:670
  39.1 0.7 copy-start.4
  87.7 1.5 %copy-start = (f32[64,80,128]{2,1,0:T(8,128)}, f32[64,80,128]{2,1,0:T(8,128)S(1)}, u32[]{:S(2)}) copy-start(f32[64,80,128]{2,1,0:T(8,128)S(1)} %get-tuple-element.46) | copy-start | bytes 7864324
  89.2 48.4 %all-to-all-start.2 = ((f32[64,80,128]{2,1,0:T(8,128)}), f32[64,80,128]{2,1,0:T(8,128)}, u32[]{:S(2)}, u32[]{:S(2)}) async-start(f32[64,80,128]{2,1,0:T(8,128)} %copy-done), calls=%async_computation.2 | async-start | bytes 5242880 | tf_op jit(solution)/shard_map/all_to_all | solution.py:737
  111.9 7.5 %copy-start.5 = (s32[1,12,512]{2,0,1:T(1,128)S(1)}, s32[1,12,512]{2,0,1:T(1,128)}, u32[]{:S(2)}) copy-start(s32[1,12,512]{2,0,1:T(1,128)} %param.13) | copy-start | bytes 73732
  111.9 1.9 %collective-permute-start = (f32[864,64]{1,0:T(8,128)S(1)}, f32[864,64]{1,0:T(8,128)S(1)}, u32[]{:S(2)}, u32[]{:S(2)}) collective-permute-start(f32[864,64]{1,0:T(8,128)S(1)} %constant_dynamic-slice_fusion.3), channel_id=1, source_target_pairs={{0,64},{64,0},{1,65},{65,1},{2,66},{66,2},{3,67},{67,3},{4,68},{68... | collective-permute-start | bytes 663560 | tf_op jit(solution)/shard_map/ppermute | solution.py:571
  113.8 5.5 %copy-start.6 = (f32[864,64]{1,0:T(8,128)}, f32[864,64]{1,0:T(8,128)S(1)}, u32[]{:S(2)}) copy-start(f32[864,64]{1,0:T(8,128)S(1)} %dynamic-slice_add_fusion) | copy-start | bytes 663556
  114.7 21.2 %collective-permute-start.1 = (f32[216,64]{1,0:T(8,128)}, f32[216,64]{1,0:T(8,128)S(1)}, u32[]{:S(2)}, u32[]{:S(2)}) collective-permute-start(f32[216,64]{1,0:T(8,128)} %get-tuple-element.53), channel_id=1, source_target_pairs={{0,16},{1,17},{2,18},{3,19},{4,20},{5,21},{6,22},{7,23},{8,24},{9,... | collective-permute-start | bytes 165896 | tf_op jit(solution)/shard_map/ppermute | solution.py:581
  116.2 19.7 %collective-permute-start.2 = (f32[216,64]{1,0:T(8,128)}, f32[216,64]{1,0:T(8,128)S(1)}, u32[]{:S(2)}, u32[]{:S(2)}) collective-permute-start(f32[216,64]{1,0:T(8,128)} %get-tuple-element.55), channel_id=1, source_target_pairs={{0,32},{1,33},{2,34},{3,35},{4,36},{5,37},{6,38},{7,39},{8,40},{9,... | collective-permute-start | bytes 165896 | tf_op jit(solution)/shard_map/ppermute | solution.py:581
  119.0 16.8 %collective-permute-start.3 = (f32[216,64]{1,0:T(8,128)S(1)}, f32[216,64]{1,0:T(8,128)}, u32[]{:S(2)}, u32[]{:S(2)}) collective-permute-start(f32[216,64]{1,0:T(8,128)S(1)} %get-tuple-element.54), channel_id=1, source_target_pairs={{0,48},{1,49},{2,50},{3,51},{4,52},{5,53},{6,54},{7,55},{8,56},{9,... | collective-permute-start | bytes 165896 | tf_op jit(solution)/shard_map/ppermute | solution.py:581
  137.6 14.5 %all-to-all-start.3 = ((f32[16,7,128]{2,1,0:T(8,128)}), f32[16,7,128]{2,1,0:T(8,128)S(1)}, u32[]{:S(2)}, u32[]{:S(2)}) async-start(f32[16,7,128]{2,1,0:T(8,128)} %reshape.77), calls=%async_computation.3 | async-start | bytes 131072 | tf_op jit(solution)/shard_map/all_to_all | solution.py:798

commit v7 on v6

--- a/solution.py
+++ b/solution.py
@@ -156,7 +156,7 @@
         cotm_ref[b] = jnp.concatenate([c[:, 0], c[:, 1]], axis=-1)
 
 
-def own_backward_kernel(d_ref, w_ref, own_ref, a_ref):
+def own_backward_kernel(d_ref, act_ref, m_ref, w_ref, own_ref, out_ref, a_ref):
     @pl.when(pl.program_id(0) == 0)
     def _():
         a_ref[...] = jnp.zeros_like(a_ref)
@@ -176,10 +176,6 @@
     for b in range(2):
         own_ref[b, :, 0] = out[:, :, b * 8:b * 8 + 8, :64]
         own_ref[b, :, 1] = out[:, :, b * 8:b * 8 + 8, 64:]
-
-
-def activated_kernel(act_ref, m_ref, out_ref):
-    for b in range(2):
         mask = m_ref[b].astype(F32)
         for h in range(2):
             t = act_ref[b, 2 * h:2 * h + 2].reshape(128, 128).T
@@ -199,13 +195,15 @@
 
 
 def halo_kernel(code_ref, recv_ref, own_hbm, cot_hbm, wf_hbm, wb_hbm,
-                act_hbm, dpre_hbm, send_ref, px_hbm, py_hbm, pz_hbm,
+                act_hbm, dpre_hbm, send_hbm, px_hbm, py_hbm, pz_hbm,
                 pre, cot_ref, wf_ref, wb_ref, act_ref, dpre_ref, px, py, pz,
-                zf, qx, qy, qz, rx, ry, rz, tmp, sems):
+                send_ref, zf, qx, qy, qz, rx, ry, rz, tmp, sems):
     arriving = [pltpu.make_async_copy(a, b, sems.at[n]) for n, (a, b) in enumerate(
         [(own_hbm, pre), (wf_hbm, wf_ref), (cot_hbm, cot_ref), (wb_hbm, wb_ref)])]
     leaving = [pltpu.make_async_copy(a, b, sems.at[4 + n]) for n, (a, b) in enumerate(
         [(px, px_hbm), (py, py_hbm), (pz, pz_hbm), (act_ref, act_hbm), (dpre_ref, dpre_hbm)])]
+    faces_out = pltpu.make_async_copy(send_ref.at[:, 0:64], send_hbm.at[:, 0:64], sems.at[9])
+    rest_out = pltpu.make_async_copy(send_ref.at[:, 64:80], send_hbm.at[:, 64:80], sems.at[10])
     for c in arriving:
         c.start()
     high8 = half_of((8, 128))
@@ -387,8 +385,12 @@
         return s * 800 + (xh * 10 + y) * 16 + b
 
     send_ref[...] = jnp.zeros_like(send_ref)
-    for b in range(12):
-        for k, (dx, dy, dz) in enumerate(OFFSETS):
+    kinds = [k for k in range(26) if KIND[k] == 0] + [k for k in range(26) if KIND[k]]
+    for n, k in enumerate(kinds):
+        if n == 6:
+            faces_out.start()
+        dx, dy, dz = OFFSETS[k]
+        for b in range(12):
             o, pos, _ = unpack_code(code_ref, b, k)
             xt, yt = target_coord(dx), target_coord(dy)
             sx, sy, sz = int(dx == 1), int(dy == 1), int(dz == 1)
@@ -423,7 +425,8 @@
                 v = placed(jnp.broadcast_to(rz[r:r + 1, :], (8, 128)), wanted[xt % 2])
                 spot = jnp.logical_and(row == pos - 5, high8)
                 send_ref[o, 72:80, :] = jnp.where(spot, v, send_ref[o, 72:80, :])
-    for c in leaving:
+    rest_out.start()
+    for c in leaving + [faces_out, rest_out]:
         c.wait()
 
 
@@ -702,11 +705,11 @@
     act, dpre, send, px, py, pz = pl.pallas_call(
         halo_kernel,
         in_specs=[whole(pltpu.SMEM), whole()] + [held] * 4,
-        out_specs=[held, held, whole(), held, held, held],
+        out_specs=[held] * 6,
         out_shape=[
             hbm_out(flat, F32),
             hbm_out(flat, F32),
-            jax.ShapeDtypeStruct((64, 80, 128), F32),
+            hbm_out((64, 80, 128), F32),
             hbm_out(side_x, BF16),
             hbm_out(side_y, BF16),
             hbm_out(side_z, BF16),
@@ -721,6 +724,7 @@
             pltpu.VMEM(side_x, BF16),
             pltpu.VMEM(side_y, BF16),
             pltpu.VMEM(side_z, BF16),
+            pltpu.VMEM((64, 80, 128), F32),
             pltpu.VMEM((3200, 128), F32),
             pltpu.VMEM((2, 3, 12, 6, 16, 128), BF16),
             pltpu.VMEM((2, 3, 2, 5, 6, 16, 128), BF16),
@@ -729,7 +733,7 @@
             pltpu.VMEM((2, 384, 128), F32),
             pltpu.VMEM((1600, 128), F32),
             pltpu.VMEM((8, 128), F32),
-            pltpu.SemaphoreType.DMA((9,)),
+            pltpu.SemaphoreType.DMA((11,)),
         ],
         compiler_params=params(44),
         name="halo",
@@ -763,32 +767,21 @@
     )(in_hbm(windows), in_hbm(px), in_hbm(py), in_hbm(pz), in_hbm(dpre))
     kernel = z.reshape(1728, 64)
     scale = 1.0 / math.sqrt(float(2 * 768 * 512))
-    act, kernel = lax.optimization_barrier((act, kernel))
     total = swap_scenes(kernel)
     dpre, total = lax.optimization_barrier((dpre, total))
     kept, sent = sum_stage(total, 16)
 
-    own = pl.pallas_call(
+    own, activated = pl.pallas_call(
         own_backward_kernel,
         grid=(6,),
-        in_specs=[packed_block, const_block((4608, 256))],
-        out_specs=brick_block,
-        out_shape=brick_shape,
+        in_specs=[packed_block, packed_block, mask_block, const_block((4608, 256))],
+        out_specs=[brick_block, turned_block],
+        out_shape=[hbm_out(brick_shape.shape, F32), hbm_out(turned_shape.shape, F32)],
         scratch_shapes=[pltpu.VMEM((3, 1, 2, 5, 10, 16, 128), BF16)],
         compiler_params=params(24),
         cost_estimate=pl.CostEstimate(flops=0, bytes_accessed=1000, transcendentals=0),
         name="own_backward",
-    )(in_hbm(dpre), in_hbm(wb))
-    activated = pl.pallas_call(
-        activated_kernel,
-        grid=(6,),
-        in_specs=[packed_block, mask_block],
-        out_specs=turned_block,
-        out_shape=turned_shape,
-        compiler_params=params(8),
-        cost_estimate=pl.CostEstimate(flops=0, bytes_accessed=1000, transcendentals=0),
-        name="activated",
-    )(in_hbm(act), mask)
+    )(in_hbm(dpre), in_hbm(act), mask, in_hbm(wb))
 
     total = kept + sent[0] + sent[1] + sent[2]
     own, total, activated = lax.optimization_barrier((own, total, activated))
@@ -816,7 +809,7 @@
         ],
         compiler_params=params(24),
         name="collect",
-    )(asked, back, own, mask)
+    )(asked, back, in_hbm(own), mask)
     share = jnp.sum(shares, axis=0).reshape(896)[:864] * scale
     return activated.transpose(0, 2, 1)[None], grad.transpose(0, 2, 1)[None], share
 

time: 154 us -> 151 us (0.981)
  Pallas kernels: 78.6 us -> 75.2 us
    pallas_call x2 -> x1, Pallas kernels: 16.5 us -> 12.4 us  [on_device(): pl.pallas_call(own_backward_kernel, grid=(6,), in_specs=[packed_block, pa...]
    unnamed x16 -> x14, local copies, waits for them, and re-layouts: 4.43 us -> 4.38 us
  transfers between devices with their start and end apart: 8 -> 8, of which waited for: 4 -> 4; matrix products, arithmetic and copies ran while one was open for 2% -> 2% of each run, Pallas kernels for 38% -> 36%
where the time goes in v7:
time: 151 us; the launch traced here: 150 us
  Pallas kernels  75.2 us (50%)
  starting transfers between devices  36.3 us (24%)
  waiting for transfers between devices  25.1 us (17%)
  local copies, waits for them, and re-layouts  6.97 us (5%)
  other arithmetic  5.92 us (4%)
    all_to_all x1, waiting for transfers between devices, on_device(): recv = lax.all_to_all(out, 'brick', split_axis=0, concat_axis=0, tiled=True)  18.4 us
    pallas_call x1, Pallas kernels, on_device(): pl.pallas_call(halo_kernel, in_specs=[whole(pltpu.SMEM), whole()] + [held...  17.7 us
    pallas_call x1, Pallas kernels, on_device(): pl.pallas_call(kernel_grad_kernel, grid=(3,), in_specs=[pl.BlockSpec((1,...  15.8 us
    pallas_call x1, Pallas kernels, on_device(): pl.pallas_call(own_forward_kernel, grid=(6,), in_specs=[lead_block((2, 51...  12.4 us
    pallas_call x1, Pallas kernels, on_device(): pl.pallas_call(own_backward_kernel, grid=(6,), in_specs=[packed_block, pa...  12.4 us
    all_to_all x1, starting transfers between devices, on_device(): lax.all_to_all(wanted, 'brick', split_axis=0, concat_axis=0, tiled=True)  11.5 us
    pallas_call x1, Pallas kernels, on_device(): pl.pallas_call(collect_kernel, grid=(4,), in_specs=[pl.BlockSpec(memory_s...  7.04 us
    all_to_all x1, starting transfers between devices, on_device(): lax.all_to_all(total, 'brick', split_axis=0, concat_axis=0, tiled=True, a...  6.86 us
  transfers between devices with their start and end apart: 8, of which 4 were waited for; matrix products, arithmetic and copies ran while one was open for 2% of the time, Pallas kernels for 36%

profile of v7, /device:TPU:0, one launch (start us, length us, event | category | flops | bytes accessed | tf_op | source)
XLA Modules:
  0.0 150.3 jit_solution(15282726645539853747)
XLA Ops:
  0.6 0.8 add_reduce_fusion.1
  1.4 0.1 reshape.80
  1.5 0.1 convert_reduce_fusion
  1.6 0.1 mul.50
  1.7 0.7 reduce.2
  2.4 0.1 reshape.67
  2.5 0.8 add_reduce_fusion
  3.3 0.1 reshape.86
  3.3 0.7 compare_select_fusion
  4.0 0.2 select_reduce_fusion
  4.2 0.7 sub.14
  4.9 11.5 %all-to-all-start = ((s32[64,1,8]{2,1,0:T(1,128)}), s32[64,1,8]{2,1,0:T(1,128)S(1)}, u32[]{:S(2)}, u32[]{:S(2)}) async-start(s32[64,1,8]{2,1,0:T(1,128)} %bitcast), calls=%async_computation | async-start | bytes 65536 | tf_op jit(solution)/shard_map/all_to_all | solution.py:632
  16.4 0.0 copy-start
  16.4 1.4 copy-done
  17.8 0.0 copy-start.2
  17.8 0.7 copy-done.2
  18.6 3.4 %tables.1 = (f32[72,64,128]{2,1,0:T(8,128)S(1)}, f32[144,8,128]{2,1,0:T(8,128)S(1)}, f32[96,8,128]{2,1,0:T(8,128)S(1)}, f32[12,512,128]{2,1,0:T(8,128)}) custom-call(f32[12,64,512]{2,1,0:T(8,128)S(1)} %bitcast.25, s32[12,1,512]{2,1,0:T(1,128)S(1)} %bitcast.28), custom_call_target="tpu_custom_call" | custom-call | tf_op jit(solution)/shard_map/tables/pallas_call | solution.py:644
  21.9 3.9 %all-to-all-done = s32[64,1,8]{2,1,0:T(1,128)S(1)} async-done(((s32[64,1,8]{2,1,0:T(1,128)}), s32[64,1,8]{2,1,0:T(1,128)S(1)}, u32[]{:S(2)}, u32[]{:S(2)}) %all-to-all-start) | async-done | bytes 2080 | tf_op jit(solution)/shard_map/all_to_all | solution.py:632
  25.9 3.7 %pack.1 = f32[64,80,128]{2,1,0:T(8,128)} custom-call(s32[64,8]{1,0:T(8,128)S(1)} %bitcast.26, f32[72,64,128]{2,1,0:T(8,128)S(1)} %get-tuple-element.27.face_ref, f32[144,8,128]{2,1,0:T(8,128)S(1)} %get-tuple-element.28.edge_ref, f32[96,8,128]{2,1,0:T(8,128)S(1)} %get-tuple-element.29.corner_ref), custom_call_target="tpu_custom_call" | custom-call | tf_op jit(solution)/shard_map/pack/pallas_call | solution.py:665
  29.6 0.0 copy-start.1
  29.6 0.0 copy-start.6
  29.6 6.5 %all-to-all-start.1 = ((f32[64,80,128]{2,1,0:T(8,128)}), f32[64,80,128]{2,1,0:T(8,128)S(1)}, u32[]{:S(2)}, u32[]{:S(2)}) async-start(f32[64,80,128]{2,1,0:T(8,128)} %pack.1), calls=%async_computation.1 | async-start | bytes 5242880 | tf_op jit(solution)/shard_map/all_to_all | solution.py:673
  36.1 0.0 copy-done.1
  36.1 2.9 %weights.1 = (bf16[4608,256]{1,0:T(8,128)(2,1)}, bf16[4608,256]{1,0:T(8,128)(2,1)}) custom-call(f32[27,64,64]{2,1,0:T(8,128)S(1)} %copy-done.1), custom_call_target="tpu_custom_call" | custom-call | bytes 6000000 | tf_op jit(solution)/shard_map/weights/pallas_call | solution.py:634
  39.1 0.0 copy-done.6
  39.1 0.1 maximum_bitcast_fusion.bias_ref
  39.1 0.0 copy-start.3
  39.1 0.7 copy-done.3
  39.9 12.4 %own_forward.1 = (f32[12,4,8,8,128]{4,3,2,1,0:T(8,128)}, f32[12,4,8,8,128]{4,3,2,1,0:T(8,128)}, bf16[3,6,2,5,10,16,128]{6,5,4,3,2,1,0:T(8,128)(2,1)}) custom-call(f32[12,512,128]{2,1,0:T(8,128)} %get-tuple-element.30.x_ref, s32[12,1,512]{2,1,0:T(1,128)S(1)} %bitcast.29, f32[12,64,512]{2,1,0:T(8,128)} %bitcast.39, ...), custom_call_target="tpu_custom_call" | custom-call | flops 7247757312 | bytes 15000000 | tf_op jit(solution)/shard_map/own_forward/pallas_call | solution.py:683
  52.3 18.4 %all-to-all-done.1.recv_ref = f32[64,80,128]{2,1,0:T(8,128)S(1)} async-done(((f32[64,80,128]{2,1,0:T(8,128)}), f32[64,80,128]{2,1,0:T(8,128)S(1)}, u32[]{:S(2)}, u32[]{:S(2)}) %all-to-all-start.1) | async-done | bytes 2621472 | tf_op jit(solution)/shard_map/all_to_all | solution.py:673
  70.6 17.7 %halo.1 = (f32[3072,128]{1,0:T(8,128)}, f32[3072,128]{1,0:T(8,128)}, f32[64,80,128]{2,1,0:T(8,128)}, bf16[2,3,10,6,16,128]{5,4,3,2,1,0:T(8,128)(2,1)}, bf16[2,3,...) custom-call(s32[312]{0:T(512)S(1)} %get-tuple-element.57.code_ref, ...), custom_call_target="tpu_custom_call" | custom-call | tf_op jit(solution)/shard_map/halo/pallas_call | solution.py:705
  88.3 6.7 %all-to-all-start.2 = ((f32[64,80,128]{2,1,0:T(8,128)}), f32[64,80,128]{2,1,0:T(8,128)S(1)}, u32[]{:S(2)}, u32[]{:S(2)}) async-start(f32[64,80,128]{2,1,0:T(8,128)} %get-tuple-element.46), calls=%async_computation.2 | async-start | bytes 5242880 | tf_op jit(solution)/shard_map/all_to_all | solution.py:741
  95.0 15.8 %kernel_grad.1 = f32[3,3,3,64,64]{4,3,2,1,0:T(8,128)S(1)} custom-call(bf16[3,6,2,5,10,16,128]{6,5,4,3,2,1,0:T(8,128)(2,1)} %get-tuple-element.36.a_ref, bf16[2,3,10,6,16,128]{5,4,3,2,1,0:T(8,128)(2,1)} %get-tuple-element.37.px_ref, bf16[2,3,2,5,6,16,128]{6,5,4,3,2,1,0:T(8,128)(2,1)} %get-tuple-element.38.py_ref, ...), custom_call_target="tpu_custom_call" | custom-call | bytes 1000 | tf_op jit(solution)/shard_map/kernel_grad/pallas_call | solution.py:745
  110.8 0.8 constant_dynamic-slice_fusion.3
  111.6 0.0 collective-permute-start
  111.6 2.1 %collective-permute-done = f32[864,64]{1,0:T(8,128)} collective-permute-done((f32[864,64]{1,0:T(8,128)}, f32[864,64]{1,0:T(8,128)}, u32[]{:S(2)}, u32[]{:S(2)}) %collective-permute-start) | collective-permute-done | bytes 221216 | tf_op jit(solution)/shard_map/ppermute | solution.py:574
  113.7 1.1 dynamic-slice_add_fusion
  114.8 0.0 copy-start.5
  114.8 0.8 copy-done.5
  115.6 1.7 %collective-permute-start.1 = (f32[216,64]{1,0:T(8,128)S(1)}, f32[216,64]{1,0:T(8,128)S(1)}, u32[]{:S(2)}, u32[]{:S(2)}) collective-permute-start(f32[216,64]{1,0:T(8,128)S(1)} %get-tuple-element.53), channel_id=1, source_target_pairs={{0,16},{1,17},{2,18},{3,19},{4,20},{5,21},{6,22},{7,23},{8,24},{9,... | collective-permute-start | bytes 165896 | tf_op jit(solution)/shard_map/ppermute | solution.py:584
  117.2 2.9 %collective-permute-start.2 = (f32[216,64]{1,0:T(8,128)S(1)}, f32[216,64]{1,0:T(8,128)S(1)}, u32[]{:S(2)}, u32[]{:S(2)}) collective-permute-start(f32[216,64]{1,0:T(8,128)S(1)} %get-tuple-element.55), channel_id=1, source_target_pairs={{0,32},{1,33},{2,34},{3,35},{4,36},{5,37},{6,38},{7,39},{8,40},{9,... | collective-permute-start | bytes 165896 | tf_op jit(solution)/shard_map/ppermute | solution.py:584
  120.1 0.2 collective-permute-start.3
  120.3 0.0 copy-start.4
  120.3 0.7 copy-done.4
  121.1 12.4 %own_backward.1 = (f32[12,4,2,8,8,64]{5,4,3,2,1,0:T(8,128)}, f32[12,64,512]{2,1,0:T(8,128)}) custom-call(f32[12,4,8,8,128]{4,3,2,1,0:T(8,128)} %bitcast.33, f32[12,4,8,8,128]{4,3,2,1,0:T(8,128)} %bitcast.34, s32[12,1,512]{2,1,0:T(1,128)S(1)} %bitcast.30, bf16[4608,256]{1,0:T(8,128)(2,1)} %get-tuple-element.34.wb_hbm.w_ref), custom_call_target="tpu_custom_call" | custom-call | bytes 1000 | tf_op jit(solution)/shard_map/own_backward/pallas_call | solution.py:774
  133.4 0.0 collective-permute-done.1
  133.4 0.0 collective-permute-done.2
  133.4 0.0 collective-permute-done.3
  133.4 0.9 add_add_fusion
  134.4 0.1 reshape.76
  134.5 0.6 reshape.77
  135.1 0.0 all-to-all-done.2.back_ref
  135.1 6.9 %all-to-all-start.3 = ((f32[16,7,128]{2,1,0:T(8,128)}), f32[16,7,128]{2,1,0:T(8,128)S(1)}, u32[]{:S(2)}, u32[]{:S(2)}) async-start(f32[16,7,128]{2,1,0:T(8,128)} %reshape.77), calls=%async_computation.3 | async-start | bytes 131072 | tf_op jit(solution)/shard_map/all_to_all | solution.py:791
  142.0 7.0 %collect.1 = f32[12,64,512]{2,1,0:T(8,128)} custom-call(s32[64,8]{1,0:T(8,128)S(1)} %bitcast.27, f32[64,80,128]{2,1,0:T(8,128)S(1)} %all-to-all-done.2.back_ref, f32[12,4,2,8,8,64]{5,4,3,2,1,0:T(8,128)} %get-tuple-element.49.own_ref, s32[12,1,512]{2,1,0:T(1,128)S(1)} %bitcast.31), custom_call_target="tpu_custom_call" | custom-call | tf_op jit(solution)/shard_map/collect/pallas_call | solution.py:793
  149.0 0.6 all-to-all-done.3
  149.7 0.6 slice_multiply_fusion
  (4 shorter events, 0.1 us)
Async XLA Ops:
  4.9 21.0 %all-to-all-start = ((s32[64,1,8]{2,1,0:T(1,128)}), s32[64,1,8]{2,1,0:T(1,128)S(1)}, u32[]{:S(2)}, u32[]{:S(2)}) async-start(s32[64,1,8]{2,1,0:T(1,128)} %bitcast), calls=%async_computation | async-start | bytes 65536 | tf_op jit(solution)/shard_map/all_to_all | solution.py:632
  16.4 1.4 copy-start
  17.8 0.7 copy-start.2
  29.6 6.5 %copy-start.1 = (f32[27,64,64]{2,1,0:T(8,128)S(1)}, f32[27,64,64]{2,1,0:T(8,128)}, u32[]{:S(2)}) copy-start(f32[27,64,64]{2,1,0:T(8,128)} %w_ref.1) | copy-start | bytes 1327108
  29.6 9.5 %copy-start.6 = (f32[64]{0:T(128)S(1)}, f32[64]{0:T(128)}, u32[]{:S(2)}) copy-start(f32[64]{0:T(128)} %param.15) | copy-start | bytes 772
  29.6 41.0 %all-to-all-start.1 = ((f32[64,80,128]{2,1,0:T(8,128)}), f32[64,80,128]{2,1,0:T(8,128)S(1)}, u32[]{:S(2)}, u32[]{:S(2)}) async-start(f32[64,80,128]{2,1,0:T(8,128)} %pack.1), calls=%async_computation.1 | async-start | bytes 5242880 | tf_op jit(solution)/shard_map/all_to_all | solution.py:673
  39.1 0.7 copy-start.3
  88.3 46.8 %all-to-all-start.2 = ((f32[64,80,128]{2,1,0:T(8,128)}), f32[64,80,128]{2,1,0:T(8,128)S(1)}, u32[]{:S(2)}, u32[]{:S(2)}) async-start(f32[64,80,128]{2,1,0:T(8,128)} %get-tuple-element.46), calls=%async_computation.2 | async-start | bytes 5242880 | tf_op jit(solution)/shard_map/all_to_all | solution.py:741
  111.6 2.1 %collective-permute-start = (f32[864,64]{1,0:T(8,128)}, f32[864,64]{1,0:T(8,128)}, u32[]{:S(2)}, u32[]{:S(2)}) collective-permute-start(f32[864,64]{1,0:T(8,128)} %constant_dynamic-slice_fusion.3), channel_id=1, source_target_pairs={{0,64},{64,0},{1,65},{65,1},{2,66},{66,2},{3,67},{67,3},{4,68},{68... | collective-permute-start | bytes 663560 | tf_op jit(solution)/shard_map/ppermute | solution.py:574
  114.8 0.8 copy-start.5
  115.6 17.9 %collective-permute-start.1 = (f32[216,64]{1,0:T(8,128)S(1)}, f32[216,64]{1,0:T(8,128)S(1)}, u32[]{:S(2)}, u32[]{:S(2)}) collective-permute-start(f32[216,64]{1,0:T(8,128)S(1)} %get-tuple-element.53), channel_id=1, source_target_pairs={{0,16},{1,17},{2,18},{3,19},{4,20},{5,21},{6,22},{7,23},{8,24},{9,... | collective-permute-start | bytes 165896 | tf_op jit(solution)/shard_map/ppermute | solution.py:584
  117.2 16.2 %collective-permute-start.2 = (f32[216,64]{1,0:T(8,128)S(1)}, f32[216,64]{1,0:T(8,128)S(1)}, u32[]{:S(2)}, u32[]{:S(2)}) collective-permute-start(f32[216,64]{1,0:T(8,128)S(1)} %get-tuple-element.55), channel_id=1, source_target_pairs={{0,32},{1,33},{2,34},{3,35},{4,36},{5,37},{6,38},{7,39},{8,40},{9,... | collective-permute-start | bytes 165896 | tf_op jit(solution)/shard_map/ppermute | solution.py:584
  120.1 13.4 %collective-permute-start.3 = (f32[216,64]{1,0:T(8,128)S(1)}, f32[216,64]{1,0:T(8,128)S(1)}, u32[]{:S(2)}, u32[]{:S(2)}) collective-permute-start(f32[216,64]{1,0:T(8,128)S(1)} %get-tuple-element.54), channel_id=1, source_target_pairs={{0,48},{1,49},{2,50},{3,51},{4,52},{5,53},{6,54},{7,55},{8,56},{9,... | collective-permute-start | bytes 165896 | tf_op jit(solution)/shard_map/ppermute | solution.py:584
  120.3 0.7 copy-start.4
  135.1 14.5 %all-to-all-start.3 = ((f32[16,7,128]{2,1,0:T(8,128)}), f32[16,7,128]{2,1,0:T(8,128)S(1)}, u32[]{:S(2)}, u32[]{:S(2)}) async-start(f32[16,7,128]{2,1,0:T(8,128)} %reshape.77), calls=%async_computation.3 | async-start | bytes 131072 | tf_op jit(solution)/shard_map/all_to_all | solution.py:791

commit v8 on v7

--- a/solution.py
+++ b/solution.py
@@ -697,7 +697,7 @@
         compiler_params=params(24),
         cost_estimate=pl.CostEstimate(flops=2 * 3072 * 4608 * 256, bytes_accessed=15000000, transcendentals=0),
         name="own_forward",
-    )(in_hbm(rows), mask, in_hbm(cot), in_hbm(wf), bias2)
+    )(in_hbm(rows), in_hbm(mask), in_hbm(cot), in_hbm(wf), bias2)
 
     flat = (3072, 128)
     side_x, side_y, side_z = (2, 3, 10, 6, 16, 128), (2, 3, 2, 5, 6, 16, 128), (2, 2, 5, 10, 16, 128)
@@ -781,7 +781,7 @@
         compiler_params=params(24),
         cost_estimate=pl.CostEstimate(flops=0, bytes_accessed=1000, transcendentals=0),
         name="own_backward",
-    )(in_hbm(dpre), in_hbm(act), mask, in_hbm(wb))
+    )(in_hbm(dpre), in_hbm(act), in_hbm(mask), in_hbm(wb))
 
     total = kept + sent[0] + sent[1] + sent[2]
     own, total, activated = lax.optimization_barrier((own, total, activated))
@@ -809,7 +809,7 @@
         ],
         compiler_params=params(24),
         name="collect",
-    )(asked, back, in_hbm(own), mask)
+    )(asked, back, in_hbm(own), in_hbm(mask))
     share = jnp.sum(shares, axis=0).reshape(896)[:864] * scale
     return activated.transpose(0, 2, 1)[None], grad.transpose(0, 2, 1)[None], share
 

time: 151 us -> 151 us (level)
    unnamed x14 -> x10, local copies, waits for them, and re-layouts: 4.38 us -> 2.9 us
where the time goes in v8:
time: 151 us; the launch traced here: 150 us
  Pallas kernels  75.1 us (50%)
  starting transfers between devices  36.3 us (24%)
  waiting for transfers between devices  26 us (17%)
  other arithmetic  5.92 us (4%)
  local copies, waits for them, and re-layouts  5.5 us (4%)
    all_to_all x1, waiting for transfers between devices, on_device(): recv = lax.all_to_all(out, 'brick', split_axis=0, concat_axis=0, tiled=True)  19.2 us
    pallas_call x1, Pallas kernels, on_device(): pl.pallas_call(halo_kernel, in_specs=[whole(pltpu.SMEM), whole()] + [held...  17.6 us
    pallas_call x1, Pallas kernels, on_device(): pl.pallas_call(kernel_grad_kernel, grid=(3,), in_specs=[pl.BlockSpec((1,...  15.8 us
    pallas_call x1, Pallas kernels, on_device(): pl.pallas_call(own_backward_kernel, grid=(6,), in_specs=[packed_block, pa...  12.5 us
    pallas_call x1, Pallas kernels, on_device(): pl.pallas_call(own_forward_kernel, grid=(6,), in_specs=[lead_block((2, 51...  12.3 us
    all_to_all x1, starting transfers between devices, on_device(): lax.all_to_all(wanted, 'brick', split_axis=0, concat_axis=0, tiled=True)  11.5 us
    pallas_call x1, Pallas kernels, on_device(): pl.pallas_call(collect_kernel, grid=(4,), in_specs=[pl.BlockSpec(memory_s...  6.97 us
    all_to_all x1, starting transfers between devices, on_device(): lax.all_to_all(total, 'brick', split_axis=0, concat_axis=0, tiled=True, a...  6.88 us
  transfers between devices with their start and end apart: 8, of which 4 were waited for; matrix products, arithmetic and copies ran while one was open for 2% of the time, Pallas kernels for 36%

profile of v8, /device:TPU:0, one launch (start us, length us, event | category | flops | bytes accessed | tf_op | source)
XLA Modules:
  0.0 149.6 jit_solution(8066549128561380893)
XLA Ops:
  0.6 0.8 add_reduce_fusion.1
  1.4 0.1 reshape.80
  1.5 0.1 convert_reduce_fusion
  1.6 0.1 mul.50
  1.7 0.7 reduce.2
  2.4 0.1 reshape.67
  2.5 0.8 add_reduce_fusion
  3.3 0.1 reshape.86
  3.3 0.7 compare_select_fusion
  4.0 0.2 select_reduce_fusion
  4.2 0.7 sub.14
  4.9 11.5 %all-to-all-start = ((s32[64,1,8]{2,1,0:T(1,128)}), s32[64,1,8]{2,1,0:T(1,128)S(1)}, u32[]{:S(2)}, u32[]{:S(2)}) async-start(s32[64,1,8]{2,1,0:T(1,128)} %bitcast), calls=%async_computation | async-start | bytes 65536 | tf_op jit(solution)/shard_map/all_to_all | solution.py:632
  16.4 0.0 copy-start
  16.4 1.4 copy-done
  17.8 0.0 copy-start.2
  17.8 0.7 copy-done.2
  18.6 3.4 %tables.1 = (f32[72,64,128]{2,1,0:T(8,128)S(1)}, f32[144,8,128]{2,1,0:T(8,128)S(1)}, f32[96,8,128]{2,1,0:T(8,128)S(1)}, f32[12,512,128]{2,1,0:T(8,128)}) custom-call(f32[12,64,512]{2,1,0:T(8,128)S(1)} %bitcast.25, s32[12,1,512]{2,1,0:T(1,128)S(1)} %bitcast.31), custom_call_target="tpu_custom_call" | custom-call | tf_op jit(solution)/shard_map/tables/pallas_call | solution.py:644
  22.0 3.9 %all-to-all-done = s32[64,1,8]{2,1,0:T(1,128)S(1)} async-done(((s32[64,1,8]{2,1,0:T(1,128)}), s32[64,1,8]{2,1,0:T(1,128)S(1)}, u32[]{:S(2)}, u32[]{:S(2)}) %all-to-all-start) | async-done | bytes 2080 | tf_op jit(solution)/shard_map/all_to_all | solution.py:632
  25.9 3.7 %pack.1 = f32[64,80,128]{2,1,0:T(8,128)} custom-call(s32[64,8]{1,0:T(8,128)S(1)} %bitcast.26, f32[72,64,128]{2,1,0:T(8,128)S(1)} %get-tuple-element.27.face_ref, f32[144,8,128]{2,1,0:T(8,128)S(1)} %get-tuple-element.28.edge_ref, f32[96,8,128]{2,1,0:T(8,128)S(1)} %get-tuple-element.29.corner_ref), custom_call_target="tpu_custom_call" | custom-call | tf_op jit(solution)/shard_map/pack/pallas_call | solution.py:665
  29.6 0.0 copy-start.1
  29.6 0.0 copy-start.4
  29.6 6.5 %all-to-all-start.1 = ((f32[64,80,128]{2,1,0:T(8,128)}), f32[64,80,128]{2,1,0:T(8,128)S(1)}, u32[]{:S(2)}, u32[]{:S(2)}) async-start(f32[64,80,128]{2,1,0:T(8,128)} %pack.1), calls=%async_computation.1 | async-start | bytes 5242880 | tf_op jit(solution)/shard_map/all_to_all | solution.py:673
  36.1 0.0 copy-done.1
  36.1 2.9 %weights.1 = (bf16[4608,256]{1,0:T(8,128)(2,1)}, bf16[4608,256]{1,0:T(8,128)(2,1)}) custom-call(f32[27,64,64]{2,1,0:T(8,128)S(1)} %copy-done.1), custom_call_target="tpu_custom_call" | custom-call | bytes 6000000 | tf_op jit(solution)/shard_map/weights/pallas_call | solution.py:634
  39.1 0.0 copy-done.4
  39.1 0.1 maximum_bitcast_fusion.bias_ref
  39.1 12.3 %own_forward.1 = (f32[12,4,8,8,128]{4,3,2,1,0:T(8,128)}, f32[12,4,8,8,128]{4,3,2,1,0:T(8,128)}, bf16[3,6,2,5,10,16,128]{6,5,4,3,2,1,0:T(8,128)(2,1)}) custom-call(f32[12,512,128]{2,1,0:T(8,128)} %get-tuple-element.30.x_ref, s32[12,1,512]{2,1,0:T(1,128)} %bitcast.28, f32[12,64,512]{2,1,0:T(8,128)} %bitcast.39, ...), custom_call_target="tpu_custom_call" | custom-call | flops 7247757312 | bytes 15000000 | tf_op jit(solution)/shard_map/own_forward/pallas_call | solution.py:683
  51.4 19.2 %all-to-all-done.1.recv_ref = f32[64,80,128]{2,1,0:T(8,128)S(1)} async-done(((f32[64,80,128]{2,1,0:T(8,128)}), f32[64,80,128]{2,1,0:T(8,128)S(1)}, u32[]{:S(2)}, u32[]{:S(2)}) %all-to-all-start.1) | async-done | bytes 2621472 | tf_op jit(solution)/shard_map/all_to_all | solution.py:673
  70.6 17.6 %halo.1 = (f32[3072,128]{1,0:T(8,128)}, f32[3072,128]{1,0:T(8,128)}, f32[64,80,128]{2,1,0:T(8,128)}, bf16[2,3,10,6,16,128]{5,4,3,2,1,0:T(8,128)(2,1)}, bf16[2,3,...) custom-call(s32[312]{0:T(512)S(1)} %get-tuple-element.57.code_ref, ...), custom_call_target="tpu_custom_call" | custom-call | tf_op jit(solution)/shard_map/halo/pallas_call | solution.py:705
  88.3 6.7 %all-to-all-start.2 = ((f32[64,80,128]{2,1,0:T(8,128)}), f32[64,80,128]{2,1,0:T(8,128)S(1)}, u32[]{:S(2)}, u32[]{:S(2)}) async-start(f32[64,80,128]{2,1,0:T(8,128)} %get-tuple-element.46), calls=%async_computation.2 | async-start | bytes 5242880 | tf_op jit(solution)/shard_map/all_to_all | solution.py:741
  94.9 15.8 %kernel_grad.1 = f32[3,3,3,64,64]{4,3,2,1,0:T(8,128)S(1)} custom-call(bf16[3,6,2,5,10,16,128]{6,5,4,3,2,1,0:T(8,128)(2,1)} %get-tuple-element.36.a_ref, bf16[2,3,10,6,16,128]{5,4,3,2,1,0:T(8,128)(2,1)} %get-tuple-element.37.px_ref, bf16[2,3,2,5,6,16,128]{6,5,4,3,2,1,0:T(8,128)(2,1)} %get-tuple-element.38.py_ref, ...), custom_call_target="tpu_custom_call" | custom-call | bytes 1000 | tf_op jit(solution)/shard_map/kernel_grad/pallas_call | solution.py:745
  110.7 0.8 constant_dynamic-slice_fusion.3
  111.5 0.0 collective-permute-start
  111.5 2.1 %collective-permute-done = f32[864,64]{1,0:T(8,128)} collective-permute-done((f32[864,64]{1,0:T(8,128)}, f32[864,64]{1,0:T(8,128)}, u32[]{:S(2)}, u32[]{:S(2)}) %collective-permute-start) | collective-permute-done | bytes 221216 | tf_op jit(solution)/shard_map/ppermute | solution.py:574
  113.6 1.1 dynamic-slice_add_fusion
  114.7 0.0 copy-start.3
  114.7 0.8 copy-done.3
  115.5 1.7 %collective-permute-start.1 = (f32[216,64]{1,0:T(8,128)S(1)}, f32[216,64]{1,0:T(8,128)S(1)}, u32[]{:S(2)}, u32[]{:S(2)}) collective-permute-start(f32[216,64]{1,0:T(8,128)S(1)} %get-tuple-element.53), channel_id=1, source_target_pairs={{0,16},{1,17},{2,18},{3,19},{4,20},{5,21},{6,22},{7,23},{8,24},{9,... | collective-permute-start | bytes 165896 | tf_op jit(solution)/shard_map/ppermute | solution.py:584
  117.2 2.9 %collective-permute-start.2 = (f32[216,64]{1,0:T(8,128)S(1)}, f32[216,64]{1,0:T(8,128)S(1)}, u32[]{:S(2)}, u32[]{:S(2)}) collective-permute-start(f32[216,64]{1,0:T(8,128)S(1)} %get-tuple-element.55), channel_id=1, source_target_pairs={{0,32},{1,33},{2,34},{3,35},{4,36},{5,37},{6,38},{7,39},{8,40},{9,... | collective-permute-start | bytes 165896 | tf_op jit(solution)/shard_map/ppermute | solution.py:584
  120.0 0.2 collective-permute-start.3
  120.3 12.5 %own_backward.1 = (f32[12,4,2,8,8,64]{5,4,3,2,1,0:T(8,128)}, f32[12,64,512]{2,1,0:T(8,128)}) custom-call(f32[12,4,8,8,128]{4,3,2,1,0:T(8,128)} %bitcast.33, f32[12,4,8,8,128]{4,3,2,1,0:T(8,128)} %bitcast.34, s32[12,1,512]{2,1,0:T(1,128)} %bitcast.29, bf16[4608,256]{1,0:T(8,128)(2,1)} %get-tuple-element.34.wb_hbm.w_ref), custom_call_target="tpu_custom_call" | custom-call | bytes 1000 | tf_op jit(solution)/shard_map/own_backward/pallas_call | solution.py:774
  132.7 0.0 collective-permute-done.1
  132.7 0.0 collective-permute-done.2
  132.7 0.0 collective-permute-done.3
  132.8 0.9 add_add_fusion
  133.7 0.1 reshape.76
  133.8 0.6 reshape.77
  134.4 0.0 all-to-all-done.2.back_ref
  134.4 6.9 %all-to-all-start.3 = ((f32[16,7,128]{2,1,0:T(8,128)}), f32[16,7,128]{2,1,0:T(8,128)S(1)}, u32[]{:S(2)}, u32[]{:S(2)}) async-start(f32[16,7,128]{2,1,0:T(8,128)} %reshape.77), calls=%async_computation.3 | async-start | bytes 131072 | tf_op jit(solution)/shard_map/all_to_all | solution.py:791
  141.3 7.0 %collect.1 = f32[12,64,512]{2,1,0:T(8,128)} custom-call(s32[64,8]{1,0:T(8,128)S(1)} %bitcast.27, f32[64,80,128]{2,1,0:T(8,128)S(1)} %all-to-all-done.2.back_ref, f32[12,4,2,8,8,64]{5,4,3,2,1,0:T(8,128)} %get-tuple-element.49.own_ref, s32[12,1,512]{2,1,0:T(1,128)} %bitcast.30), custom_call_target="tpu_custom_call" | custom-call | tf_op jit(solution)/shard_map/collect/pallas_call | solution.py:793
  148.3 0.7 all-to-all-done.3
  149.0 0.6 slice_multiply_fusion
  (4 shorter events, 0.1 us)
Async XLA Ops:
  4.9 21.0 %all-to-all-start = ((s32[64,1,8]{2,1,0:T(1,128)}), s32[64,1,8]{2,1,0:T(1,128)S(1)}, u32[]{:S(2)}, u32[]{:S(2)}) async-start(s32[64,1,8]{2,1,0:T(1,128)} %bitcast), calls=%async_computation | async-start | bytes 65536 | tf_op jit(solution)/shard_map/all_to_all | solution.py:632
  16.4 1.4 copy-start
  17.8 0.7 copy-start.2
  29.6 6.6 %copy-start.1 = (f32[27,64,64]{2,1,0:T(8,128)S(1)}, f32[27,64,64]{2,1,0:T(8,128)}, u32[]{:S(2)}) copy-start(f32[27,64,64]{2,1,0:T(8,128)} %w_ref.1) | copy-start | bytes 1327108
  29.6 9.5 %copy-start.4 = (f32[64]{0:T(128)S(1)}, f32[64]{0:T(128)}, u32[]{:S(2)}) copy-start(f32[64]{0:T(128)} %param.15) | copy-start | bytes 772
  29.6 41.1 %all-to-all-start.1 = ((f32[64,80,128]{2,1,0:T(8,128)}), f32[64,80,128]{2,1,0:T(8,128)S(1)}, u32[]{:S(2)}, u32[]{:S(2)}) async-start(f32[64,80,128]{2,1,0:T(8,128)} %pack.1), calls=%async_computation.1 | async-start | bytes 5242880 | tf_op jit(solution)/shard_map/all_to_all | solution.py:673
  88.3 46.2 %all-to-all-start.2 = ((f32[64,80,128]{2,1,0:T(8,128)}), f32[64,80,128]{2,1,0:T(8,128)S(1)}, u32[]{:S(2)}, u32[]{:S(2)}) async-start(f32[64,80,128]{2,1,0:T(8,128)} %get-tuple-element.46), calls=%async_computation.2 | async-start | bytes 5242880 | tf_op jit(solution)/shard_map/all_to_all | solution.py:741
  111.5 2.1 %collective-permute-start = (f32[864,64]{1,0:T(8,128)}, f32[864,64]{1,0:T(8,128)}, u32[]{:S(2)}, u32[]{:S(2)}) collective-permute-start(f32[864,64]{1,0:T(8,128)} %constant_dynamic-slice_fusion.3), channel_id=1, source_target_pairs={{0,64},{64,0},{1,65},{65,1},{2,66},{66,2},{3,67},{67,3},{4,68},{68... | collective-permute-start | bytes 663560 | tf_op jit(solution)/shard_map/ppermute | solution.py:574
  114.7 0.8 copy-start.3
  115.5 17.2 %collective-permute-start.1 = (f32[216,64]{1,0:T(8,128)S(1)}, f32[216,64]{1,0:T(8,128)S(1)}, u32[]{:S(2)}, u32[]{:S(2)}) collective-permute-start(f32[216,64]{1,0:T(8,128)S(1)} %get-tuple-element.53), channel_id=1, source_target_pairs={{0,16},{1,17},{2,18},{3,19},{4,20},{5,21},{6,22},{7,23},{8,24},{9,... | collective-permute-start | bytes 165896 | tf_op jit(solution)/shard_map/ppermute | solution.py:584
  117.2 15.6 %collective-permute-start.2 = (f32[216,64]{1,0:T(8,128)S(1)}, f32[216,64]{1,0:T(8,128)S(1)}, u32[]{:S(2)}, u32[]{:S(2)}) collective-permute-start(f32[216,64]{1,0:T(8,128)S(1)} %get-tuple-element.55), channel_id=1, source_target_pairs={{0,32},{1,33},{2,34},{3,35},{4,36},{5,37},{6,38},{7,39},{8,40},{9,... | collective-permute-start | bytes 165896 | tf_op jit(solution)/shard_map/ppermute | solution.py:584
  120.0 12.7 %collective-permute-start.3 = (f32[216,64]{1,0:T(8,128)S(1)}, f32[216,64]{1,0:T(8,128)S(1)}, u32[]{:S(2)}, u32[]{:S(2)}) collective-permute-start(f32[216,64]{1,0:T(8,128)S(1)} %get-tuple-element.54), channel_id=1, source_target_pairs={{0,48},{1,49},{2,50},{3,51},{4,52},{5,53},{6,54},{7,55},{8,56},{9,... | collective-permute-start | bytes 165896 | tf_op jit(solution)/shard_map/ppermute | solution.py:584
  134.4 14.6 %all-to-all-start.3 = ((f32[16,7,128]{2,1,0:T(8,128)}), f32[16,7,128]{2,1,0:T(8,128)S(1)}, u32[]{:S(2)}, u32[]{:S(2)}) async-start(f32[16,7,128]{2,1,0:T(8,128)} %reshape.77), calls=%async_computation.3 | async-start | bytes 131072 | tf_op jit(solution)/shard_map/all_to_all | solution.py:791
